TPU v7x, 32 devices: a whole 2x2x4 slice. The times are simulated.
32 devices in a mesh: row: 4 (over y, core), col: 8 (over z, x).
Axes of the slice: x: 2, y: 2, z: 4, core: 2. Of those that a mesh axis runs over, the one named last changes fastest.
Arguments:
- sigma_top: float32 [8192, 8192], P('row', 'col')
- panel: float32 [4, 8192, 512], P(None, ('row', 'col')), may hold values from -0.0007324219 to 0.0007324219
- parent_panel: float32 [3, 512, 512], replicated, may hold values from -0.1875 to 0.1875
- diag_inverse: float32 [4, 512, 512], replicated, as said below
- block_depth: int32 [64], replicated, may hold values from 0 to 4, as said below
Outputs:
- sigma_cols: float32 [4, 8192, 512], P(None, ('row', 'col'))
- sigma_link: float32 [3, 512, 512], P(None, 'row')
- sigma_diag: float32 [4, 512, 512], P(None, 'row')
Inputs may be any that keep to these rules, and one draw needn't show every extreme that they name: Ancestor rows are nested: supernode k holds block b among its ancestor rows exactly when block_depth[b] > k. Each diag_inverse[k] is lower triangular. sigma_top is symmetric: sigma_top[i, j] = sigma_top[j, i] exactly.
All inputs are finite; a program needn't handle non-finite values.
Results may differ from a plain program's by a relative error of at most 0.0001.
Values sent between devices are 32-bit elements; how exact they have to be, the bound alone decides.
A program may use at most 128 MiB of HBM per device.

v0:
```python
import jax
import jax.numpy as jnp
from jax import lax
from jax.sharding import PartitionSpec as P

STEPS = 4
BLOCK = 128


def broadcast(value, axis, root):
    mine = lax.axis_index(axis) == root
    return lax.psum(jnp.where(mine, value, jnp.zeros_like(value)), axis)


def row_depth(block_depth, first_row, row_total):
    blocks = (first_row + jnp.arange(row_total, dtype=jnp.int32)) // BLOCK
    block_ids = jnp.arange(block_depth.shape[0], dtype=jnp.int32)
    matched = (blocks[:, None] == block_ids[None, :]).astype(jnp.int32)
    return jnp.sum(matched * block_depth[None, :], axis=1)


def shards(sigma_top, panel, parent_panel, diag_inverse, block_depth):
    highest = lax.Precision.HIGHEST
    row_count = lax.axis_size("row")
    col_count = lax.axis_size("col")
    row_index = lax.axis_index("row")
    col_index = lax.axis_index("col")
    per_row = col_count // row_count
    share_rows = panel.shape[1]
    width = panel.shape[2]
    group_rows = sigma_top.shape[1]
    out_rows = width // row_count
    own_depth = row_depth(block_depth, (row_index * col_count + col_index) * share_rows, share_rows)
    col_depth = row_depth(block_depth, col_index * group_rows, group_rows)
    own_masks = []
    masked_list = []
    col_panels = []
    for section in range(STEPS):
        own_mask = jnp.where(own_depth > section, 1.0, 0.0).astype(jnp.float32)[:, None]
        col_mask = jnp.where(col_depth > section, 1.0, 0.0).astype(jnp.float32)[:, None]
        this_panel = panel[section]
        own_masks.append(own_mask)
        masked_list.append(own_mask * this_panel)
        row_group = lax.all_gather(this_panel, "col", axis=0, tiled=True)
        selected = lax.dynamic_slice_in_dim(
            row_group, col_index % per_row * group_rows, group_rows, 0
        )
        column_part = broadcast(selected, "row", col_index // per_row)
        col_panels.append(col_mask * column_part)
    products = []
    for section in range(STEPS):

        def panel_term(row_start, row_total, col_panel=col_panels[section]):
            return jnp.dot(
                sigma_top, col_panel, precision=highest, preferred_element_type=jnp.float32
            )

        products.append(
            lax.psum_scatter(
                panel_term(jnp.int32(0), share_rows * lax.axis_size("col")),
                "col",
                scatter_dimension=0,
                tiled=True,
            )
        )
    column_list = []
    cross_parts = []
    diag_parts = []
    for section in range(STEPS):
        summed = products[section]
        if section > 0:
            earlier = column_list[-1]
            cross_parts.append(jnp.dot(earlier.T, masked_list[section], precision=highest))
            summed = summed + jnp.dot(earlier, parent_panel[section - 1], precision=highest)
        current_cols = -own_masks[section] * summed
        column_list.append(current_cols)
        diag_parts.append(jnp.dot(masked_list[section].T, current_cols, precision=highest))
    link_list = []
    diagonals = []
    for section in range(STEPS):
        inverse = diag_inverse[section]
        offset = jnp.dot(inverse.T, inverse, precision=highest)
        if section > 0:
            parent = parent_panel[section - 1]
            crossed = lax.psum(cross_parts[section - 1], ("row", "col"))
            link_block = -(crossed + jnp.dot(diagonals[-1], parent, precision=highest))
            link_list.append(link_block)
            offset = offset - jnp.dot(parent.T, link_block, precision=highest)
        diagonals.append(offset - lax.psum(diag_parts[section], ("row", "col")))
    link_stack = lax.dynamic_slice_in_dim(jnp.stack(link_list), row_index * out_rows, out_rows, 1)
    diag_stack = lax.dynamic_slice_in_dim(jnp.stack(diagonals), row_index * out_rows, out_rows, 1)
    return (jnp.stack(column_list), link_stack, diag_stack)


def solution(mesh):
    return jax.shard_map(
        shards,
        mesh=mesh,
        in_specs=(P("row", "col"), P(None, ("row", "col"), None), P(), P(), P()),
        out_specs=(P(None, ("row", "col"), None), P(None, "row", None), P(None, "row", None)),
        check_vma=False,
    )
```

profile of v0, /device:TPU:0, one launch (start us, length us, event | category | flops | bytes accessed | tf_op | source)
XLA Modules:
  0.0 1066.4 jit_solution(9244824371448028596)
XLA Ops:
  7.2 2.9 fusion.89
  10.1 0.7 all-gather.13.cloned.1.call-update
  10.9 0.7 all-gather.11.cloned.1.call-update
  12.2 74.6 %all-gather.15.cloned.1.call-done = f32[1,2048,512]{2,1,0:T(8,128)} async-done(((f32[1,256,512]{2,1,0:T(8,128)}), f32[1,2048,512]{2,1,0:T(8,128)}) %all-gather.15.cloned.1.call-update) | async-done | bytes 4194320 | tf_op jit(solution)/shard_map/all_gather | solution.py:44
  86.8 3.1 select_bitcast_fusion
  90.0 70.7 %all-gather.13.cloned.1.call-done = f32[1,2048,512]{2,1,0:T(8,128)} async-done(((f32[1,256,512]{2,1,0:T(8,128)}), f32[1,2048,512]{2,1,0:T(8,128)}) %all-gather.13.cloned.1.call-update) | async-done | bytes 4194320 | tf_op jit(solution)/shard_map/all_gather | solution.py:44
  160.6 3.1 select_bitcast_fusion.1
  163.8 71.3 %all-gather.11.cloned.1.call-done = f32[1,2048,512]{2,1,0:T(8,128)} async-done(((f32[1,256,512]{2,1,0:T(8,128)}), f32[1,2048,512]{2,1,0:T(8,128)}) %all-gather.11.cloned.1.call-update) | async-done | bytes 4194320 | tf_op jit(solution)/shard_map/all_gather | solution.py:44
  235.0 3.2 select_bitcast_fusion.2
  238.2 71.1 %all-gather.9.cloned.1.call-done = f32[1,2048,512]{2,1,0:T(8,128)} async-done(((f32[1,256,512]{2,1,0:T(8,128)}), f32[1,2048,512]{2,1,0:T(8,128)}) %all-gather.9.cloned.1.call-update) | async-done | bytes 4194320 | tf_op jit(solution)/shard_map/all_gather | solution.py:44
  309.3 3.2 select_bitcast_fusion.3
  312.6 0.6 copy-done.24
  313.3 151.6 %all-reduce.7.cloned.1.call-done = (f32[1024,512]{1,0:T(8,128)}, f32[1024,512]{1,0:T(8,128)}, f32[1024,512]{1,0:T(8,128)}, f32[1024,512]{1,0:T(8,128)}) async-done(((f32[1024,512]{1,0:T(8,128)}, f32[1024,512]{1,0:T(8,128)}, f32[1024,512]{1,0:T(8,128)}, f32[1024,512]{1,0:T(8,128)}), (f32[1024,512]{1,0:T(8,128)}, f32[1024,512]{1,0:T(8,128)}, f32[1024,512]{1,0:T(8,128)}, ...) | async-done | bytes 8388624 | tf_op jit(solution)/shard_map/psum | solution.py:12
  464.9 31.0 %convolution_bitcast_fusion.2 = f32[2048,512]{0,1:T(8,128)} fusion(f32[2048,1024]{1,0:T(8,128)} %param.5, f32[1024,512]{1,0:T(8,128)} %get-tuple-element.18, f32[1024]{0:T(1024)S(1)} %get-tuple-element.27), kind=kOutput, calls=%fused_computation.6 | convolution fusion | flops 12885426176 | bytes 14684160 | tf_op jit(solution)/shard_map/dot_general | solution.py:54
  495.9 1.5 copy-done.17
  497.4 30.6 %convolution_bitcast_fusion.3 = f32[2048,512]{0,1:T(8,128)} fusion(f32[2048,1024]{1,0:T(8,128)} %param.5, f32[1024,512]{1,0:T(8,128)S(1)} %copy-done.17, f32[1024]{0:T(1024)S(1)} %get-tuple-element.24), kind=kOutput, calls=%fused_computation.7 | convolution fusion | flops 12885426176 | bytes 14684160 | tf_op jit(solution)/shard_map/dot_general | solution.py:54
  528.1 1.5 copy-done.16
  529.7 30.5 %convolution_bitcast_fusion.1 = f32[2048,512]{0,1:T(8,128)} fusion(f32[2048,1024]{1,0:T(8,128)} %param.5, f32[1024,512]{1,0:T(8,128)S(1)} %copy-done.16, f32[1024]{0:T(1024)S(1)} %get-tuple-element.26), kind=kOutput, calls=%fused_computation.5 | convolution fusion | flops 12885426176 | bytes 14684160 | tf_op jit(solution)/shard_map/dot_general | solution.py:54
  560.3 1.5 copy-done.15
  561.8 30.9 %convolution_bitcast_fusion = f32[2048,512]{0,1:T(8,128)} fusion(f32[2048,1024]{1,0:T(8,128)} %param.5, f32[1024,512]{1,0:T(8,128)S(1)} %copy-done.15, f32[1024]{0:T(1024)S(1)} %get-tuple-element.25), kind=kOutput, calls=%fused_computation.4 | convolution fusion | flops 12885426176 | bytes 14684160 | tf_op jit(solution)/shard_map/dot_general | solution.py:54
  593.0 83.8 %reduce-scatter.5.cloned.1.call-done = f32[256,512]{0,1:T(8,128)} async-done(((f32[2048,512]{0,1:T(8,128)}), f32[256,512]{0,1:T(8,128)}) %reduce-scatter.5.cloned.1.call-update) | async-done | bytes 524304 | tf_op jit(solution)/shard_map/reduce_scatter | solution.py:59
  676.7 3.2 fusion.14
  679.9 2.1 fusion.59
  682.0 2.9 fusion.56
  684.9 83.5 %reduce-scatter.9.cloned.1.call-done = f32[256,512]{0,1:T(8,128)} async-done(((f32[2048,512]{0,1:T(8,128)}), f32[256,512]{0,1:T(8,128)}) %reduce-scatter.9.cloned.1.call-update) | async-done | bytes 524304 | tf_op jit(solution)/shard_map/reduce_scatter | solution.py:59
  768.4 3.2 fusion.15
  771.6 2.9 fusion.58
  774.5 2.1 fusion.61
  776.7 83.9 %reduce-scatter.11.cloned.1.call-done = f32[256,512]{0,1:T(8,128)} async-done(((f32[2048,512]{0,1:T(8,128)}), f32[256,512]{0,1:T(8,128)}) %reduce-scatter.11.cloned.1.call-update) | async-done | bytes 524304 | tf_op jit(solution)/shard_map/reduce_scatter | solution.py:59
  860.6 3.2 fusion.16
  863.8 3.1 fusion.60
  866.9 2.1 fusion.57
  869.0 2.9 fusion.55
  871.9 4.4 fusion.24
  876.3 4.8 fusion.22
  881.1 4.5 fusion.20
  885.7 1.5 pad_maximum_fusion
  887.2 3.1 copy.21
  890.3 151.5 %all-reduce.5.cloned.1.call-done = (f32[512,512]{1,0:T(8,128)}, f32[512,512]{1,0:T(8,128)}, f32[512,512]{1,0:T(8,128)}, f32[512,512]{1,0:T(8,128)}, f32[512,512]...) async-done(((f32[512,512]{1,0:T(8,128)}, f32[512,512]{1,0:T(8,128)}, f32[512,512]{1,0:T(8,128)}, f32[512,512]{1,0:T(8,128)}, f32[512,512]{1,0:T(8,128)}, ...) | async-done | bytes 7340048 | tf_op jit(solution)/shard_map/psum | solution.py:85
  1041.8 3.8 convolution_subtract_fusion
  1045.7 1.9 fusion.13
  1047.6 1.9 fusion.12
  1049.5 1.9 fusion.10
  1051.4 1.9 fusion.9
  1053.4 1.9 fusion.7
  1055.2 1.9 fusion.6
  1057.1 0.9 fusion.54
  1058.1 1.1 fusion.19
  (72 shorter events, 1.4 us)
Async XLA Ops:
  7.2 79.7 %all-gather.15.cloned.1.call-start = ((), (), s32[]{:S(2)}) async-start(), calls=%async_computation.11 | async-start | bytes 4718592 | tf_op jit(solution)/shard_map/all_gather | solution.py:44
  10.1 150.5 %all-gather.13.cloned.1.call-start = ((), (), s32[]{:S(2)}) async-start(), calls=%async_computation.10 | async-start | bytes 4718592 | tf_op jit(solution)/shard_map/all_gather | solution.py:44
  10.8 224.2 %all-gather.11.cloned.1.call-start = ((), (), s32[]{:S(2)}) async-start(), calls=%async_computation.9 | async-start | bytes 4718592 | tf_op jit(solution)/shard_map/all_gather | solution.py:44
  11.6 297.7 %all-gather.9.cloned.1.call-start = ((), (), s32[]{:S(2)}) async-start(), calls=%async_computation.8 | async-start | bytes 4718592 | tf_op jit(solution)/shard_map/all_gather | solution.py:44
  12.2 452.7 %all-reduce.7.cloned.1.call-start = ((), (), s32[]{:S(2)}) async-start(), calls=%async_computation.13 | async-start | bytes 16777216 | tf_op jit(solution)/shard_map/psum | solution.py:12
  312.5 0.7 copy-start.24
  312.5 280.5 %reduce-scatter.7.cloned.1.call-start = ((), (), s32[]{:S(2)}) async-start(), calls=%async_computation.5 | async-start | bytes 4718592 | tf_op jit(solution)/shard_map/reduce_scatter | solution.py:59
  495.8 1.6 copy-start.17
  495.9 180.9 %reduce-scatter.5.cloned.1.call-start = ((), (), s32[]{:S(2)}) async-start(), calls=%async_computation.4 | async-start | bytes 4718592 | tf_op jit(solution)/shard_map/reduce_scatter | solution.py:59
  528.1 1.6 copy-start.16
  528.1 240.3 %reduce-scatter.9.cloned.1.call-start = ((), (), s32[]{:S(2)}) async-start(), calls=%async_computation.6 | async-start | bytes 4718592 | tf_op jit(solution)/shard_map/reduce_scatter | solution.py:59
  560.2 1.6 copy-start.15
  560.2 300.3 %reduce-scatter.11.cloned.1.call-start = ((), (), s32[]{:S(2)}) async-start(), calls=%async_computation.7 | async-start | bytes 4718592 | tf_op jit(solution)/shard_map/reduce_scatter | solution.py:59
  592.7 84.0 %copy-start = (f32[3,512,512]{2,1,0:T(8,128)S(1)}, f32[3,512,512]{2,1,0:T(8,128)}, u32[]{:S(2)}) copy-start(f32[3,512,512]{2,1,0:T(8,128)} %param.7) | copy-start | bytes 9437188
  592.8 449.0 %all-reduce.5.cloned.1.call-start = ((), (), s32[]{:S(2)}) async-start(), calls=%async_computation.12 | async-start | bytes 14680064 | tf_op jit(solution)/shard_map/psum | solution.py:85
  676.7 3.2 copy-start.1
  679.9 2.1 copy-start.6
  768.4 3.2 copy-start.2
  771.6 2.9 copy-start.4
  860.6 3.2 copy-start.3
  860.6 6.3 copy-start.8
  863.8 5.2 copy-start.10
  876.3 9.3 copy-start.9
  881.1 4.5 copy-start.5
  881.1 4.5 copy-start.7
  881.1 4.5 copy-start.11
  1041.8 3.8 copy-start.23
  1045.7 1.9 copy-start.14
  1045.7 1.9 copy-start.20
  1047.6 1.9 copy-start.22
  1049.5 1.9 copy-start.13
  1049.5 1.9 copy-start.19
  1051.4 1.9 copy-start.21
  1053.3 1.9 copy-start.12
  1053.3 1.9 copy-start.18
Sparse Core Ops, SparseCore 0:
  10.7 76.0 all-gather.14
  88.9 71.6 all-gather.12
  163.3 71.6 all-gather.10
  237.6 71.6 all-gather.8
  312.6 152.1 all-reduce.6
  496.0 88.5 reduce-scatter.6
  588.7 88.0 reduce-scatter.4
  680.4 88.0 reduce-scatter.8
  772.5 88.0 reduce-scatter.10
  872.0 169.7 all-reduce.4
where the time goes:
time: 1080 us; the launch traced here: 1070 us
  waiting for transfers between devices  844 us (78%)
  matrix products  180 us (17%)
  other arithmetic  16.4 us (2%)
  between operations  15 us (1%)
  local copies, waits for them, and re-layouts  11.2 us (1%)
    all_gather x4, waiting for transfers between devices, shards(): row_group = lax.all_gather(this_panel, 'col', axis=0, tiled=True)  288 us
    reduce_scatter x4, waiting for transfers between devices, shards(): lax.psum_scatter(panel_term(jnp.int32(0), share_rows * lax.axis_size('col...  251 us
    psum x1, waiting for transfers between devices, broadcast(): return lax.psum(jnp.where(mine, value, jnp.zeros_like(value)), axis)  152 us
    psum x1, waiting for transfers between devices, shards(): crossed = lax.psum(cross_parts[section - 1], ('row', 'col'))  151 us
    dot_general x4, matrix products, panel_term(): jnp.dot(sigma_top, col_panel, precision=highest, preferred_element_type=j...  123 us
  transfers between devices with their start and end apart: 10, of which 9 were waited for; matrix products, arithmetic and copies ran while one was open for 13% of the time, Pallas kernels for 0%

commit v1 on v0

v1 whole, which is shorter than its diff:
```python
import jax
import jax.numpy as jnp
from jax import lax
from jax.sharding import PartitionSpec as P

STEPS = 4
BLOCK = 128
HIGH = lax.Precision.HIGH


def dot(a, b):
    return jnp.dot(a, b, precision=HIGH, preferred_element_type=jnp.float32)


def dot_t(a, b):
    return lax.dot_general(
        a, b, (((0,), (0,)), ((), ())), precision=HIGH, preferred_element_type=jnp.float32
    )


def split(value):
    upper = lax.reduce_precision(value, 8, 7)
    return upper.astype(jnp.bfloat16), (value - upper).astype(jnp.bfloat16)


def row_depth(block_depth, first_row, row_total):
    blocks = (first_row + jnp.arange(row_total, dtype=jnp.int32)) // BLOCK
    block_ids = jnp.arange(block_depth.shape[0], dtype=jnp.int32)
    matched = (blocks[:, None] == block_ids[None, :]).astype(jnp.int32)
    return jnp.sum(matched * block_depth[None, :], axis=1)


def pick(value, which):
    return lax.dynamic_index_in_dim(value, which, 1, keepdims=False)


def shards(sigma_top, panel, parent_panel, diag_inverse, block_depth):
    row_count = lax.axis_size("row")
    col_count = lax.axis_size("col")
    row_index = lax.axis_index("row")
    col_index = lax.axis_index("col")
    share = panel.shape[1]
    width = panel.shape[2]
    depth = sigma_top.shape[1]
    out_rows = width // row_count
    own_depth = row_depth(block_depth, (row_index * col_count + col_index) * share, share)
    own_masks = [
        jnp.where(own_depth > k, 1.0, 0.0).astype(jnp.float32)[:, None] for k in range(STEPS)
    ]
    masked = [own_masks[k] * panel[k] for k in range(STEPS)]

    swap = [
        (g, (g % row_count) * col_count + g // row_count) for g in range(row_count * col_count)
    ]
    right = []
    for k in range(STEPS):
        part = lax.ppermute(masked[k], ("row", "col"), swap)
        whole = lax.all_gather(part, "row", axis=0, tiled=True)
        upper, lower = split(whole)
        right.append(jnp.concatenate([upper, upper, lower], axis=0))

    pairs = sigma_top.reshape(col_count // 2, 2, share, depth)
    bit = col_index % 2
    left = []
    for which in (1 - bit, bit):
        upper, lower = split(pick(pairs, which).reshape(col_count // 2 * share, depth))
        left.append(jnp.concatenate([upper, lower, upper], axis=1))

    def exchange(value, stage):
        return lax.ppermute(value, "col", [(c, c ^ (1 << stage)) for c in range(col_count)])

    products = []
    for k in range(STEPS):
        gone = jnp.dot(left[0], right[k], preferred_element_type=jnp.float32)
        gone = exchange(gone, 0)
        total = jnp.dot(left[1], right[k], preferred_element_type=jnp.float32) + gone
        stage = 1
        while (1 << stage) < col_count:
            bit = (col_index >> stage) % 2
            pieces = total.reshape(total.shape[0] // (2 * share), 2, share, width)
            gone = exchange(pick(pieces, 1 - bit), stage)
            total = (pick(pieces, bit) + gone).reshape(-1, width)
            stage += 1
        products.append(total)

    columns = []
    links = []
    diagonals = []
    token = None
    for k in range(STEPS):
        summed = products[k]
        if k > 0:
            summed = summed + dot(columns[-1], parent_panel[k - 1])
        columns.append(-own_masks[k] * summed)
        parts = [dot_t(masked[k], columns[k])]
        if k > 0:
            parts.append(dot_t(columns[k - 1], masked[k]))
        parts = jnp.stack(parts)
        if token is not None:
            parts, token = lax.optimization_barrier((parts, token))
        token = lax.psum(parts, ("row", "col"))
        diagonal = dot_t(diag_inverse[k], diag_inverse[k]) - token[0]
        if k > 0:
            parent = parent_panel[k - 1]
            links.append(-(token[1] + dot(diagonals[-1], parent)))
            diagonal = diagonal - dot_t(parent, links[-1])
        diagonals.append(diagonal)
    link_stack = lax.dynamic_slice_in_dim(jnp.stack(links), row_index * out_rows, out_rows, 1)
    diag_stack = lax.dynamic_slice_in_dim(jnp.stack(diagonals), row_index * out_rows, out_rows, 1)
    return (jnp.stack(columns), link_stack, diag_stack)


def solution(mesh):
    return jax.shard_map(
        shards,
        mesh=mesh,
        in_specs=(P("row", "col"), P(None, ("row", "col"), None), P(), P(), P()),
        out_specs=(P(None, ("row", "col"), None), P(None, "row", None), P(None, "row", None)),
        check_vma=False,
    )
```

time: 1080 us -> 973 us (0.901)
  matrix products: 180 us -> 76.7 us
  waiting for transfers between devices: 844 us -> 754 us
  starting transfers between devices: 0.4 us -> 76.1 us
  other arithmetic: 16.4 us -> 30.3 us
    reduce_scatter x4 -> x0, waiting for transfers between devices: 251 us -> none  [shards(): lax.psum_scatter(panel_term(jnp.int32(0), share_rows * lax.axis_size('col...]
    psum x2 -> x4, waiting for transfers between devices: 303 us -> 509 us  [shards(): token = lax.psum(parts, ('row', 'col'))]
    all_gather x4, waiting for transfers between devices: 288 us -> 89.2 us  [shards(): whole = lax.all_gather(part, 'row', axis=0, tiled=True)]
    ppermute x0 -> x16, waiting for transfers between devices: none -> 157 us  [the longest x12 156 us: exchange(): lax.ppermute(value, 'col', [(c, c ^ 1 << stage) for c in range(col_count)])]
    dot_general x24 -> x28, matrix products: 180 us -> 76.7 us  [the longest x14 29.3 us: dot_t(): lax.dot_general(a, b, (((0,), (0,)), ((), ())), precision=HIGH, preferred...]
    ppermute x0 -> x16, starting transfers between devices: none -> 75.4 us  [the longest x12 72.7 us: exchange(): lax.ppermute(value, 'col', [(c, c ^ 1 << stage) for c in range(col_count)])]
    convert_element_type x0 -> x6, other arithmetic: none -> 15.6 us  [split(): return (upper.astype(jnp.bfloat16), (value - upper).astype(jnp.bfloat16))]
    select_n x6 -> x0, other arithmetic: 12.6 us -> none  [the longest x4 12.6 us: broadcast(): return lax.psum(jnp.where(mine, value, jnp.zeros_like(value)), axis)]
  transfers between devices with their start and end apart: 10 -> 24, of which waited for: 9 -> 12; matrix products, arithmetic and copies ran while one was open for 13% -> 11% of each run, Pallas kernels for 0% -> 0%
where the time goes in v1:
time: 973 us; the launch traced here: 969 us
  waiting for transfers between devices  754 us (77%)
  matrix products  76.7 us (8%)
  starting transfers between devices  76.1 us (8%)
  other arithmetic  30.3 us (3%)
  local copies, waits for them, and re-layouts  16.7 us (2%)
  between operations  15.1 us (2%)
    psum x4, waiting for transfers between devices, shards(): token = lax.psum(parts, ('row', 'col'))  509 us
    ppermute x12, waiting for transfers between devices, exchange(): lax.ppermute(value, 'col', [(c, c ^ 1 << stage) for c in range(col_count)])  156 us
    all_gather x4, waiting for transfers between devices, shards(): whole = lax.all_gather(part, 'row', axis=0, tiled=True)  89.2 us
    ppermute x12, starting transfers between devices, exchange(): lax.ppermute(value, 'col', [(c, c ^ 1 << stage) for c in range(col_count)])  72.7 us
    dot_general x14, matrix products, dot_t(): lax.dot_general(a, b, (((0,), (0,)), ((), ())), precision=HIGH, preferred...  29.3 us
  transfers between devices with their start and end apart: 24, of which 12 were waited for; matrix products, arithmetic and copies ran while one was open for 11% of the time, Pallas kernels for 0%

profile of v1, /device:TPU:0, one launch (start us, length us, event | category | flops | bytes accessed | tf_op | source)
XLA Modules:
  0.0 969.4 jit_solution(6063693176812613222)
XLA Ops:
  8.0 1.7 bitcast_multiply_fusion
  15.2 6.7 constant_dynamic-slice_fusion.5
  22.0 2.2 fusion.1
  24.2 5.1 fusion
  30.4 56.2 %all-gather.5.cloned.1.call-done = f32[1024,512]{1,0:T(8,128)} async-done(((f32[256,512]{1,0:T(8,128)}), f32[1024,512]{1,0:T(8,128)}) %all-gather.5.cloned.1.call-update) | async-done | bytes 2097168 | tf_op jit(solution)/shard_map/all_gather | solution.py:58
  86.6 2.1 reduce-precision_convert_fusion.5
  88.8 4.7 fusion.12
  93.5 35.0 %collective-permute-start.1 = (f32[1024,512]{1,0:T(8,128)}, f32[1024,512]{1,0:T(8,128)}, u32[]{:S(2)}, u32[]{:S(2)}) collective-permute-start(f32[1024,512]{1,0:T(8,128)} %fusion.12), channel_id=1, source_target_pairs={{0,1},{1,0},{2,3},{3,2},{4,5},{5,4},{6,7},{7,6},{8,9},{9,8},{10,11... | collective-permute-start | bytes 6291464 | tf_op jit(solution)/shard_map/ppermute | solution.py:70
  128.4 2.1 reduce-precision_convert_fusion.4
  130.7 4.7 fusion.10
  135.4 15.8 %all-gather.9.cloned.1.call-done = f32[1024,512]{1,0:T(8,128)} async-done(((f32[256,512]{1,0:T(8,128)}), f32[1024,512]{1,0:T(8,128)}) %all-gather.9.cloned.1.call-update) | async-done | bytes 2097168 | tf_op jit(solution)/shard_map/all_gather | solution.py:58
  151.2 2.1 reduce-precision_convert_fusion.3
  153.5 4.7 fusion.8
  159.7 17.2 %all-gather.11.cloned.1.call-done = f32[1024,512]{1,0:T(8,128)} async-done(((f32[256,512]{1,0:T(8,128)}), f32[1024,512]{1,0:T(8,128)}) %all-gather.11.cloned.1.call-update) | async-done | bytes 2097168 | tf_op jit(solution)/shard_map/all_gather | solution.py:58
  176.9 2.1 reduce-precision_convert_fusion.2
  179.1 4.7 fusion.6
  185.4 5.6 fusion.14
  192.6 27.6 %collective-permute-done.5 = f32[1024,512]{1,0:T(8,128)} collective-permute-done((f32[1024,512]{1,0:T(8,128)}, f32[1024,512]{1,0:T(8,128)}, u32[]{:S(2)}, u32[]{:S(2)}) %collective-permute-start.5) | collective-permute-done | bytes 2097184 | tf_op jit(solution)/shard_map/ppermute | solution.py:70
  220.2 5.0 fusion.15
  226.7 38.5 %collective-permute-done.9 = f32[1024,512]{1,0:T(8,128)} collective-permute-done((f32[1024,512]{1,0:T(8,128)}, f32[1024,512]{1,0:T(8,128)}, u32[]{:S(2)}, u32[]{:S(2)}) %collective-permute-start.9) | collective-permute-done | bytes 2097184 | tf_op jit(solution)/shard_map/ppermute | solution.py:70
  265.2 5.0 fusion.16
  271.6 29.3 %collective-permute-done.13 = f32[1024,512]{1,0:T(8,128)S(1)} collective-permute-done((f32[1024,512]{1,0:T(8,128)}, f32[1024,512]{1,0:T(8,128)S(1)}, u32[]{:S(2)}, u32[]{:S(2)}) %collective-permute-start.13) | collective-permute-done | bytes 2097184 | tf_op jit(solution)/shard_map/ppermute | solution.py:70
  300.9 3.4 fusion.17
  304.4 10.6 %collective-permute-start.14 = (f32[2,256,512]{2,1,0:T(8,128)S(1)}, f32[2,256,512]{2,1,0:T(8,128)S(1)}, u32[]{:S(2)}, u32[]{:S(2)}) collective-permute-start(f32[2,256,512]{2,1,0:T(8,128)S(1)} %dynamic-slice_bitcast_fusion), channel_id=1, source_target_pairs={{0,2},{1,3},{2,0},{3,1},{4,6},{5,7},{6,4},{7,5},{8,10},{9,11},{10,... | collective-permute-start | bytes 3145736 | tf_op jit(solution)/shard_map/ppermute | solution.py:70
  315.2 13.1 %collective-permute-start.3 = (f32[1,256,512]{2,1,0:T(8,128)S(1)}, f32[1,256,512]{2,1,0:T(8,128)S(1)}, u32[]{:S(2)}, u32[]{:S(2)}) collective-permute-start(f32[1,256,512]{2,1,0:T(8,128)S(1)} %constant_dynamic-slice_fusion.3), channel_id=1, source_target_pairs={{0,4},{1,5},{2,6},{3,7},{4,0},{5,1},{6,2},{7,3},{8,12},{9,13},{10,... | collective-permute-start | bytes 1572872 | tf_op jit(solution)/shard_map/ppermute | solution.py:70
  330.7 2.9 collective-permute-start.11
  333.6 23.2 %collective-permute-done.14 = f32[2,256,512]{2,1,0:T(8,128)S(1)} collective-permute-done((f32[2,256,512]{2,1,0:T(8,128)S(1)}, f32[2,256,512]{2,1,0:T(8,128)S(1)}, u32[]{:S(2)}, u32[]{:S(2)}) %collective-permute-start.14) | collective-permute-done | bytes 1048608 | tf_op jit(solution)/shard_map/ppermute | solution.py:70
  357.9 3.9 collective-permute-start.15
  362.7 2.7 convolution_bitcast_fusion.7
  365.5 2.1 fusion.66
  367.7 37.9 %collective-permute-done.11 = f32[1,256,512]{2,1,0:T(8,128)} collective-permute-done((f32[1,256,512]{2,1,0:T(8,128)}, f32[1,256,512]{2,1,0:T(8,128)}, u32[]{:S(2)}, u32[]{:S(2)}) %collective-permute-start.11) | collective-permute-done | bytes 524320 | tf_op jit(solution)/shard_map/ppermute | solution.py:70
  407.9 1.7 convolution_bitcast_fusion.8
  412.8 125.7 %all-reduce.5.cloned.1.call-done = f32[1,512,512]{2,1,0:T(8,128)} async-done(((f32[1,512,512]{2,1,0:T(8,128)}), f32[1,512,512]{2,1,0:T(8,128)}) %all-reduce.5.cloned.1.call-update) | async-done | bytes 1048592 | tf_op jit(solution)/shard_map/psum | solution.py:101
  538.6 2.9 convolution_bitcast_fusion.6
  541.5 2.9 convolution_bitcast_fusion.5
  544.3 1.7 fusion.61
  549.0 3.2 pad_maximum_fusion.8
  552.2 125.7 %all-reduce.7.cloned.1.call-done = f32[2,512,512]{2,1,0:T(8,128)} async-done(((f32[2,512,512]{2,1,0:T(8,128)}), f32[2,512,512]{2,1,0:T(8,128)}) %all-reduce.7.cloned.1.call-update) | async-done | bytes 2097168 | tf_op jit(solution)/shard_map/psum | solution.py:101
  678.1 3.2 pad_maximum_fusion.6
  681.3 2.4 convolution_subtract_fusion.3
  683.7 2.1 convolution_subtract_fusion.2
  685.8 2.0 fusion.24
  687.8 128.1 %all-reduce.9.cloned.1.call-done = f32[2,512,512]{2,1,0:T(8,128)} async-done(((f32[2,512,512]{2,1,0:T(8,128)}), f32[2,512,512]{2,1,0:T(8,128)}) %all-reduce.9.cloned.1.call-update) | async-done | bytes 2097168 | tf_op jit(solution)/shard_map/psum | solution.py:101
  815.9 2.7 fusion.23
  818.6 2.9 convolution_subtract_fusion.1
  823.6 2.1 fusion.21
  825.7 129.1 %all-reduce.11.cloned.1.call-done = f32[2,512,512]{2,1,0:T(8,128)} async-done(((f32[2,512,512]{2,1,0:T(8,128)}), f32[2,512,512]{2,1,0:T(8,128)}) %all-reduce.11.cloned.1.call-update) | async-done | bytes 2097168 | tf_op jit(solution)/shard_map/psum | solution.py:101
  954.8 3.0 convolution_subtract_fusion
  (172 shorter events, 35.0 us)
Async XLA Ops:
  7.2 79.4 %all-gather.5.cloned.1.call-start = ((), (), s32[]{:S(2)}) async-start(), calls=%async_computation | async-start | bytes 2621440 | tf_op jit(solution)/shard_map/all_gather | solution.py:58
  9.7 12.2 %copy-start.14 = (f32[256,512]{1,0:T(8,128)}, f32[256,512]{1,0:T(8,128)S(1)}, u32[]{:S(2)}) copy-start(f32[256,512]{1,0:T(8,128)S(1)} %get-tuple-element.17) | copy-start | bytes 1572868
  9.7 12.2 %copy-start.17 = (f32[256,512]{1,0:T(8,128)}, f32[256,512]{1,0:T(8,128)S(1)}, u32[]{:S(2)}) copy-start(f32[256,512]{1,0:T(8,128)S(1)} %get-tuple-element.20) | copy-start | bytes 1572868
  9.7 12.2 %copy-start.29 = (f32[256,512]{1,0:T(8,128)}, f32[256,512]{1,0:T(8,128)S(1)}, u32[]{:S(2)}) copy-start(f32[256,512]{1,0:T(8,128)S(1)} %get-tuple-element.18) | copy-start | bytes 1572868
  9.8 0.7 collective-permute-start
  11.3 117.2 %all-gather.7.cloned.1.call-start = ((), (), s32[]{:S(2)}) async-start(), calls=%async_computation.1 | async-start | bytes 2621440 | tf_op jit(solution)/shard_map/all_gather | solution.py:58
  11.3 0.7 collective-permute-start.4
  12.9 138.4 %all-gather.9.cloned.1.call-start = ((), (), s32[]{:S(2)}) async-start(), calls=%async_computation.2 | async-start | bytes 2621440 | tf_op jit(solution)/shard_map/all_gather | solution.py:58
  12.9 0.7 collective-permute-start.8
  14.4 162.4 %all-gather.11.cloned.1.call-start = ((), (), s32[]{:S(2)}) async-start(), calls=%async_computation.3 | async-start | bytes 2621440 | tf_op jit(solution)/shard_map/all_gather | solution.py:58
  14.5 14.9 %collective-permute-start.12 = (f32[256,512]{1,0:T(8,128)S(1)}, f32[256,512]{1,0:T(8,128)S(1)}, u32[]{:S(2)}, u32[]{:S(2)}) collective-permute-start(f32[256,512]{1,0:T(8,128)S(1)} %get-tuple-element.17), channel_id=1, source_target_pairs={{0,0},{1,8},{2,16},{3,24},{4,1},{5,9},{6,17},{7,25},{8,2},{9,10},{... | collective-permute-start | bytes 1572872 | tf_op jit(solution)/shard_map/ppermute | solution.py:57
  30.2 508.3 %all-reduce.5.cloned.1.call-start = ((), (), s32[]{:S(2)}) async-start(), calls=%async_computation.4 | async-start | bytes 2097152 | tf_op jit(solution)/shard_map/psum | solution.py:101
  93.5 91.8 %collective-permute-start.1 = (f32[1024,512]{1,0:T(8,128)}, f32[1024,512]{1,0:T(8,128)}, u32[]{:S(2)}, u32[]{:S(2)}) collective-permute-start(f32[1024,512]{1,0:T(8,128)} %fusion.12), channel_id=1, source_target_pairs={{0,1},{1,0},{2,3},{3,2},{4,5},{5,4},{6,7},{7,6},{8,9},{9,8},{10,11... | collective-permute-start | bytes 6291464 | tf_op jit(solution)/shard_map/ppermute | solution.py:70
  130.5 4.9 copy-start.41
  135.4 84.8 %collective-permute-start.5 = (f32[1024,512]{1,0:T(8,128)}, f32[1024,512]{1,0:T(8,128)}, u32[]{:S(2)}, u32[]{:S(2)}) collective-permute-start(f32[1024,512]{1,0:T(8,128)} %fusion.10), channel_id=1, source_target_pairs={{0,1},{1,0},{2,3},{3,2},{4,5},{5,4},{6,7},{7,6},{8,9},{9,8},{10,11... | collective-permute-start | bytes 6291464 | tf_op jit(solution)/shard_map/ppermute | solution.py:70
  153.3 4.9 copy-start.45
  158.2 107.0 %collective-permute-start.9 = (f32[1024,512]{1,0:T(8,128)}, f32[1024,512]{1,0:T(8,128)}, u32[]{:S(2)}, u32[]{:S(2)}) collective-permute-start(f32[1024,512]{1,0:T(8,128)} %fusion.8), channel_id=1, source_target_pairs={{0,1},{1,0},{2,3},{3,2},{4,5},{5,4},{6,7},{7,6},{8,9},{9,8},{10,11... | collective-permute-start | bytes 6291464 | tf_op jit(solution)/shard_map/ppermute | solution.py:70
  179.1 6.2 copy-start.35
  179.1 6.2 copy-start.36
  179.1 6.2 copy-start.38
  179.1 6.2 copy-start.40
  183.9 117.0 %collective-permute-start.13 = (f32[1024,512]{1,0:T(8,128)}, f32[1024,512]{1,0:T(8,128)S(1)}, u32[]{:S(2)}, u32[]{:S(2)}) collective-permute-start(f32[1024,512]{1,0:T(8,128)} %fusion.6), channel_id=1, source_target_pairs={{0,1},{1,0},{2,3},{3,2},{4,5},{5,4},{6,7},{7,6},{8,9},{9,8},{10,11... | collective-permute-start | bytes 6291464 | tf_op jit(solution)/shard_map/ppermute | solution.py:70
  185.4 34.9 %copy-start.42 = (bf16[1024,512]{1,0:T(8,128)(2,1)S(1)}, bf16[1024,512]{1,0:T(8,128)(2,1)}, u32[]{:S(2)}) copy-start(bf16[1024,512]{1,0:T(8,128)(2,1)} %copy-done.41) | copy-start | bytes 3145732
  185.4 34.9 %copy-start.44 = (bf16[1024,512]{1,0:T(8,128)(2,1)S(1)}, bf16[1024,512]{1,0:T(8,128)(2,1)}, u32[]{:S(2)}) copy-start(bf16[1024,512]{1,0:T(8,128)(2,1)} %copy-done.43) | copy-start | bytes 3145732
  191.0 74.1 %copy-start.46 = (bf16[1024,512]{1,0:T(8,128)(2,1)S(1)}, bf16[1024,512]{1,0:T(8,128)(2,1)}, u32[]{:S(2)}) copy-start(bf16[1024,512]{1,0:T(8,128)(2,1)} %copy-done.45) | copy-start | bytes 3145732
  191.1 74.1 %copy-start.48 = (bf16[1024,512]{1,0:T(8,128)(2,1)S(1)}, bf16[1024,512]{1,0:T(8,128)(2,1)}, u32[]{:S(2)}) copy-start(bf16[1024,512]{1,0:T(8,128)(2,1)} %copy-done.47) | copy-start | bytes 3145732
  191.1 123.9 %collective-permute-start.2 = (f32[2,256,512]{2,1,0:T(8,128)S(1)}, f32[2,256,512]{2,1,0:T(8,128)S(1)}, u32[]{:S(2)}, u32[]{:S(2)}) collective-permute-start(f32[2,256,512]{2,1,0:T(8,128)S(1)} %dynamic-slice_bitcast_fusion.3), channel_id=1, source_target_pairs={{0,2},{1,3},{2,0},{3,1},{4,6},{5,7},{6,4},{7,5},{8,10},{9,11},{10,... | collective-permute-start | bytes 3145736 | tf_op jit(solution)/shard_map/ppermute | solution.py:70
  225.3 103.0 %collective-permute-start.6 = (f32[2,256,512]{2,1,0:T(8,128)S(1)}, f32[2,256,512]{2,1,0:T(8,128)S(1)}, u32[]{:S(2)}, u32[]{:S(2)}) collective-permute-start(f32[2,256,512]{2,1,0:T(8,128)S(1)} %dynamic-slice_bitcast_fusion.2), channel_id=1, source_target_pairs={{0,2},{1,3},{2,0},{3,1},{4,6},{5,7},{6,4},{7,5},{8,10},{9,11},{10,... | collective-permute-start | bytes 3145736 | tf_op jit(solution)/shard_map/ppermute | solution.py:70
  270.3 59.2 %collective-permute-start.10 = (f32[2,256,512]{2,1,0:T(8,128)S(1)}, f32[2,256,512]{2,1,0:T(8,128)S(1)}, u32[]{:S(2)}, u32[]{:S(2)}) collective-permute-start(f32[2,256,512]{2,1,0:T(8,128)S(1)} %dynamic-slice_bitcast_fusion.1), channel_id=1, source_target_pairs={{0,2},{1,3},{2,0},{3,1},{4,6},{5,7},{6,4},{7,5},{8,10},{9,11},{10,... | collective-permute-start | bytes 3145736 | tf_op jit(solution)/shard_map/ppermute | solution.py:70
  304.4 52.4 %collective-permute-start.14 = (f32[2,256,512]{2,1,0:T(8,128)S(1)}, f32[2,256,512]{2,1,0:T(8,128)S(1)}, u32[]{:S(2)}, u32[]{:S(2)}) collective-permute-start(f32[2,256,512]{2,1,0:T(8,128)S(1)} %dynamic-slice_bitcast_fusion), channel_id=1, source_target_pairs={{0,2},{1,3},{2,0},{3,1},{4,6},{5,7},{6,4},{7,5},{8,10},{9,11},{10,... | collective-permute-start | bytes 3145736 | tf_op jit(solution)/shard_map/ppermute | solution.py:70
  315.2 46.6 %collective-permute-start.3 = (f32[1,256,512]{2,1,0:T(8,128)S(1)}, f32[1,256,512]{2,1,0:T(8,128)S(1)}, u32[]{:S(2)}, u32[]{:S(2)}) collective-permute-start(f32[1,256,512]{2,1,0:T(8,128)S(1)} %constant_dynamic-slice_fusion.3), channel_id=1, source_target_pairs={{0,4},{1,5},{2,6},{3,7},{4,0},{5,1},{6,2},{7,3},{8,12},{9,13},{10,... | collective-permute-start | bytes 1572872 | tf_op jit(solution)/shard_map/ppermute | solution.py:70
  328.6 5.0 copy-start.22
  329.5 36.0 %collective-permute-start.7 = (f32[1,256,512]{2,1,0:T(8,128)}, f32[1,256,512]{2,1,0:T(8,128)}, u32[]{:S(2)}, u32[]{:S(2)}) collective-permute-start(f32[1,256,512]{2,1,0:T(8,128)} %constant_dynamic-slice_fusion.2), channel_id=1, source_target_pairs={{0,4},{1,5},{2,6},{3,7},{4,0},{5,1},{6,2},{7,3},{8,12},{9,13},{10,... | collective-permute-start | bytes 1572872 | tf_op jit(solution)/shard_map/ppermute | solution.py:70
  329.7 32.2 %copy-start.23 = (f32[2,256,512]{2,1,0:T(8,128)}, f32[2,256,512]{2,1,0:T(8,128)S(1)}, u32[]{:S(2)}) copy-start(f32[2,256,512]{2,1,0:T(8,128)S(1)} %bitcast_add_fusion.1) | copy-start | bytes 3145732
  330.7 74.8 %collective-permute-start.11 = (f32[1,256,512]{2,1,0:T(8,128)}, f32[1,256,512]{2,1,0:T(8,128)}, u32[]{:S(2)}, u32[]{:S(2)}) collective-permute-start(f32[1,256,512]{2,1,0:T(8,128)} %constant_dynamic-slice_fusion.1), channel_id=1, source_target_pairs={{0,4},{1,5},{2,6},{3,7},{4,0},{5,1},{6,2},{7,3},{8,12},{9,13},{10,... | collective-permute-start | bytes 1572872 | tf_op jit(solution)/shard_map/ppermute | solution.py:70
  357.1 8.5 copy-start
  357.9 186.4 %collective-permute-start.15 = (f32[1,256,512]{2,1,0:T(8,128)}, f32[1,256,512]{2,1,0:T(8,128)}, u32[]{:S(2)}, u32[]{:S(2)}) collective-permute-start(f32[1,256,512]{2,1,0:T(8,128)} %constant_dynamic-slice_fusion), channel_id=1, source_target_pairs={{0,4},{1,5},{2,6},{3,7},{4,0},{5,1},{6,2},{7,3},{8,12},{9,13},{10,... | collective-permute-start | bytes 1572872 | tf_op jit(solution)/shard_map/ppermute | solution.py:70
  365.4 312.4 %all-reduce.7.cloned.1.call-start = ((), (), s32[]{:S(2)}) async-start(), calls=%async_computation.5 | async-start | bytes 4194304 | tf_op jit(solution)/shard_map/psum | solution.py:101
  365.5 40.0 %copy-start.24 = (f32[2,256,512]{2,1,0:T(8,128)S(1)}, f32[2,256,512]{2,1,0:T(8,128)}, u32[]{:S(2)}) copy-start(f32[2,256,512]{2,1,0:T(8,128)} %copy-done.23) | copy-start | bytes 3145732
  365.5 41.7 %copy-start.30 = (f32[256,512]{1,0:T(8,128)S(1)}, f32[256,512]{1,0:T(8,128)}, u32[]{:S(2)}) copy-start(f32[256,512]{1,0:T(8,128)} %copy-done.29) | copy-start | bytes 1572868
  367.6 42.0 %copy-start.3 = (f32[256,512]{1,0:T(8,128)}, f32[256,512]{1,0:T(8,128)S(1)}, u32[]{:S(2)}) copy-start(f32[256,512]{1,0:T(8,128)S(1)} %fusion.66) | copy-start | bytes 1572868
  367.6 40.3 %copy-start.2 = (f32[1,256,512]{2,1,0:T(8,128)S(1)}, f32[1,256,512]{2,1,0:T(8,128)}, u32[]{:S(2)}) copy-start(f32[1,256,512]{2,1,0:T(8,128)} %copy-done.1) | copy-start | bytes 1572868
  538.5 277.4 %all-reduce.9.cloned.1.call-start = ((), (), s32[]{:S(2)}) async-start(), calls=%async_computation.6 | async-start | bytes 4194304 | tf_op jit(solution)/shard_map/psum | solution.py:101
  538.5 5.8 copy-start.5
  538.5 5.8 copy-start.21
  541.5 5.4 copy-start.16
  677.9 276.9 %all-reduce.11.cloned.1.call-start = ((), (), s32[]{:S(2)}) async-start(), calls=%async_computation.7 | async-start | bytes 4194304 | tf_op jit(solution)/shard_map/psum | solution.py:101
  678.1 5.5 copy-start.26
  (29 other events, 74.3 us)
Sparse Core Ops, SparseCore 0:
  11.4 75.1 all-gather.4
  88.1 27.3 all-gather.6
  117.6 33.5 all-gather.8
  153.2 23.6 all-gather.10
  365.6 172.8 all-reduce.4
  545.1 132.7 all-reduce.6
  683.2 132.6 all-reduce.8
  822.1 132.6 all-reduce.10

commit v2 on v1

--- a/solution.py
+++ b/solution.py
@@ -30,6 +30,12 @@
     return jnp.sum(matched * block_depth[None, :], axis=1)
 
 
+def after(value, earlier):
+    if earlier is None:
+        return value
+    return lax.optimization_barrier((value, earlier))[0]
+
+
 def pick(value, which):
     return lax.dynamic_index_in_dim(value, which, 1, keepdims=False)
 
@@ -53,8 +59,9 @@
         (g, (g % row_count) * col_count + g // row_count) for g in range(row_count * col_count)
     ]
     right = []
+    part = None
     for k in range(STEPS):
-        part = lax.ppermute(masked[k], ("row", "col"), swap)
+        part = lax.ppermute(after(masked[k], part), ("row", "col"), swap)
         whole = lax.all_gather(part, "row", axis=0, tiled=True)
         upper, lower = split(whole)
         right.append(jnp.concatenate([upper, upper, lower], axis=0))
@@ -66,48 +73,70 @@
         upper, lower = split(pick(pairs, which).reshape(col_count // 2 * share, depth))
         left.append(jnp.concatenate([upper, lower, upper], axis=1))
 
-    def exchange(value, stage):
-        return lax.ppermute(value, "col", [(c, c ^ (1 << stage)) for c in range(col_count)])
+    def exchange(value, axis, stage):
+        count = lax.axis_size(axis)
+        return lax.ppermute(value, axis, [(i, i ^ (1 << stage)) for i in range(count)])
 
-    products = []
+    def reduce_slab(parts):
+        for stage in range(row_count.bit_length() - 1):
+            halves = parts.reshape(parts.shape[0], -1, 2, out_rows, width)
+            bit = (row_index >> stage) % 2
+            gone = lax.dynamic_index_in_dim(halves, 1 - bit, 2, keepdims=False)
+            kept = lax.dynamic_index_in_dim(halves, bit, 2, keepdims=False)
+            parts = kept + exchange(gone, "row", stage)
+        parts = parts.reshape(-1, out_rows, width)
+        for stage in range(col_count.bit_length() - 1):
+            parts = parts + exchange(parts, "col", stage)
+        return parts
+
+    columns = []
+    diag_sums = []
+    cross_sums = []
+    nearer = []
     for k in range(STEPS):
         gone = jnp.dot(left[0], right[k], preferred_element_type=jnp.float32)
-        gone = exchange(gone, 0)
+        gone = exchange(after(gone, nearer[k - 2] if k > 1 else None), "col", 0)
         total = jnp.dot(left[1], right[k], preferred_element_type=jnp.float32) + gone
-        stage = 1
-        while (1 << stage) < col_count:
+        for stage in range(1, col_count.bit_length() - 1):
             bit = (col_index >> stage) % 2
             pieces = total.reshape(total.shape[0] // (2 * share), 2, share, width)
-            gone = exchange(pick(pieces, 1 - bit), stage)
+            gone = exchange(pick(pieces, 1 - bit), "col", stage)
             total = (pick(pieces, bit) + gone).reshape(-1, width)
-            stage += 1
-        products.append(total)
+            if stage == 1:
+                nearer.append(gone)
+        if k > 0:
+            total = total + dot(columns[-1], parent_panel[k - 1])
+        columns.append(-own_masks[k] * total)
+        parts = [dot_t(masked[k], columns[k])]
+        if k + 1 < STEPS:
+            parts.append(dot_t(columns[k], masked[k + 1]))
+        slab = reduce_slab(jnp.stack(parts))
+        if k + 1 < STEPS:
+            sums = lax.all_gather(slab, "row", axis=1, tiled=True)
+            diag_sums.append(sums[0])
+            cross_sums.append(sums[1])
 
-    columns = []
+    def own_slab(value):
+        return lax.dynamic_slice_in_dim(value, row_index * out_rows, out_rows, 0)
+
+    def own_columns(value):
+        return lax.dynamic_slice_in_dim(value, row_index * out_rows, out_rows, 1)
+
     links = []
     diagonals = []
-    token = None
-    for k in range(STEPS):
-        summed = products[k]
+    for k in range(STEPS - 1):
+        diagonal = dot_t(diag_inverse[k], diag_inverse[k]) - diag_sums[k]
         if k > 0:
-            summed = summed + dot(columns[-1], parent_panel[k - 1])
-        columns.append(-own_masks[k] * summed)
-        parts = [dot_t(masked[k], columns[k])]
-        if k > 0:
-            parts.append(dot_t(columns[k - 1], masked[k]))
-        parts = jnp.stack(parts)
-        if token is not None:
-            parts, token = lax.optimization_barrier((parts, token))
-        token = lax.psum(parts, ("row", "col"))
-        diagonal = dot_t(diag_inverse[k], diag_inverse[k]) - token[0]
-        if k > 0:
-            parent = parent_panel[k - 1]
-            links.append(-(token[1] + dot(diagonals[-1], parent)))
-            diagonal = diagonal - dot_t(parent, links[-1])
+            diagonal = diagonal - dot_t(parent_panel[k - 1], links[-1])
         diagonals.append(diagonal)
-    link_stack = lax.dynamic_slice_in_dim(jnp.stack(links), row_index * out_rows, out_rows, 1)
-    diag_stack = lax.dynamic_slice_in_dim(jnp.stack(diagonals), row_index * out_rows, out_rows, 1)
-    return (jnp.stack(columns), link_stack, diag_stack)
+        links.append(-(cross_sums[k] + dot(diagonal, parent_panel[k])))
+    last = dot_t(own_columns(diag_inverse[-1]), diag_inverse[-1])
+    last = last - dot_t(own_columns(parent_panel[-1]), links[-1]) - slab[0]
+    return (
+        jnp.stack(columns),
+        jnp.stack([own_slab(value) for value in links]),
+        jnp.stack([own_slab(value) for value in diagonals] + [last]),
+    )
 
 
 def solution(mesh):

time: 973 us -> 607 us (0.62)
  waiting for transfers between devices: 754 us -> 325 us
  local copies, waits for them, and re-layouts: 16.7 us -> 41.6 us
  other arithmetic: 30.3 us -> 54.1 us
  starting transfers between devices: 76.1 us -> 87.4 us
    psum x4 -> x0, waiting for transfers between devices: 509 us -> none  [shards(): token = lax.psum(parts, ('row', 'col'))]
    ppermute x16 -> x36, waiting for transfers between devices: 157 us -> 252 us  [the longest x32 252 us: exchange(): lax.ppermute(value, axis, [(i, i ^ 1 << stage) for i in range(count)])]
    all_gather x4, waiting for transfers between devices: 89.2 us -> 73.6 us  [shards(): whole = lax.all_gather(part, 'row', axis=0, tiled=True)]
    another operation x0 -> x13, local copies, waits for them, and re-layouts: none -> 15.3 us
    add x0 -> x15, other arithmetic: none -> 14.1 us  [the longest x11 10.3 us: reduce_slab(): parts = parts + exchange(parts, 'col', stage)]
    ppermute x16 -> x36, starting transfers between devices: 75.4 us -> 86.7 us  [the longest x32 83.2 us: exchange(): lax.ppermute(value, axis, [(i, i ^ 1 << stage) for i in range(count)])]
  transfers between devices with their start and end apart: 24 -> 43, of which waited for: 12 -> 20; matrix products, arithmetic and copies ran while one was open for 11% -> 26% of each run, Pallas kernels for 0% -> 0%
where the time goes in v2:
time: 607 us; the launch traced here: 601 us
  waiting for transfers between devices  325 us (54%)
  starting transfers between devices  87.4 us (14%)
  matrix products  76.8 us (13%)
  other arithmetic  54.1 us (9%)
  local copies, waits for them, and re-layouts  41.6 us (7%)
  between operations  15.4 us (3%)
    ppermute x32, waiting for transfers between devices, exchange(): lax.ppermute(value, axis, [(i, i ^ 1 << stage) for i in range(count)])  252 us
    ppermute x32, starting transfers between devices, exchange(): lax.ppermute(value, axis, [(i, i ^ 1 << stage) for i in range(count)])  83.2 us
    all_gather x4, waiting for transfers between devices, shards(): whole = lax.all_gather(part, 'row', axis=0, tiled=True)  73.6 us
    dot_general x14, matrix products, dot_t(): lax.dot_general(a, b, (((0,), (0,)), ((), ())), precision=HIGH, preferred...  27.9 us
    dot_general x4, matrix products, shards(): jnp.dot(left[1], right[k], preferred_element_type=jnp.float32) + gone  21.9 us
    dot_general x4, matrix products, shards(): gone = jnp.dot(left[0], right[k], preferred_element_type=jnp.float32)  18.9 us
    convert_element_type x6, other arithmetic, split(): return (upper.astype(jnp.bfloat16), (value - upper).astype(jnp.bfloat16))  17.6 us
    another operation x7, local copies, waits for them, and re-layouts  12.3 us
  transfers between devices with their start and end apart: 43, of which 20 were waited for; matrix products, arithmetic and copies ran while one was open for 26% of the time, Pallas kernels for 0%

profile of v2, /device:TPU:0, one launch (start us, length us, event | category | flops | bytes accessed | tf_op | source)
XLA Modules:
  0.0 600.5 jit_solution(8765199740465812437)
XLA Ops:
  13.6 6.8 %constant_dynamic-slice_fusion.8 = (f32[4,1,256,1024]{3,2,1,0:T(8,128)}, f32[4,1,256,1024]{3,2,1,0:T(8,128)S(1)}) fusion(f32[4,2,256,1024]{3,2,1,0:T(8,128)} %bitcast.294, s32[]{:T(128)S(6)} %select_n.171, s32[]{:T(128)S(6)} %select_n.172), kind=kLoop, calls=%fused_computation.191 | loop fusion | bytes 16777224 | tf_op jit(solution)/shard_map/jit(dynamic_index_in_dim)/dynamic_slice | solution.py:40
  20.4 2.9 fusion.1
  24.2 60.6 %all-gather.8.cloned.1.call-done = f32[1024,512]{1,0:T(8,128)} async-done(((f32[256,512]{1,0:T(8,128)}), f32[1024,512]{1,0:T(8,128)}) %all-gather.8.cloned.1.call-update) | async-done | bytes 2097168 | tf_op jit(solution)/shard_map/all_gather | solution.py:65
  87.6 4.7 fusion.12
  92.4 2.7 collective-permute-start.1
  102.6 5.2 fusion
  108.0 13.0 %all-gather.10.cloned.1.call-done = f32[1024,512]{1,0:T(8,128)} async-done(((f32[256,512]{1,0:T(8,128)}), f32[1024,512]{1,0:T(8,128)}) %all-gather.10.cloned.1.call-update) | async-done | bytes 2097168 | tf_op jit(solution)/shard_map/all_gather | solution.py:65
  123.2 29.3 %collective-permute-done.1 = f32[1024,512]{1,0:T(8,128)} collective-permute-done((f32[1024,512]{1,0:T(8,128)}, f32[1024,512]{1,0:T(8,128)}, u32[]{:S(2)}, u32[]{:S(2)}) %collective-permute-start.1) | collective-permute-done | bytes 2097184 | tf_op jit(solution)/shard_map/ppermute | solution.py:78
  152.5 6.1 %fusion.14 = f32[1024,512]{1,0:T(8,128)S(1)} fusion(f32[1024,512]{1,0:T(8,128)} %collective-permute-done.1, bf16[1024,512]{1,0:T(8,128)(2,1)} %copy-done.53, bf16[1024,512]{1,0:T(8,128)(2,1)} %copy-done.52, bf16[1024,1024]{1,0:T(8,128)(2,1)S(1)} %copy-done.47, bf16[1024,1024]{1,0:T(8,128)(2,1)S(1)} %copy-done.44), kind=kOutput, calls=%fused_computation.45 | convolution fusion | flops 3250061312 | bytes 10485760 | tf_op jit(solution)/shard_map/dot_general | solution.py:99
  161.7 4.7 fusion.10
  171.0 12.5 %collective-permute-done.2 = f32[2,256,512]{2,1,0:T(8,128)} collective-permute-done((f32[2,256,512]{2,1,0:T(8,128)}, f32[2,256,512]{2,1,0:T(8,128)}, u32[]{:S(2)}, u32[]{:S(2)}) %collective-permute-start.2) | collective-permute-done | bytes 1048608 | tf_op jit(solution)/shard_map/ppermute | solution.py:78
  184.9 9.7 %collective-permute-start.3 = (f32[1,256,512]{2,1,0:T(8,128)S(1)}, f32[1,256,512]{2,1,0:T(8,128)S(1)}, u32[]{:S(2)}, u32[]{:S(2)}) collective-permute-start(f32[1,256,512]{2,1,0:T(8,128)S(1)} %constant_dynamic-slice_fusion.6), channel_id=1, source_target_pairs={{0,4},{1,5},{2,6},{3,7},{4,0},{5,1},{6,2},{7,3},{8,12},{9,13},{10,... | collective-permute-start | bytes 1572872 | tf_op jit(solution)/shard_map/ppermute | solution.py:78
  194.6 4.7 fusion.8
  199.4 18.1 %collective-permute-done.3 = f32[1,256,512]{2,1,0:T(8,128)S(1)} collective-permute-done((f32[1,256,512]{2,1,0:T(8,128)S(1)}, f32[1,256,512]{2,1,0:T(8,128)S(1)}, u32[]{:S(2)}, u32[]{:S(2)}) %collective-permute-start.3) | collective-permute-done | bytes 524320 | tf_op jit(solution)/shard_map/ppermute | solution.py:78
  223.7 5.4 fusion.15
  230.2 28.1 %collective-permute-done.9 = f32[1024,512]{1,0:T(8,128)} collective-permute-done((f32[1024,512]{1,0:T(8,128)}, f32[1024,512]{1,0:T(8,128)}, u32[]{:S(2)}, u32[]{:S(2)}) %collective-permute-start.9) | collective-permute-done | bytes 2097184 | tf_op jit(solution)/shard_map/ppermute | solution.py:78
  258.3 5.0 fusion.16
  266.6 14.9 %collective-permute-start.17 = (f32[2,1,128,512]{3,2,0,1:T(8,128)}, f32[2,1,128,512]{3,2,0,1:T(8,128)}, u32[]{:S(2)}, u32[]{:S(2)}) collective-permute-start(f32[2,1,128,512]{3,2,0,1:T(8,128)} %constant_dynamic-slice_fusion.2), channel_id=1, source_target_pairs={{0,16},{8,24},{16,0},{24,8},{1,17},{9,25},{17,1},{25,9},{2,18},{10... | collective-permute-start | bytes 1572872 | tf_op jit(solution)/shard_map/ppermute | solution.py:78
  281.5 3.3 reduce-precision_convert_fusion.2
  286.5 10.6 %collective-permute-start.7 = (f32[1,256,512]{2,1,0:T(8,128)S(1)}, f32[1,256,512]{2,1,0:T(8,128)S(1)}, u32[]{:S(2)}, u32[]{:S(2)}) collective-permute-start(f32[1,256,512]{2,1,0:T(8,128)S(1)} %constant_dynamic-slice_fusion.5), channel_id=1, source_target_pairs={{0,4},{1,5},{2,6},{3,7},{4,0},{5,1},{6,2},{7,3},{8,12},{9,13},{10,... | collective-permute-start | bytes 1572872 | tf_op jit(solution)/shard_map/ppermute | solution.py:78
  301.6 5.4 collective-permute-start.11
  307.1 23.7 %collective-permute-done.7 = f32[1,256,512]{2,1,0:T(8,128)S(1)} collective-permute-done((f32[1,256,512]{2,1,0:T(8,128)S(1)}, f32[1,256,512]{2,1,0:T(8,128)S(1)}, u32[]{:S(2)}, u32[]{:S(2)}) %collective-permute-start.7) | collective-permute-done | bytes 524320 | tf_op jit(solution)/shard_map/ppermute | solution.py:78
  334.2 2.9 convolution_bitcast_fusion.5
  337.2 2.9 convolution_bitcast_fusion.4
  350.2 3.9 fusion.21
  354.3 4.7 fusion.6
  360.3 3.2 collective-permute-start.20
  368.1 19.2 %collective-permute-done.20 = f32[2,128,512]{2,1,0:T(8,128)S(1)} collective-permute-done((f32[2,128,512]{2,1,0:T(8,128)S(1)}, f32[2,128,512]{2,1,0:T(8,128)S(1)}, u32[]{:S(2)}, u32[]{:S(2)}) %collective-permute-start.20) | collective-permute-done | bytes 524320 | tf_op jit(solution)/shard_map/ppermute | solution.py:78
  391.6 26.9 %collective-permute-done.23 = f32[2,128,512]{2,1,0:T(8,128)S(1)} collective-permute-done((f32[2,128,512]{2,1,0:T(8,128)S(1)}, f32[2,128,512]{2,1,0:T(8,128)S(1)}, u32[]{:S(2)}, u32[]{:S(2)}) %collective-permute-start.23) | collective-permute-done | bytes 524320 | tf_op jit(solution)/shard_map/ppermute | solution.py:78
  421.7 10.6 %collective-permute-done.24 = f32[2,128,512]{2,1,0:T(8,128)S(1)} collective-permute-done((f32[2,128,512]{2,1,0:T(8,128)S(1)}, f32[2,128,512]{2,1,0:T(8,128)S(1)}, u32[]{:S(2)}, u32[]{:S(2)}) %collective-permute-start.24) | collective-permute-done | bytes 524320 | tf_op jit(solution)/shard_map/ppermute | solution.py:78
  432.5 2.9 collective-permute-start.25
  435.4 5.3 fusion.17
  442.2 15.5 %collective-permute-done.25 = f32[2,128,512]{2,1,0:T(8,128)S(1)} collective-permute-done((f32[2,128,512]{2,1,0:T(8,128)S(1)}, f32[2,128,512]{2,1,0:T(8,128)S(1)}, u32[]{:S(2)}, u32[]{:S(2)}) %collective-permute-start.25) | collective-permute-done | bytes 524320 | tf_op jit(solution)/shard_map/ppermute | solution.py:78
  460.8 5.1 collective-permute-start.27
  465.9 10.1 %collective-permute-done.14 = f32[2,256,512]{2,1,0:T(8,128)} collective-permute-done((f32[2,256,512]{2,1,0:T(8,128)}, f32[2,256,512]{2,1,0:T(8,128)}, u32[]{:S(2)}, u32[]{:S(2)}) %collective-permute-start.14) | collective-permute-done | bytes 1048608 | tf_op jit(solution)/shard_map/ppermute | solution.py:78
  477.5 7.0 %collective-permute-done.27 = f32[2,1,128,512]{3,2,0,1:T(8,128)S(1)} collective-permute-done((f32[2,1,128,512]{3,2,0,1:T(8,128)S(1)}, f32[2,1,128,512]{3,2,0,1:T(8,128)S(1)}, u32[]{:S(2)}, u32[]{:S(2)}) %collective-permute-start.27) | collective-permute-done | bytes 524320 | tf_op jit(solution)/shard_map/ppermute | solution.py:78
  488.2 6.6 %collective-permute-done.28 = f32[2,128,512]{2,1,0:T(8,128)} collective-permute-done((f32[2,128,512]{2,1,0:T(8,128)}, f32[2,128,512]{2,1,0:T(8,128)}, u32[]{:S(2)}, u32[]{:S(2)}) %collective-permute-start.28) | collective-permute-done | bytes 524320 | tf_op jit(solution)/shard_map/ppermute | solution.py:78
  498.2 8.8 %collective-permute-done.15 = f32[1,256,512]{2,1,0:T(8,128)} collective-permute-done((f32[1,256,512]{2,1,0:T(8,128)}, f32[1,256,512]{2,1,0:T(8,128)}, u32[]{:S(2)}, u32[]{:S(2)}) %collective-permute-start.15) | collective-permute-done | bytes 524320 | tf_op jit(solution)/shard_map/ppermute | solution.py:78
  510.4 3.6 collective-permute-done.29
  514.9 3.3 collective-permute-start.30
  519.0 22.8 %collective-permute-done.30 = f32[2,128,512]{2,1,0:T(8,128)} collective-permute-done((f32[2,128,512]{2,1,0:T(8,128)}, f32[2,128,512]{2,1,0:T(8,128)}, u32[]{:S(2)}, u32[]{:S(2)}) %collective-permute-start.30) | collective-permute-done | bytes 524320 | tf_op jit(solution)/shard_map/ppermute | solution.py:78
  548.1 3.6 fusion.45
  558.0 3.3 collective-permute-done.33
  565.3 3.2 collective-permute-done.34
  569.2 3.4 collective-permute-start.35
  572.6 3.0 fusion.38
  579.1 3.1 fusion.35
  585.6 3.1 fusion.31
  (288 shorter events, 119.8 us)
Async XLA Ops:
  7.2 77.6 %all-gather.8.cloned.1.call-start = ((), (), s32[]{:S(2)}) async-start(), calls=%async_computation | async-start | bytes 2621440 | tf_op jit(solution)/shard_map/all_gather | solution.py:65
  9.7 85.3 %copy-start.22 = (f32[256,512]{1,0:T(8,128)}, f32[256,512]{1,0:T(8,128)S(1)}, u32[]{:S(2)}) copy-start(f32[256,512]{1,0:T(8,128)S(1)} %get-tuple-element.11) | copy-start | bytes 1572868
  9.7 0.7 collective-permute-start
  11.3 109.8 %all-gather.10.cloned.1.call-start = ((), (), s32[]{:S(2)}) async-start(), calls=%async_computation.1 | async-start | bytes 2621440 | tf_op jit(solution)/shard_map/all_gather | solution.py:65
  11.3 0.7 collective-permute-start.4
  12.9 156.0 %all-gather.12.cloned.1.call-start = ((), (), s32[]{:S(2)}) async-start(), calls=%async_computation.2 | async-start | bytes 2621440 | tf_op jit(solution)/shard_map/all_gather | solution.py:65
  12.9 10.4 %collective-permute-start.8 = (f32[256,512]{1,0:T(8,128)S(1)}, f32[256,512]{1,0:T(8,128)S(1)}, u32[]{:S(2)}, u32[]{:S(2)}) collective-permute-start(f32[256,512]{1,0:T(8,128)S(1)} %get-tuple-element.9), channel_id=1, source_target_pairs={{0,0},{1,8},{2,16},{3,24},{4,1},{5,9},{6,17},{7,25},{8,2},{9,10},{... | collective-permute-start | bytes 1572872 | tf_op jit(solution)/shard_map/ppermute | solution.py:64
  24.2 257.3 %all-gather.14.cloned.1.call-start = ((), (), s32[]{:S(2)}) async-start(), calls=%async_computation.3 | async-start | bytes 2621440 | tf_op jit(solution)/shard_map/all_gather | solution.py:65
  92.4 60.1 %collective-permute-start.1 = (f32[1024,512]{1,0:T(8,128)}, f32[1024,512]{1,0:T(8,128)}, u32[]{:S(2)}, u32[]{:S(2)}) collective-permute-start(f32[1024,512]{1,0:T(8,128)} %fusion.12), channel_id=1, source_target_pairs={{0,1},{1,0},{2,3},{3,2},{4,5},{5,4},{6,7},{7,6},{8,9},{9,8},{10,11... | collective-permute-start | bytes 6291464 | tf_op jit(solution)/shard_map/ppermute | solution.py:78
  95.0 12.8 %collective-permute-start.12 = (f32[256,512]{1,0:T(8,128)S(1)}, f32[256,512]{1,0:T(8,128)}, u32[]{:S(2)}, u32[]{:S(2)}) collective-permute-start(f32[256,512]{1,0:T(8,128)S(1)} %get-tuple-element.11), channel_id=1, source_target_pairs={{0,0},{1,8},{2,16},{3,24},{4,1},{5,9},{6,17},{7,25},{8,2},{9,10},{... | collective-permute-start | bytes 1572872 | tf_op jit(solution)/shard_map/ppermute | solution.py:64
  107.8 464.7 %all-gather.16.cloned.1.call-start = ((), (), s32[]{:S(2)}) async-start(), calls=%async_computation.4 | async-start | bytes 2621440 | tf_op jit(solution)/shard_map/all_gather | solution.py:115
  159.8 23.7 %collective-permute-start.2 = (f32[2,256,512]{2,1,0:T(8,128)}, f32[2,256,512]{2,1,0:T(8,128)}, u32[]{:S(2)}, u32[]{:S(2)}) collective-permute-start(f32[2,256,512]{2,1,0:T(8,128)} %dynamic-slice_bitcast_fusion.3), channel_id=1, source_target_pairs={{0,2},{1,3},{2,0},{3,1},{4,6},{5,7},{6,4},{7,5},{8,10},{9,11},{10,... | collective-permute-start | bytes 3145736 | tf_op jit(solution)/shard_map/ppermute | solution.py:78
  166.4 54.9 %collective-permute-start.5 = (f32[1024,512]{1,0:T(8,128)}, f32[1024,512]{1,0:T(8,128)}, u32[]{:S(2)}, u32[]{:S(2)}) collective-permute-start(f32[1024,512]{1,0:T(8,128)} %fusion.10), channel_id=1, source_target_pairs={{0,1},{1,0},{2,3},{3,2},{4,5},{5,4},{6,7},{7,6},{8,9},{9,8},{10,11... | collective-permute-start | bytes 6291464 | tf_op jit(solution)/shard_map/ppermute | solution.py:78
  184.9 32.5 %collective-permute-start.3 = (f32[1,256,512]{2,1,0:T(8,128)S(1)}, f32[1,256,512]{2,1,0:T(8,128)S(1)}, u32[]{:S(2)}, u32[]{:S(2)}) collective-permute-start(f32[1,256,512]{2,1,0:T(8,128)S(1)} %constant_dynamic-slice_fusion.6), channel_id=1, source_target_pairs={{0,4},{1,5},{2,6},{3,7},{4,0},{5,1},{6,2},{7,3},{8,12},{9,13},{10,... | collective-permute-start | bytes 1572872 | tf_op jit(solution)/shard_map/ppermute | solution.py:78
  199.4 59.0 %collective-permute-start.9 = (f32[1024,512]{1,0:T(8,128)}, f32[1024,512]{1,0:T(8,128)}, u32[]{:S(2)}, u32[]{:S(2)}) collective-permute-start(f32[1024,512]{1,0:T(8,128)} %fusion.8), channel_id=1, source_target_pairs={{0,1},{1,0},{2,3},{3,2},{4,5},{5,4},{6,7},{7,6},{8,9},{9,8},{10,11... | collective-permute-start | bytes 6291464 | tf_op jit(solution)/shard_map/ppermute | solution.py:78
  221.3 8.7 %collective-permute-start.16 = (f32[2,2,128,512]{3,2,0,1:T(8,128)S(1)}, f32[2,2,128,512]{3,2,0,1:T(8,128)S(1)}, u32[]{:S(2)}, u32[]{:S(2)}) collective-permute-start(f32[2,2,128,512]{3,2,0,1:T(8,128)S(1)} %copy.46), channel_id=1, source_target_pairs={{0,8},{8,0},{16,24},{24,16},{1,9},{9,1},{17,25},{25,17},{2,10},{10... | collective-permute-start | bytes 3145736 | tf_op jit(solution)/shard_map/ppermute | solution.py:78
  229.3 55.6 %collective-permute-start.6 = (f32[2,256,512]{2,1,0:T(8,128)S(1)}, f32[2,256,512]{2,1,0:T(8,128)}, u32[]{:S(2)}, u32[]{:S(2)}) collective-permute-start(f32[2,256,512]{2,1,0:T(8,128)S(1)} %dynamic-slice_bitcast_fusion.2), channel_id=1, source_target_pairs={{0,2},{1,3},{2,0},{3,1},{4,6},{5,7},{6,4},{7,5},{8,10},{9,11},{10,... | collective-permute-start | bytes 3145736 | tf_op jit(solution)/shard_map/ppermute | solution.py:78
  264.5 34.8 %collective-permute-start.10 = (f32[2,256,512]{2,1,0:T(8,128)}, f32[2,256,512]{2,1,0:T(8,128)}, u32[]{:S(2)}, u32[]{:S(2)}) collective-permute-start(f32[2,256,512]{2,1,0:T(8,128)} %dynamic-slice_bitcast_fusion.1), channel_id=1, source_target_pairs={{0,2},{1,3},{2,0},{3,1},{4,6},{5,7},{6,4},{7,5},{8,10},{9,11},{10,... | collective-permute-start | bytes 3145736 | tf_op jit(solution)/shard_map/ppermute | solution.py:78
  266.6 30.4 %collective-permute-start.17 = (f32[2,1,128,512]{3,2,0,1:T(8,128)}, f32[2,1,128,512]{3,2,0,1:T(8,128)}, u32[]{:S(2)}, u32[]{:S(2)}) collective-permute-start(f32[2,1,128,512]{3,2,0,1:T(8,128)} %constant_dynamic-slice_fusion.2), channel_id=1, source_target_pairs={{0,16},{8,24},{16,0},{24,8},{1,17},{9,25},{17,1},{25,9},{2,18},{10... | collective-permute-start | bytes 1572872 | tf_op jit(solution)/shard_map/ppermute | solution.py:78
  286.5 44.3 %copy-start = (f32[3,512,512]{2,1,0:T(8,128)S(1)}, f32[3,512,512]{2,1,0:T(8,128)}, u32[]{:S(2)}) copy-start(f32[3,512,512]{2,1,0:T(8,128)} %param.7) | copy-start | bytes 9437188
  286.5 44.2 %collective-permute-start.7 = (f32[1,256,512]{2,1,0:T(8,128)S(1)}, f32[1,256,512]{2,1,0:T(8,128)S(1)}, u32[]{:S(2)}, u32[]{:S(2)}) collective-permute-start(f32[1,256,512]{2,1,0:T(8,128)S(1)} %constant_dynamic-slice_fusion.5), channel_id=1, source_target_pairs={{0,4},{1,5},{2,6},{3,7},{4,0},{5,1},{6,2},{7,3},{8,12},{9,13},{10,... | collective-permute-start | bytes 1572872 | tf_op jit(solution)/shard_map/ppermute | solution.py:78
  299.0 41.1 %collective-permute-start.18 = (f32[2,128,512]{2,1,0:T(8,128)}, f32[2,128,512]{2,1,0:T(8,128)}, u32[]{:S(2)}, u32[]{:S(2)}) collective-permute-start(f32[2,128,512]{2,1,0:T(8,128)} %add_bitcast_fusion.2), channel_id=1, source_target_pairs={{0,1},{1,0},{2,3},{3,2},{4,5},{5,4},{6,7},{7,6},{8,9},{9,8},{10,11... | collective-permute-start | bytes 1572872 | tf_op jit(solution)/shard_map/ppermute | solution.py:78
  301.6 40.6 %collective-permute-start.11 = (f32[1,256,512]{2,1,0:T(8,128)}, f32[1,256,512]{2,1,0:T(8,128)}, u32[]{:S(2)}, u32[]{:S(2)}) collective-permute-start(f32[1,256,512]{2,1,0:T(8,128)} %constant_dynamic-slice_fusion.4), channel_id=1, source_target_pairs={{0,4},{1,5},{2,6},{3,7},{4,0},{5,1},{6,2},{7,3},{8,12},{9,13},{10,... | collective-permute-start | bytes 1572872 | tf_op jit(solution)/shard_map/ppermute | solution.py:78
  342.2 16.9 %collective-permute-start.19 = (f32[2,128,512]{2,1,0:T(8,128)}, f32[2,128,512]{2,1,0:T(8,128)}, u32[]{:S(2)}, u32[]{:S(2)}) collective-permute-start(f32[2,128,512]{2,1,0:T(8,128)} %add.271), channel_id=1, source_target_pairs={{0,2},{1,3},{2,0},{3,1},{4,6},{5,7},{6,4},{7,5},{8,10},{9,11},{10,... | collective-permute-start | bytes 1572872 | tf_op jit(solution)/shard_map/ppermute | solution.py:78
  354.2 9.4 %collective-permute-start.21 = (f32[2,2,128,512]{3,2,0,1:T(8,128)S(1)}, f32[2,2,128,512]{3,2,0,1:T(8,128)S(1)}, u32[]{:S(2)}, u32[]{:S(2)}) collective-permute-start(f32[2,2,128,512]{3,2,0,1:T(8,128)S(1)} %copy.50), channel_id=1, source_target_pairs={{0,8},{8,0},{16,24},{24,16},{1,9},{9,1},{17,25},{25,17},{2,10},{10... | collective-permute-start | bytes 3145736 | tf_op jit(solution)/shard_map/ppermute | solution.py:78
  359.1 76.3 %collective-permute-start.13 = (f32[1024,512]{1,0:T(8,128)}, f32[1024,512]{1,0:T(8,128)}, u32[]{:S(2)}, u32[]{:S(2)}) collective-permute-start(f32[1024,512]{1,0:T(8,128)} %fusion.6), channel_id=1, source_target_pairs={{0,1},{1,0},{2,3},{3,2},{4,5},{5,4},{6,7},{7,6},{8,9},{9,8},{10,11... | collective-permute-start | bytes 6291464 | tf_op jit(solution)/shard_map/ppermute | solution.py:78
  360.3 26.9 %collective-permute-start.20 = (f32[2,128,512]{2,1,0:T(8,128)S(1)}, f32[2,128,512]{2,1,0:T(8,128)S(1)}, u32[]{:S(2)}, u32[]{:S(2)}) collective-permute-start(f32[2,128,512]{2,1,0:T(8,128)S(1)} %add.272), channel_id=1, source_target_pairs={{0,4},{1,5},{2,6},{3,7},{4,0},{5,1},{6,2},{7,3},{8,12},{9,13},{10,... | collective-permute-start | bytes 1572872 | tf_op jit(solution)/shard_map/ppermute | solution.py:78
  365.6 22.7 %collective-permute-start.22 = (f32[2,1,128,512]{3,2,0,1:T(8,128)}, f32[2,1,128,512]{3,2,0,1:T(8,128)}, u32[]{:S(2)}, u32[]{:S(2)}) collective-permute-start(f32[2,1,128,512]{3,2,0,1:T(8,128)} %constant_dynamic-slice_fusion.1), channel_id=1, source_target_pairs={{0,16},{8,24},{16,0},{24,8},{1,17},{9,25},{17,1},{25,9},{2,18},{10... | collective-permute-start | bytes 1572872 | tf_op jit(solution)/shard_map/ppermute | solution.py:78
  388.2 190.9 %all-gather.18.cloned.1.call-start = ((), (), s32[]{:S(2)}) async-start(), calls=%async_computation.5 | async-start | bytes 2621440 | tf_op jit(solution)/shard_map/all_gather | solution.py:115
  388.3 47.1 %copy-start.46 = (bf16[1024,1024]{1,0:T(8,128)(2,1)S(1)}, bf16[1024,1024]{1,0:T(8,128)(2,1)}, u32[]{:S(2)}) copy-start(bf16[1024,1024]{1,0:T(8,128)(2,1)} %get-tuple-element.15) | copy-start | bytes 6291460
  388.3 47.1 %copy-start.49 = (bf16[1024,1024]{1,0:T(8,128)(2,1)S(1)}, bf16[1024,1024]{1,0:T(8,128)(2,1)}, u32[]{:S(2)}) copy-start(bf16[1024,1024]{1,0:T(8,128)(2,1)} %get-tuple-element.16) | copy-start | bytes 6291460
  388.3 47.1 %copy-start.55 = (bf16[1024,512]{1,0:T(8,128)(2,1)S(1)}, bf16[1024,512]{1,0:T(8,128)(2,1)}, u32[]{:S(2)}) copy-start(bf16[1024,512]{1,0:T(8,128)(2,1)} %get-tuple-element.31) | copy-start | bytes 3145732
  389.7 28.7 %collective-permute-start.23 = (f32[2,128,512]{2,1,0:T(8,128)S(1)}, f32[2,128,512]{2,1,0:T(8,128)S(1)}, u32[]{:S(2)}, u32[]{:S(2)}) collective-permute-start(f32[2,128,512]{2,1,0:T(8,128)S(1)} %add_bitcast_fusion.1), channel_id=1, source_target_pairs={{0,1},{1,0},{2,3},{3,2},{4,5},{5,4},{6,7},{7,6},{8,9},{9,8},{10,11... | collective-permute-start | bytes 1572872 | tf_op jit(solution)/shard_map/ppermute | solution.py:78
  418.6 13.8 %collective-permute-start.24 = (f32[2,128,512]{2,1,0:T(8,128)S(1)}, f32[2,128,512]{2,1,0:T(8,128)S(1)}, u32[]{:S(2)}, u32[]{:S(2)}) collective-permute-start(f32[2,128,512]{2,1,0:T(8,128)S(1)} %add.278), channel_id=1, source_target_pairs={{0,2},{1,3},{2,0},{3,1},{4,6},{5,7},{6,4},{7,5},{8,10},{9,11},{10,... | collective-permute-start | bytes 1572872 | tf_op jit(solution)/shard_map/ppermute | solution.py:78
  421.7 37.1 %collective-permute-start.26 = (f32[2,2,128,512]{3,2,0,1:T(8,128)}, f32[2,2,128,512]{3,2,0,1:T(8,128)}, u32[]{:S(2)}, u32[]{:S(2)}) collective-permute-start(f32[2,2,128,512]{3,2,0,1:T(8,128)} %copy.55), channel_id=1, source_target_pairs={{0,8},{8,0},{16,24},{24,16},{1,9},{9,1},{17,25},{25,17},{2,10},{10... | collective-permute-start | bytes 3145736 | tf_op jit(solution)/shard_map/ppermute | solution.py:78
  432.5 25.2 %collective-permute-start.25 = (f32[2,128,512]{2,1,0:T(8,128)S(1)}, f32[2,128,512]{2,1,0:T(8,128)S(1)}, u32[]{:S(2)}, u32[]{:S(2)}) collective-permute-start(f32[2,128,512]{2,1,0:T(8,128)S(1)} %add.279), channel_id=1, source_target_pairs={{0,4},{1,5},{2,6},{3,7},{4,0},{5,1},{6,2},{7,3},{8,12},{9,13},{10,... | collective-permute-start | bytes 1572872 | tf_op jit(solution)/shard_map/ppermute | solution.py:78
  441.9 34.1 %collective-permute-start.14 = (f32[2,256,512]{2,1,0:T(8,128)}, f32[2,256,512]{2,1,0:T(8,128)}, u32[]{:S(2)}, u32[]{:S(2)}) collective-permute-start(f32[2,256,512]{2,1,0:T(8,128)} %dynamic-slice_bitcast_fusion), channel_id=1, source_target_pairs={{0,2},{1,3},{2,0},{3,1},{4,6},{5,7},{6,4},{7,5},{8,10},{9,11},{10,... | collective-permute-start | bytes 3145736 | tf_op jit(solution)/shard_map/ppermute | solution.py:78
  458.6 127.1 %all-gather.20.cloned.1.call-start = ((), (), s32[]{:S(2)}) async-start(), calls=%async_computation.6 | async-start | bytes 2621440 | tf_op jit(solution)/shard_map/all_gather | solution.py:115
  460.8 23.7 %collective-permute-start.27 = (f32[2,1,128,512]{3,2,0,1:T(8,128)S(1)}, f32[2,1,128,512]{3,2,0,1:T(8,128)S(1)}, u32[]{:S(2)}, u32[]{:S(2)}) collective-permute-start(f32[2,1,128,512]{3,2,0,1:T(8,128)S(1)} %constant_dynamic-slice_fusion), channel_id=1, source_target_pairs={{0,16},{8,24},{16,0},{24,8},{1,17},{9,25},{17,1},{25,9},{2,18},{10... | collective-permute-start | bytes 1572872 | tf_op jit(solution)/shard_map/ppermute | solution.py:78
  485.3 9.5 %collective-permute-start.28 = (f32[2,128,512]{2,1,0:T(8,128)}, f32[2,128,512]{2,1,0:T(8,128)}, u32[]{:S(2)}, u32[]{:S(2)}) collective-permute-start(f32[2,128,512]{2,1,0:T(8,128)} %add_bitcast_fusion), channel_id=1, source_target_pairs={{0,1},{1,0},{2,3},{3,2},{4,5},{5,4},{6,7},{7,6},{8,9},{9,8},{10,11... | collective-permute-start | bytes 1572872 | tf_op jit(solution)/shard_map/ppermute | solution.py:78
  486.1 20.9 %collective-permute-start.15 = (f32[1,256,512]{2,1,0:T(8,128)}, f32[1,256,512]{2,1,0:T(8,128)}, u32[]{:S(2)}, u32[]{:S(2)}) collective-permute-start(f32[1,256,512]{2,1,0:T(8,128)} %constant_dynamic-slice_fusion.3), channel_id=1, source_target_pairs={{0,4},{1,5},{2,6},{3,7},{4,0},{5,1},{6,2},{7,3},{8,12},{9,13},{10,... | collective-permute-start | bytes 1572872 | tf_op jit(solution)/shard_map/ppermute | solution.py:78
  496.1 18.0 %collective-permute-start.29 = (f32[2,128,512]{2,1,0:T(8,128)S(1)}, f32[2,128,512]{2,1,0:T(8,128)S(1)}, u32[]{:S(2)}, u32[]{:S(2)}) collective-permute-start(f32[2,128,512]{2,1,0:T(8,128)S(1)} %add.284), channel_id=1, source_target_pairs={{0,2},{1,3},{2,0},{3,1},{4,6},{5,7},{6,4},{7,5},{8,10},{9,11},{10,... | collective-permute-start | bytes 1572872 | tf_op jit(solution)/shard_map/ppermute | solution.py:78
  514.9 26.9 %collective-permute-start.30 = (f32[2,128,512]{2,1,0:T(8,128)}, f32[2,128,512]{2,1,0:T(8,128)}, u32[]{:S(2)}, u32[]{:S(2)}) collective-permute-start(f32[2,128,512]{2,1,0:T(8,128)} %add.285), channel_id=1, source_target_pairs={{0,4},{1,5},{2,6},{3,7},{4,0},{5,1},{6,2},{7,3},{8,12},{9,13},{10,... | collective-permute-start | bytes 1572872 | tf_op jit(solution)/shard_map/ppermute | solution.py:78
  519.0 24.9 %collective-permute-start.31 = (f32[1,2,128,512]{3,2,1,0:T(8,128)}, f32[1,2,128,512]{3,2,1,0:T(8,128)}, u32[]{:S(2)}, u32[]{:S(2)}) collective-permute-start(f32[1,2,128,512]{3,2,1,0:T(8,128)} %dynamic-slice_bitcast_fusion.4), channel_id=1, source_target_pairs={{0,8},{8,0},{16,24},{24,16},{1,9},{9,1},{17,25},{25,17},{2,10},{10... | collective-permute-start | bytes 1572872 | tf_op jit(solution)/shard_map/ppermute | solution.py:78
  545.5 8.6 %collective-permute-start.32 = (f32[1,1,128,512]{3,2,1,0:T(8,128)S(1)}, f32[1,1,128,512]{3,2,1,0:T(8,128)S(1)}, u32[]{:S(2)}, u32[]{:S(2)}) collective-permute-start(f32[1,1,128,512]{3,2,1,0:T(8,128)S(1)} %constant_dynamic-slice_fusion.9), channel_id=1, source_target_pairs={{0,16},{8,24},{16,0},{24,8},{1,17},{9,25},{17,1},{25,9},{2,18},{10... | collective-permute-start | bytes 786440 | tf_op jit(solution)/shard_map/ppermute | solution.py:78
  554.1 7.2 %collective-permute-start.33 = (f32[1,128,512]{2,1,0:T(8,128)S(1)}, f32[1,128,512]{2,1,0:T(8,128)S(1)}, u32[]{:S(2)}, u32[]{:S(2)}) collective-permute-start(f32[1,128,512]{2,1,0:T(8,128)S(1)} %add_bitcast_fusion.3), channel_id=1, source_target_pairs={{0,1},{1,0},{2,3},{3,2},{4,5},{5,4},{6,7},{7,6},{8,9},{9,8},{10,11... | collective-permute-start | bytes 786440 | tf_op jit(solution)/shard_map/ppermute | solution.py:78
  561.4 7.1 %collective-permute-start.34 = (f32[1,128,512]{2,1,0:T(8,128)S(1)}, f32[1,128,512]{2,1,0:T(8,128)S(1)}, u32[]{:S(2)}, u32[]{:S(2)}) collective-permute-start(f32[1,128,512]{2,1,0:T(8,128)S(1)} %add.290), channel_id=1, source_target_pairs={{0,2},{1,3},{2,0},{3,1},{4,6},{5,7},{6,4},{7,5},{8,10},{9,11},{10,... | collective-permute-start | bytes 786440 | tf_op jit(solution)/shard_map/ppermute | solution.py:78
  569.2 22.1 %collective-permute-start.35 = (f32[1,128,512]{2,1,0:T(8,128)}, f32[1,128,512]{2,1,0:T(8,128)}, u32[]{:S(2)}, u32[]{:S(2)}) collective-permute-start(f32[1,128,512]{2,1,0:T(8,128)} %add.291), channel_id=1, source_target_pairs={{0,4},{1,5},{2,6},{3,7},{4,0},{5,1},{6,2},{7,3},{8,12},{9,13},{10,... | collective-permute-start | bytes 786440 | tf_op jit(solution)/shard_map/ppermute | solution.py:78
  (67 other events, 792.8 us)
Sparse Core Ops, SparseCore 0:
  11.4 73.3 all-gather.7
  86.3 34.7 all-gather.9
  123.2 24.3 all-gather.11
  149.0 47.2 all-gather.13
  388.3 25.3 all-gather.15
  458.7 31.1 all-gather.17
  544.1 25.0 all-gather.19

commit v3 on v2

--- a/solution.py
+++ b/solution.py
@@ -90,9 +90,9 @@
         return parts
 
     columns = []
-    diag_sums = []
-    cross_sums = []
     nearer = []
+    parts = []
+    early = STEPS - 3
     for k in range(STEPS):
         gone = jnp.dot(left[0], right[k], preferred_element_type=jnp.float32)
         gone = exchange(after(gone, nearer[k - 2] if k > 1 else None), "col", 0)
@@ -107,14 +107,20 @@
         if k > 0:
             total = total + dot(columns[-1], parent_panel[k - 1])
         columns.append(-own_masks[k] * total)
-        parts = [dot_t(masked[k], columns[k])]
+        parts.append(dot_t(masked[k], columns[k]))
         if k + 1 < STEPS:
             parts.append(dot_t(columns[k], masked[k + 1]))
-        slab = reduce_slab(jnp.stack(parts))
-        if k + 1 < STEPS:
-            sums = lax.all_gather(slab, "row", axis=1, tiled=True)
-            diag_sums.append(sums[0])
-            cross_sums.append(sums[1])
+        if k == early:
+            nearer[k] = parts = jnp.stack(parts)
+            sums = lax.psum(parts, ("row", "col"))
+            parts = []
+        elif k > early:
+            slab = reduce_slab(jnp.stack(parts))
+            parts = []
+            if k + 1 < STEPS:
+                sums = jnp.concatenate([sums, lax.all_gather(slab, "row", axis=1, tiled=True)])
+    diag_sums = sums[0::2]
+    cross_sums = sums[1::2]
 
     def own_slab(value):
         return lax.dynamic_slice_in_dim(value, row_index * out_rows, out_rows, 0)

time: 607 us -> 587 us (0.967)
  other arithmetic: 54.1 us -> 30.7 us
  waiting for transfers between devices: 325 us -> 338 us
  matrix products: 76.8 us -> 67.4 us
  starting transfers between devices: 87.4 us -> 95.8 us
  local copies, waits for them, and re-layouts: 41.6 us -> 34.6 us
    ppermute x32 -> x22, waiting for transfers between devices: 252 us -> 205 us  [exchange(): lax.ppermute(value, axis, [(i, i ^ 1 << stage) for i in range(count)])]
    psum x0 -> x1, waiting for transfers between devices: none -> 30.6 us  [shards(): sums = lax.psum(parts, ('row', 'col'))]
    all_gather x4, waiting for transfers between devices: 73.6 us -> 88.3 us  [shards(): whole = lax.all_gather(part, 'row', axis=0, tiled=True)]
    all_gather x3 -> x1, waiting for transfers between devices: 0.01 us -> 14 us  [shards(): lax.all_gather(slab, 'row', axis=1, tiled=True)]
    dot_general x14, matrix products: 27.9 us -> 15.3 us  [dot_t(): lax.dot_general(a, b, (((0,), (0,)), ((), ())), precision=HIGH, preferred...]
    ppermute x32 -> x22, starting transfers between devices: 83.2 us -> 91.3 us  [exchange(): lax.ppermute(value, axis, [(i, i ^ 1 << stage) for i in range(count)])]
    another operation x7 -> x3, local copies, waits for them, and re-layouts: 12.3 us -> 5.06 us
    add x11 -> x5, other arithmetic: 10.3 us -> 3.79 us  [reduce_slab(): parts = parts + exchange(parts, 'col', stage)]
  transfers between devices with their start and end apart: 43 -> 32, of which waited for: 20 -> 20; matrix products, arithmetic and copies ran while one was open for 26% -> 21% of each run, Pallas kernels for 0% -> 0%
where the time goes in v3:
time: 587 us; the launch traced here: 582 us
  waiting for transfers between devices  338 us (58%)
  starting transfers between devices  95.8 us (16%)
  matrix products  67.4 us (11%)
  local copies, waits for them, and re-layouts  34.6 us (6%)
  other arithmetic  30.7 us (5%)
  between operations  15.2 us (3%)
    ppermute x22, waiting for transfers between devices, exchange(): lax.ppermute(value, axis, [(i, i ^ 1 << stage) for i in range(count)])  205 us
    ppermute x22, starting transfers between devices, exchange(): lax.ppermute(value, axis, [(i, i ^ 1 << stage) for i in range(count)])  91.3 us
    all_gather x4, waiting for transfers between devices, shards(): whole = lax.all_gather(part, 'row', axis=0, tiled=True)  88.3 us
    psum x1, waiting for transfers between devices, shards(): sums = lax.psum(parts, ('row', 'col'))  30.6 us
    dot_general x4, matrix products, shards(): jnp.dot(left[1], right[k], preferred_element_type=jnp.float32) + gone  24.5 us
    dot_general x4, matrix products, shards(): gone = jnp.dot(left[0], right[k], preferred_element_type=jnp.float32)  19.1 us
    dot_general x14, matrix products, dot_t(): lax.dot_general(a, b, (((0,), (0,)), ((), ())), precision=HIGH, preferred...  15.3 us
    all_gather x1, waiting for transfers between devices, shards(): lax.all_gather(slab, 'row', axis=1, tiled=True)  14 us
  transfers between devices with their start and end apart: 32, of which 20 were waited for; matrix products, arithmetic and copies ran while one was open for 21% of the time, Pallas kernels for 0%

profile of v3, /device:TPU:0, one launch (start us, length us, event | category | flops | bytes accessed | tf_op | source)
XLA Modules:
  0.0 581.8 jit_solution(14444755927009025371)
XLA Ops:
  14.5 6.7 %constant_dynamic-slice_fusion.6 = (f32[4,1,256,1024]{3,2,1,0:T(8,128)}, f32[4,1,256,1024]{3,2,1,0:T(8,128)S(1)}) fusion(f32[4,2,256,1024]{3,2,1,0:T(8,128)} %bitcast.232, s32[]{:T(128)S(6)} %select_n.155, s32[]{:T(128)S(6)} %select_n.156), kind=kLoop, calls=%fused_computation.162 | loop fusion | bytes 16777224 | tf_op jit(solution)/shard_map/jit(dynamic_index_in_dim)/dynamic_slice | solution.py:40
  21.3 2.2 fusion.1
  25.1 59.7 %all-gather.6.cloned.1.call-done = f32[1024,512]{1,0:T(8,128)} async-done(((f32[256,512]{1,0:T(8,128)}), f32[1024,512]{1,0:T(8,128)}) %all-gather.6.cloned.1.call-update) | async-done | bytes 2097168 | tf_op jit(solution)/shard_map/all_gather | solution.py:65
  84.8 2.1 reduce-precision_convert_fusion.5
  87.0 4.7 fusion.12
  91.7 13.8 %collective-permute-start.1 = (f32[1024,512]{1,0:T(8,128)}, f32[1024,512]{1,0:T(8,128)}, u32[]{:S(2)}, u32[]{:S(2)}) collective-permute-start(f32[1024,512]{1,0:T(8,128)} %fusion.12), channel_id=1, source_target_pairs={{0,1},{1,0},{2,3},{3,2},{4,5},{5,4},{6,7},{7,6},{8,9},{9,8},{10,11... | collective-permute-start | bytes 6291464 | tf_op jit(solution)/shard_map/ppermute | solution.py:78
  105.6 2.9 fusion
  109.7 8.3 %all-gather.8.cloned.1.call-done = f32[1024,512]{1,0:T(8,128)} async-done(((f32[256,512]{1,0:T(8,128)}), f32[1024,512]{1,0:T(8,128)}) %all-gather.8.cloned.1.call-update) | async-done | bytes 2097168 | tf_op jit(solution)/shard_map/all_gather | solution.py:65
  118.0 2.1 reduce-precision_convert_fusion.4
  120.2 4.8 fusion.10
  126.2 20.2 %all-gather.10.cloned.1.call-done = f32[1024,512]{1,0:T(8,128)} async-done(((f32[256,512]{1,0:T(8,128)}), f32[1024,512]{1,0:T(8,128)}) %all-gather.10.cloned.1.call-update) | async-done | bytes 2097168 | tf_op jit(solution)/shard_map/all_gather | solution.py:65
  148.3 4.2 collective-permute-done.1
  152.5 7.3 %fusion.14 = f32[1024,512]{1,0:T(8,128)S(1)} fusion(f32[1024,512]{1,0:T(8,128)} %collective-permute-done.1, bf16[1024,512]{1,0:T(8,128)(2,1)} %copy-done.36, bf16[1024,512]{1,0:T(8,128)(2,1)S(1)} %copy-done.35, bf16[1024,1024]{1,0:T(8,128)(2,1)} %get-tuple-element.18, bf16[1024,1024]{1,0:T(8,128)(2,1)} %get-tuple-element.17), kind=kOutput, calls=%fused_computation.38 | convolution fusion | flops 3250061312 | bytes 10485760 | tf_op jit(solution)/shard_map/dot_general | solution.py:99
  160.1 4.8 fusion.8
  164.9 9.9 %collective-permute-done.2 = f32[2,256,512]{2,1,0:T(8,128)S(1)} collective-permute-done((f32[2,256,512]{2,1,0:T(8,128)S(1)}, f32[2,256,512]{2,1,0:T(8,128)S(1)}, u32[]{:S(2)}, u32[]{:S(2)}) %collective-permute-start.2) | collective-permute-done | bytes 1048608 | tf_op jit(solution)/shard_map/ppermute | solution.py:78
  174.8 2.6 collective-permute-start.9
  177.4 2.1 reduce-precision_convert_fusion.2
  179.5 18.0 %collective-permute-done.5 = f32[1024,512]{1,0:T(8,128)} collective-permute-done((f32[1024,512]{1,0:T(8,128)}, f32[1024,512]{1,0:T(8,128)}, u32[]{:S(2)}, u32[]{:S(2)}) %collective-permute-start.5) | collective-permute-done | bytes 2097184 | tf_op jit(solution)/shard_map/ppermute | solution.py:78
  197.5 6.0 %fusion.15 = f32[1024,512]{1,0:T(8,128)S(1)} fusion(f32[1024,512]{1,0:T(8,128)} %collective-permute-done.5, bf16[1024,512]{1,0:T(8,128)(2,1)} %copy-done.42, bf16[1024,512]{1,0:T(8,128)(2,1)} %copy-done.41, bf16[1024,1024]{1,0:T(8,128)(2,1)S(1)} %copy-done.21, bf16[1024,1024]{1,0:T(8,128)(2,1)S(1)} %copy-done.19), kind=kOutput, calls=%fused_computation.39 | convolution fusion | flops 3250061312 | bytes 10485760 | tf_op jit(solution)/shard_map/dot_general | solution.py:99
  204.0 9.4 %collective-permute-start.3 = (f32[1,256,512]{2,1,0:T(8,128)S(1)}, f32[1,256,512]{2,1,0:T(8,128)S(1)}, u32[]{:S(2)}, u32[]{:S(2)}) collective-permute-start(f32[1,256,512]{2,1,0:T(8,128)S(1)} %constant_dynamic-slice_fusion.4), channel_id=1, source_target_pairs={{0,4},{1,5},{2,6},{3,7},{4,0},{5,1},{6,2},{7,3},{8,12},{9,13},{10,... | collective-permute-start | bytes 1572872 | tf_op jit(solution)/shard_map/ppermute | solution.py:78
  213.4 29.0 %collective-permute-done.9 = f32[1024,512]{1,0:T(8,128)} collective-permute-done((f32[1024,512]{1,0:T(8,128)}, f32[1024,512]{1,0:T(8,128)}, u32[]{:S(2)}, u32[]{:S(2)}) %collective-permute-start.9) | collective-permute-done | bytes 2097184 | tf_op jit(solution)/shard_map/ppermute | solution.py:78
  242.4 5.3 fusion.16
  247.9 4.7 fusion.6
  252.9 9.4 %collective-permute-start.7 = (f32[1,256,512]{2,1,0:T(8,128)S(1)}, f32[1,256,512]{2,1,0:T(8,128)S(1)}, u32[]{:S(2)}, u32[]{:S(2)}) collective-permute-start(f32[1,256,512]{2,1,0:T(8,128)S(1)} %constant_dynamic-slice_fusion.3), channel_id=1, source_target_pairs={{0,4},{1,5},{2,6},{3,7},{4,0},{5,1},{6,2},{7,3},{8,12},{9,13},{10,... | collective-permute-start | bytes 1572872 | tf_op jit(solution)/shard_map/ppermute | solution.py:78
  263.8 6.8 %collective-permute-done.10 = f32[2,256,512]{2,1,0:T(8,128)S(1)} collective-permute-done((f32[2,256,512]{2,1,0:T(8,128)S(1)}, f32[2,256,512]{2,1,0:T(8,128)S(1)}, u32[]{:S(2)}, u32[]{:S(2)}) %collective-permute-start.10) | collective-permute-done | bytes 1048608 | tf_op jit(solution)/shard_map/ppermute | solution.py:78
  271.7 11.3 %collective-permute-start.11 = (f32[1,256,512]{2,1,0:T(8,128)}, f32[1,256,512]{2,1,0:T(8,128)}, u32[]{:S(2)}, u32[]{:S(2)}) collective-permute-start(f32[1,256,512]{2,1,0:T(8,128)} %constant_dynamic-slice_fusion.2), channel_id=1, source_target_pairs={{0,4},{1,5},{2,6},{3,7},{4,0},{5,1},{6,2},{7,3},{8,12},{9,13},{10,... | collective-permute-start | bytes 1572872 | tf_op jit(solution)/shard_map/ppermute | solution.py:78
  285.1 2.5 pad_maximum_fusion.2
  287.6 3.0 collective-permute-start.13
  290.6 20.7 %collective-permute-done.11 = f32[1,256,512]{2,1,0:T(8,128)} collective-permute-done((f32[1,256,512]{2,1,0:T(8,128)}, f32[1,256,512]{2,1,0:T(8,128)}, u32[]{:S(2)}, u32[]{:S(2)}) %collective-permute-start.11) | collective-permute-done | bytes 524320 | tf_op jit(solution)/shard_map/ppermute | solution.py:78
  311.3 2.8 fusion.57
  324.1 2.1 collective-permute-done.16
  328.0 29.6 %collective-permute-start.17 = (f32[2,1,128,512]{3,2,0,1:T(8,128)S(1)}, f32[2,1,128,512]{3,2,0,1:T(8,128)S(1)}, u32[]{:S(2)}, u32[]{:S(2)}) collective-permute-start(f32[2,1,128,512]{3,2,0,1:T(8,128)S(1)} %constant_dynamic-slice_fusion), channel_id=1, source_target_pairs={{0,16},{8,24},{16,0},{24,8},{1,17},{9,25},{17,1},{25,9},{2,18},{10... | collective-permute-start | bytes 1572872 | tf_op jit(solution)/shard_map/ppermute | solution.py:78
  357.7 6.0 %fusion.17 = f32[1024,512]{1,0:T(8,128)S(1)} fusion(f32[1024,512]{1,0:T(8,128)} %collective-permute-done.13, bf16[1024,512]{1,0:T(8,128)(2,1)} %copy-done.33, bf16[1024,512]{1,0:T(8,128)(2,1)} %copy-done.32, bf16[1024,1024]{1,0:T(8,128)(2,1)S(1)} %copy-done.22, bf16[1024,1024]{1,0:T(8,128)(2,1)S(1)} %copy-done.20), kind=kOutput, calls=%fused_computation.41 | convolution fusion | flops 3250061312 | bytes 10485760 | tf_op jit(solution)/shard_map/dot_general | solution.py:99
  363.7 14.0 %collective-permute-done.17 = f32[2,1,128,512]{3,2,0,1:T(8,128)S(1)} collective-permute-done((f32[2,1,128,512]{3,2,0,1:T(8,128)S(1)}, f32[2,1,128,512]{3,2,0,1:T(8,128)S(1)}, u32[]{:S(2)}, u32[]{:S(2)}) %collective-permute-start.17) | collective-permute-done | bytes 524320 | tf_op jit(solution)/shard_map/ppermute | solution.py:78
  379.4 12.2 %collective-permute-done.18 = f32[2,128,512]{2,1,0:T(8,128)S(1)} collective-permute-done((f32[2,128,512]{2,1,0:T(8,128)S(1)}, f32[2,128,512]{2,1,0:T(8,128)S(1)}, u32[]{:S(2)}, u32[]{:S(2)}) %collective-permute-start.18) | collective-permute-done | bytes 524320 | tf_op jit(solution)/shard_map/ppermute | solution.py:78
  391.8 32.4 %collective-permute-done.19 = f32[2,128,512]{2,1,0:T(8,128)S(1)} collective-permute-done((f32[2,128,512]{2,1,0:T(8,128)S(1)}, f32[2,128,512]{2,1,0:T(8,128)S(1)}, u32[]{:S(2)}, u32[]{:S(2)}) %collective-permute-start.19) | collective-permute-done | bytes 524320 | tf_op jit(solution)/shard_map/ppermute | solution.py:78
  429.3 34.8 %collective-permute-done.20 = f32[2,128,512]{2,1,0:T(8,128)S(1)} collective-permute-done((f32[2,128,512]{2,1,0:T(8,128)S(1)}, f32[2,128,512]{2,1,0:T(8,128)S(1)}, u32[]{:S(2)}, u32[]{:S(2)}) %collective-permute-start.20) | collective-permute-done | bytes 524320 | tf_op jit(solution)/shard_map/ppermute | solution.py:78
  464.9 2.0 copy.37
  467.0 7.7 %collective-permute-done.15 = f32[1,256,512]{2,1,0:T(8,128)} collective-permute-done((f32[1,256,512]{2,1,0:T(8,128)}, f32[1,256,512]{2,1,0:T(8,128)}, u32[]{:S(2)}, u32[]{:S(2)}) %collective-permute-start.15) | collective-permute-done | bytes 524320 | tf_op jit(solution)/shard_map/ppermute | solution.py:78
  482.0 9.4 %collective-permute-done.22 = f32[1,1,128,512]{3,2,1,0:T(8,128)S(1)} collective-permute-done((f32[1,1,128,512]{3,2,1,0:T(8,128)S(1)}, f32[1,1,128,512]{3,2,1,0:T(8,128)S(1)}, u32[]{:S(2)}, u32[]{:S(2)}) %collective-permute-start.22) | collective-permute-done | bytes 262176 | tf_op jit(solution)/shard_map/ppermute | solution.py:78
  492.8 2.3 slice.85
  495.1 2.5 fusion.25
  497.6 2.1 collective-permute-done.23
  500.8 30.6 %all-reduce.2.cloned.1.call-done = f32[4,512,512]{2,1,0:T(8,128)} async-done(((f32[4,512,512]{2,1,0:T(8,128)}), f32[4,512,512]{2,1,0:T(8,128)}) %all-reduce.2.cloned.1.call-update) | async-done | bytes 4194320 | tf_op jit(solution)/shard_map/psum | solution.py:115
  531.3 4.8 constant_dynamic-update-slice_fusion.1
  540.7 14.0 %all-gather.14.cloned.1.call-done = f32[2,512,512]{2,1,0:T(8,128)} async-done(((f32[2,128,512]{2,1,0:T(8,128)}), f32[2,512,512]{2,1,0:T(8,128)}) %all-gather.14.cloned.1.call-update) | async-done | bytes 2097168 | tf_op jit(solution)/shard_map/all_gather | solution.py:121
  554.7 3.1 constant_dynamic-update-slice_fusion
  557.9 3.7 fusion.94
  (198 shorter events, 66.1 us)
Async XLA Ops:
  7.2 77.6 %all-gather.6.cloned.1.call-start = ((), (), s32[]{:S(2)}) async-start(), calls=%async_computation | async-start | bytes 2621440 | tf_op jit(solution)/shard_map/all_gather | solution.py:65
  9.7 98.7 %copy-start.8 = (f32[256,512]{1,0:T(8,128)}, f32[256,512]{1,0:T(8,128)S(1)}, u32[]{:S(2)}) copy-start(f32[256,512]{1,0:T(8,128)S(1)} %get-tuple-element.9) | copy-start | bytes 1572868
  9.8 0.7 collective-permute-start
  11.3 106.7 %all-gather.8.cloned.1.call-start = ((), (), s32[]{:S(2)}) async-start(), calls=%async_computation.1 | async-start | bytes 2621440 | tf_op jit(solution)/shard_map/all_gather | solution.py:65
  11.3 0.7 collective-permute-start.4
  12.9 133.5 %all-gather.10.cloned.1.call-start = ((), (), s32[]{:S(2)}) async-start(), calls=%async_computation.2 | async-start | bytes 2621440 | tf_op jit(solution)/shard_map/all_gather | solution.py:65
  12.9 0.7 collective-permute-start.8
  14.5 162.9 %all-gather.12.cloned.1.call-start = ((), (), s32[]{:S(2)}) async-start(), calls=%async_computation.3 | async-start | bytes 2621440 | tf_op jit(solution)/shard_map/all_gather | solution.py:65
  23.5 96.6 %copy-start.23 = (bf16[1024,1024]{1,0:T(8,128)(2,1)}, bf16[1024,1024]{1,0:T(8,128)(2,1)S(1)}, u32[]{:S(2)}) copy-start(bf16[1024,1024]{1,0:T(8,128)(2,1)S(1)} %get-tuple-element.19) | copy-start | bytes 6291460
  23.5 85.9 %collective-permute-start.12 = (f32[256,512]{1,0:T(8,128)S(1)}, f32[256,512]{1,0:T(8,128)}, u32[]{:S(2)}, u32[]{:S(2)}) collective-permute-start(f32[256,512]{1,0:T(8,128)S(1)} %get-tuple-element.11), channel_id=1, source_target_pairs={{0,0},{1,8},{2,16},{3,24},{4,1},{5,9},{6,17},{7,25},{8,2},{9,10},{... | collective-permute-start | bytes 1572872 | tf_op jit(solution)/shard_map/ppermute | solution.py:64
  91.7 60.8 %collective-permute-start.1 = (f32[1024,512]{1,0:T(8,128)}, f32[1024,512]{1,0:T(8,128)}, u32[]{:S(2)}, u32[]{:S(2)}) collective-permute-start(f32[1024,512]{1,0:T(8,128)} %fusion.12), channel_id=1, source_target_pairs={{0,1},{1,0},{2,3},{3,2},{4,5},{5,4},{6,7},{7,6},{8,9},{9,8},{10,11... | collective-permute-start | bytes 6291464 | tf_op jit(solution)/shard_map/ppermute | solution.py:78
  109.5 421.9 %all-reduce.2.cloned.1.call-start = ((), (), s32[]{:S(2)}) async-start(), calls=%async_computation.4 | async-start | bytes 8388608 | tf_op jit(solution)/shard_map/psum | solution.py:115
  125.0 27.5 %copy-start.35 = (bf16[1024,512]{1,0:T(8,128)(2,1)S(1)}, bf16[1024,512]{1,0:T(8,128)(2,1)}, u32[]{:S(2)}) copy-start(bf16[1024,512]{1,0:T(8,128)(2,1)} %copy-done.34) | copy-start | bytes 3145732
  125.0 72.5 %collective-permute-start.5 = (f32[1024,512]{1,0:T(8,128)}, f32[1024,512]{1,0:T(8,128)}, u32[]{:S(2)}, u32[]{:S(2)}) collective-permute-start(f32[1024,512]{1,0:T(8,128)} %fusion.10), channel_id=1, source_target_pairs={{0,1},{1,0},{2,3},{3,2},{4,5},{5,4},{6,7},{7,6},{8,9},{9,8},{10,11... | collective-permute-start | bytes 6291464 | tf_op jit(solution)/shard_map/ppermute | solution.py:78
  159.9 14.9 %collective-permute-start.2 = (f32[2,256,512]{2,1,0:T(8,128)S(1)}, f32[2,256,512]{2,1,0:T(8,128)S(1)}, u32[]{:S(2)}, u32[]{:S(2)}) collective-permute-start(f32[2,256,512]{2,1,0:T(8,128)S(1)} %dynamic-slice_bitcast_fusion.3), channel_id=1, source_target_pairs={{0,2},{1,3},{2,0},{3,1},{4,6},{5,7},{6,4},{7,5},{8,10},{9,11},{10,... | collective-permute-start | bytes 3145736 | tf_op jit(solution)/shard_map/ppermute | solution.py:78
  174.8 67.6 %collective-permute-start.9 = (f32[1024,512]{1,0:T(8,128)}, f32[1024,512]{1,0:T(8,128)}, u32[]{:S(2)}, u32[]{:S(2)}) collective-permute-start(f32[1024,512]{1,0:T(8,128)} %fusion.8), channel_id=1, source_target_pairs={{0,1},{1,0},{2,3},{3,2},{4,5},{5,4},{6,7},{7,6},{8,9},{9,8},{10,11... | collective-permute-start | bytes 6291464 | tf_op jit(solution)/shard_map/ppermute | solution.py:78
  177.4 20.1 %copy-start.19 = (bf16[1024,1024]{1,0:T(8,128)(2,1)S(1)}, bf16[1024,1024]{1,0:T(8,128)(2,1)}, u32[]{:S(2)}) copy-start(bf16[1024,1024]{1,0:T(8,128)(2,1)} %get-tuple-element.17) | copy-start | bytes 6291460
  177.4 20.1 %copy-start.21 = (bf16[1024,1024]{1,0:T(8,128)(2,1)S(1)}, bf16[1024,1024]{1,0:T(8,128)(2,1)}, u32[]{:S(2)}) copy-start(bf16[1024,1024]{1,0:T(8,128)(2,1)} %get-tuple-element.18) | copy-start | bytes 6291460
  179.5 68.4 %copy-start.32 = (bf16[1024,512]{1,0:T(8,128)(2,1)}, bf16[1024,512]{1,0:T(8,128)(2,1)S(1)}, u32[]{:S(2)}) copy-start(bf16[1024,512]{1,0:T(8,128)(2,1)S(1)} %get-tuple-element.29) | copy-start | bytes 3145732
  179.5 68.4 %copy-start.33 = (bf16[1024,512]{1,0:T(8,128)(2,1)}, bf16[1024,512]{1,0:T(8,128)(2,1)S(1)}, u32[]{:S(2)}) copy-start(bf16[1024,512]{1,0:T(8,128)(2,1)S(1)} %get-tuple-element.30) | copy-start | bytes 3145732
  203.5 38.9 %copy-start.38 = (bf16[1024,512]{1,0:T(8,128)(2,1)S(1)}, bf16[1024,512]{1,0:T(8,128)(2,1)}, u32[]{:S(2)}) copy-start(bf16[1024,512]{1,0:T(8,128)(2,1)} %copy-done.37) | copy-start | bytes 3145732
  203.5 38.9 %copy-start.40 = (bf16[1024,512]{1,0:T(8,128)(2,1)S(1)}, bf16[1024,512]{1,0:T(8,128)(2,1)}, u32[]{:S(2)}) copy-start(bf16[1024,512]{1,0:T(8,128)(2,1)} %copy-done.39) | copy-start | bytes 3145732
  203.6 49.1 %collective-permute-start.6 = (f32[2,256,512]{2,1,0:T(8,128)S(1)}, f32[2,256,512]{2,1,0:T(8,128)S(1)}, u32[]{:S(2)}, u32[]{:S(2)}) collective-permute-start(f32[2,256,512]{2,1,0:T(8,128)S(1)} %dynamic-slice_bitcast_fusion.2), channel_id=1, source_target_pairs={{0,2},{1,3},{2,0},{3,1},{4,6},{5,7},{6,4},{7,5},{8,10},{9,11},{10,... | collective-permute-start | bytes 3145736 | tf_op jit(solution)/shard_map/ppermute | solution.py:78
  203.9 43.9 %copy-start.25 = (bf16[1024,1024]{1,0:T(8,128)(2,1)S(1)}, bf16[1024,1024]{1,0:T(8,128)(2,1)}, u32[]{:S(2)}) copy-start(bf16[1024,1024]{1,0:T(8,128)(2,1)} %copy-done.23) | copy-start | bytes 6291460
  203.9 43.9 %copy-start.29 = (bf16[1024,1024]{1,0:T(8,128)(2,1)S(1)}, bf16[1024,1024]{1,0:T(8,128)(2,1)}, u32[]{:S(2)}) copy-start(bf16[1024,1024]{1,0:T(8,128)(2,1)} %get-tuple-element.20) | copy-start | bytes 6291460
  204.0 58.3 %collective-permute-start.3 = (f32[1,256,512]{2,1,0:T(8,128)S(1)}, f32[1,256,512]{2,1,0:T(8,128)S(1)}, u32[]{:S(2)}, u32[]{:S(2)}) collective-permute-start(f32[1,256,512]{2,1,0:T(8,128)S(1)} %constant_dynamic-slice_fusion.4), channel_id=1, source_target_pairs={{0,4},{1,5},{2,6},{3,7},{4,0},{5,1},{6,2},{7,3},{8,12},{9,13},{10,... | collective-permute-start | bytes 1572872 | tf_op jit(solution)/shard_map/ppermute | solution.py:78
  247.8 22.9 %collective-permute-start.10 = (f32[2,256,512]{2,1,0:T(8,128)S(1)}, f32[2,256,512]{2,1,0:T(8,128)S(1)}, u32[]{:S(2)}, u32[]{:S(2)}) collective-permute-start(f32[2,256,512]{2,1,0:T(8,128)S(1)} %dynamic-slice_bitcast_fusion.1), channel_id=1, source_target_pairs={{0,2},{1,3},{2,0},{3,1},{4,6},{5,7},{6,4},{7,5},{8,10},{9,11},{10,... | collective-permute-start | bytes 3145736 | tf_op jit(solution)/shard_map/ppermute | solution.py:78
  252.9 30.1 %collective-permute-start.7 = (f32[1,256,512]{2,1,0:T(8,128)S(1)}, f32[1,256,512]{2,1,0:T(8,128)S(1)}, u32[]{:S(2)}, u32[]{:S(2)}) collective-permute-start(f32[1,256,512]{2,1,0:T(8,128)S(1)} %constant_dynamic-slice_fusion.3), channel_id=1, source_target_pairs={{0,4},{1,5},{2,6},{3,7},{4,0},{5,1},{6,2},{7,3},{8,12},{9,13},{10,... | collective-permute-start | bytes 1572872 | tf_op jit(solution)/shard_map/ppermute | solution.py:78
  262.4 20.6 %copy-start.2 = (f32[1,256,512]{2,1,0:T(8,128)}, f32[1,256,512]{2,1,0:T(8,128)S(1)}, u32[]{:S(2)}) copy-start(f32[1,256,512]{2,1,0:T(8,128)S(1)} %add_multiply_fusion) | copy-start | bytes 1572868
  263.1 19.9 %copy-start = (f32[3,512,512]{2,1,0:T(8,128)S(1)}, f32[3,512,512]{2,1,0:T(8,128)}, u32[]{:S(2)}) copy-start(f32[3,512,512]{2,1,0:T(8,128)} %param.7) | copy-start | bytes 9437188
  263.8 19.8 %copy-start.9 = (f32[256,512]{1,0:T(8,128)S(1)}, f32[256,512]{1,0:T(8,128)}, u32[]{:S(2)}) copy-start(f32[256,512]{1,0:T(8,128)} %copy-done.8) | copy-start | bytes 1572868
  271.7 39.6 %collective-permute-start.11 = (f32[1,256,512]{2,1,0:T(8,128)}, f32[1,256,512]{2,1,0:T(8,128)}, u32[]{:S(2)}, u32[]{:S(2)}) collective-permute-start(f32[1,256,512]{2,1,0:T(8,128)} %constant_dynamic-slice_fusion.2), channel_id=1, source_target_pairs={{0,4},{1,5},{2,6},{3,7},{4,0},{5,1},{6,2},{7,3},{8,12},{9,13},{10,... | collective-permute-start | bytes 1572872 | tf_op jit(solution)/shard_map/ppermute | solution.py:78
  287.6 70.0 %collective-permute-start.13 = (f32[1024,512]{1,0:T(8,128)}, f32[1024,512]{1,0:T(8,128)}, u32[]{:S(2)}, u32[]{:S(2)}) collective-permute-start(f32[1024,512]{1,0:T(8,128)} %fusion.6), channel_id=1, source_target_pairs={{0,1},{1,0},{2,3},{3,2},{4,5},{5,4},{6,7},{7,6},{8,9},{9,8},{10,11... | collective-permute-start | bytes 6291464 | tf_op jit(solution)/shard_map/ppermute | solution.py:78
  322.1 4.1 collective-permute-start.16
  323.6 231.1 %all-gather.14.cloned.1.call-start = ((), (), s32[]{:S(2)}) async-start(), calls=%async_computation.5 | async-start | bytes 2621440 | tf_op jit(solution)/shard_map/all_gather | solution.py:121
  324.1 33.6 %copy-start.20 = (bf16[1024,1024]{1,0:T(8,128)(2,1)S(1)}, bf16[1024,1024]{1,0:T(8,128)(2,1)}, u32[]{:S(2)}) copy-start(bf16[1024,1024]{1,0:T(8,128)(2,1)} %get-tuple-element.17) | copy-start | bytes 6291460
  324.1 33.6 %copy-start.22 = (bf16[1024,1024]{1,0:T(8,128)(2,1)S(1)}, bf16[1024,1024]{1,0:T(8,128)(2,1)}, u32[]{:S(2)}) copy-start(bf16[1024,1024]{1,0:T(8,128)(2,1)} %get-tuple-element.18) | copy-start | bytes 6291460
  328.0 49.6 %collective-permute-start.17 = (f32[2,1,128,512]{3,2,0,1:T(8,128)S(1)}, f32[2,1,128,512]{3,2,0,1:T(8,128)S(1)}, u32[]{:S(2)}, u32[]{:S(2)}) collective-permute-start(f32[2,1,128,512]{3,2,0,1:T(8,128)S(1)} %constant_dynamic-slice_fusion), channel_id=1, source_target_pairs={{0,16},{8,24},{16,0},{24,8},{1,17},{9,25},{17,1},{25,9},{2,18},{10... | collective-permute-start | bytes 1572872 | tf_op jit(solution)/shard_map/ppermute | solution.py:78
  377.8 13.9 %collective-permute-start.18 = (f32[2,128,512]{2,1,0:T(8,128)S(1)}, f32[2,128,512]{2,1,0:T(8,128)S(1)}, u32[]{:S(2)}, u32[]{:S(2)}) collective-permute-start(f32[2,128,512]{2,1,0:T(8,128)S(1)} %add_bitcast_fusion), channel_id=1, source_target_pairs={{0,1},{1,0},{2,3},{3,2},{4,5},{5,4},{6,7},{7,6},{8,9},{9,8},{10,11... | collective-permute-start | bytes 1572872 | tf_op jit(solution)/shard_map/ppermute | solution.py:78
  379.4 46.4 %collective-permute-start.14 = (f32[2,256,512]{2,1,0:T(8,128)S(1)}, f32[2,256,512]{2,1,0:T(8,128)S(1)}, u32[]{:S(2)}, u32[]{:S(2)}) collective-permute-start(f32[2,256,512]{2,1,0:T(8,128)S(1)} %dynamic-slice_bitcast_fusion), channel_id=1, source_target_pairs={{0,2},{1,3},{2,0},{3,1},{4,6},{5,7},{6,4},{7,5},{8,10},{9,11},{10,... | collective-permute-start | bytes 3145736 | tf_op jit(solution)/shard_map/ppermute | solution.py:78
  391.7 32.5 %collective-permute-start.19 = (f32[2,128,512]{2,1,0:T(8,128)S(1)}, f32[2,128,512]{2,1,0:T(8,128)S(1)}, u32[]{:S(2)}, u32[]{:S(2)}) collective-permute-start(f32[2,128,512]{2,1,0:T(8,128)S(1)} %add.231), channel_id=1, source_target_pairs={{0,2},{1,3},{2,0},{3,1},{4,6},{5,7},{6,4},{7,5},{8,10},{9,11},{10,... | collective-permute-start | bytes 1572872 | tf_op jit(solution)/shard_map/ppermute | solution.py:78
  424.3 39.8 %collective-permute-start.20 = (f32[2,128,512]{2,1,0:T(8,128)S(1)}, f32[2,128,512]{2,1,0:T(8,128)S(1)}, u32[]{:S(2)}, u32[]{:S(2)}) collective-permute-start(f32[2,128,512]{2,1,0:T(8,128)S(1)} %add.232), channel_id=1, source_target_pairs={{0,4},{1,5},{2,6},{3,7},{4,0},{5,1},{6,2},{7,3},{8,12},{9,13},{10,... | collective-permute-start | bytes 1572872 | tf_op jit(solution)/shard_map/ppermute | solution.py:78
  427.8 46.9 %collective-permute-start.15 = (f32[1,256,512]{2,1,0:T(8,128)}, f32[1,256,512]{2,1,0:T(8,128)}, u32[]{:S(2)}, u32[]{:S(2)}) collective-permute-start(f32[1,256,512]{2,1,0:T(8,128)} %constant_dynamic-slice_fusion.1), channel_id=1, source_target_pairs={{0,4},{1,5},{2,6},{3,7},{4,0},{5,1},{6,2},{7,3},{8,12},{9,13},{10,... | collective-permute-start | bytes 1572872 | tf_op jit(solution)/shard_map/ppermute | solution.py:78
  478.1 2.0 collective-permute-start.21
  480.2 11.2 %collective-permute-start.22 = (f32[1,1,128,512]{3,2,1,0:T(8,128)S(1)}, f32[1,1,128,512]{3,2,1,0:T(8,128)S(1)}, u32[]{:S(2)}, u32[]{:S(2)}) collective-permute-start(f32[1,1,128,512]{3,2,1,0:T(8,128)S(1)} %constant_dynamic-slice_fusion.7), channel_id=1, source_target_pairs={{0,16},{8,24},{16,0},{24,8},{1,17},{9,25},{17,1},{25,9},{2,18},{10... | collective-permute-start | bytes 786440 | tf_op jit(solution)/shard_map/ppermute | solution.py:78
  491.5 8.2 %collective-permute-start.23 = (f32[1,128,512]{2,1,0:T(8,128)S(1)}, f32[1,128,512]{2,1,0:T(8,128)}, u32[]{:S(2)}, u32[]{:S(2)}) collective-permute-start(f32[1,128,512]{2,1,0:T(8,128)S(1)} %add_bitcast_fusion.1), channel_id=1, source_target_pairs={{0,1},{1,0},{2,3},{3,2},{4,5},{5,4},{6,7},{7,6},{8,9},{9,8},{10,11... | collective-permute-start | bytes 786440 | tf_op jit(solution)/shard_map/ppermute | solution.py:78
  500.7 36.9 %collective-permute-start.24 = (f32[1,128,512]{2,1,0:T(8,128)S(1)}, f32[1,128,512]{2,1,0:T(8,128)}, u32[]{:S(2)}, u32[]{:S(2)}) collective-permute-start(f32[1,128,512]{2,1,0:T(8,128)S(1)} %add.240), channel_id=1, source_target_pairs={{0,2},{1,3},{2,0},{3,1},{4,6},{5,7},{6,4},{7,5},{8,10},{9,11},{10,... | collective-permute-start | bytes 786440 | tf_op jit(solution)/shard_map/ppermute | solution.py:78
  539.3 33.4 %collective-permute-start.25 = (f32[1,128,512]{2,1,0:T(8,128)}, f32[1,128,512]{2,1,0:T(8,128)S(1)}, u32[]{:S(2)}, u32[]{:S(2)}) collective-permute-start(f32[1,128,512]{2,1,0:T(8,128)} %add.241), channel_id=1, source_target_pairs={{0,4},{1,5},{2,6},{3,7},{4,0},{5,1},{6,2},{7,3},{8,12},{9,13},{10,... | collective-permute-start | bytes 786440 | tf_op jit(solution)/shard_map/ppermute | solution.py:78
  (31 other events, 190.9 us)
Sparse Core Ops, SparseCore 0:
  11.4 73.3 all-gather.5
  86.3 31.6 all-gather.7
  120.1 26.2 all-gather.9
  147.8 29.2 all-gather.11
  323.8 207.5 all-reduce.1
  532.7 21.9 all-gather.13

commit v4 on v3

--- a/solution.py
+++ b/solution.py
@@ -96,14 +96,13 @@
     for k in range(STEPS):
         gone = jnp.dot(left[0], right[k], preferred_element_type=jnp.float32)
         gone = exchange(after(gone, nearer[k - 2] if k > 1 else None), "col", 0)
+        nearer.append(gone)
         total = jnp.dot(left[1], right[k], preferred_element_type=jnp.float32) + gone
         for stage in range(1, col_count.bit_length() - 1):
             bit = (col_index >> stage) % 2
             pieces = total.reshape(total.shape[0] // (2 * share), 2, share, width)
             gone = exchange(pick(pieces, 1 - bit), "col", stage)
             total = (pick(pieces, bit) + gone).reshape(-1, width)
-            if stage == 1:
-                nearer.append(gone)
         if k > 0:
             total = total + dot(columns[-1], parent_panel[k - 1])
         columns.append(-own_masks[k] * total)
@@ -111,8 +110,8 @@
         if k + 1 < STEPS:
             parts.append(dot_t(columns[k], masked[k + 1]))
         if k == early:
-            nearer[k] = parts = jnp.stack(parts)
-            sums = lax.psum(parts, ("row", "col"))
+            sums = lax.psum_scatter(jnp.stack(parts), "row", scatter_dimension=1, tiled=True)
+            sums = lax.all_gather(lax.psum(sums, "col"), "row", axis=1, tiled=True)
             parts = []
         elif k > early:
             slab = reduce_slab(jnp.stack(parts))

time: 587 us -> 693 us (1.18)
  waiting for transfers between devices: 338 us -> 457 us
  starting transfers between devices: 95.8 us -> 57.4 us
  other arithmetic: 30.7 us -> 38.6 us
  local copies, waits for them, and re-layouts: 34.6 us -> 42.2 us
  matrix products: 67.4 us -> 74.5 us
    ppermute x22, waiting for transfers between devices: 205 us -> 300 us  [exchange(): lax.ppermute(value, axis, [(i, i ^ 1 << stage) for i in range(count)])]
    psum x1, waiting for transfers between devices: 30.6 us -> 69.5 us  [shards(): sums = lax.all_gather(lax.psum(sums, 'col'), 'row', axis=1, tiled=True)]
    ppermute x22, starting transfers between devices: 91.3 us -> 52.9 us  [exchange(): lax.ppermute(value, axis, [(i, i ^ 1 << stage) for i in range(count)])]
    all_gather x1, waiting for transfers between devices: 14 us -> 0.01 us  [shards(): lax.all_gather(slab, 'row', axis=1, tiled=True)]
  transfers between devices with their start and end apart: 32 -> 34, of which waited for: 20 -> 21; matrix products, arithmetic and copies ran while one was open for 21% -> 21% of each run, Pallas kernels for 0% -> 0%
where the time goes in v4:
time: 693 us; the launch traced here: 685 us
  waiting for transfers between devices  457 us (66%)
  matrix products  74.5 us (11%)
  starting transfers between devices  57.4 us (8%)
  local copies, waits for them, and re-layouts  42.2 us (6%)
  other arithmetic  38.6 us (6%)
  between operations  15.2 us (2%)
    ppermute x22, waiting for transfers between devices, exchange(): lax.ppermute(value, axis, [(i, i ^ 1 << stage) for i in range(count)])  300 us
    all_gather x4, waiting for transfers between devices, shards(): whole = lax.all_gather(part, 'row', axis=0, tiled=True)  87.6 us
    psum x1, waiting for transfers between devices, shards(): sums = lax.all_gather(lax.psum(sums, 'col'), 'row', axis=1, tiled=True)  69.5 us
    ppermute x22, starting transfers between devices, exchange(): lax.ppermute(value, axis, [(i, i ^ 1 << stage) for i in range(count)])  52.9 us
    dot_general x4, matrix products, shards(): jnp.dot(left[1], right[k], preferred_element_type=jnp.float32) + gone  26.8 us
    dot_general x4, matrix products, shards(): gone = jnp.dot(left[0], right[k], preferred_element_type=jnp.float32)  22.7 us
    dot_general x14, matrix products, dot_t(): lax.dot_general(a, b, (((0,), (0,)), ((), ())), precision=HIGH, preferred...  16.7 us
    convert_element_type x6, other arithmetic, split(): return (upper.astype(jnp.bfloat16), (value - upper).astype(jnp.bfloat16))  16.3 us
  transfers between devices with their start and end apart: 34, of which 21 were waited for; matrix products, arithmetic and copies ran while one was open for 21% of the time, Pallas kernels for 0%

profile of v4, /device:TPU:0, one launch (start us, length us, event | category | flops | bytes accessed | tf_op | source)
XLA Modules:
  0.0 685.3 jit_solution(6171351049566432400)
XLA Ops:
  8.0 2.5 bitcast_multiply_fusion.3
  13.7 6.8 constant_dynamic-slice_fusion.6
  20.5 2.2 fusion.1
  22.7 57.5 %all-gather.7.cloned.1.call-done = f32[1024,512]{1,0:T(8,128)} async-done(((f32[256,512]{1,0:T(8,128)}), f32[1024,512]{1,0:T(8,128)}) %all-gather.7.cloned.1.call-update) | async-done | bytes 2097168 | tf_op jit(solution)/shard_map/all_gather | solution.py:65
  80.2 2.1 reduce-precision_convert_fusion.5
  82.4 4.8 fusion.12
  88.6 21.7 %all-gather.9.cloned.1.call-done = f32[1024,512]{1,0:T(8,128)} async-done(((f32[256,512]{1,0:T(8,128)}), f32[1024,512]{1,0:T(8,128)}) %all-gather.9.cloned.1.call-update) | async-done | bytes 2097168 | tf_op jit(solution)/shard_map/all_gather | solution.py:65
  110.4 2.1 reduce-precision_convert_fusion.4
  112.6 4.7 fusion.10
  119.5 4.4 fusion
  125.3 19.9 %collective-permute-done.1 = f32[1024,512]{1,0:T(8,128)} collective-permute-done((f32[1024,512]{1,0:T(8,128)}, f32[1024,512]{1,0:T(8,128)}, u32[]{:S(2)}, u32[]{:S(2)}) %collective-permute-start.1) | collective-permute-done | bytes 2097184 | tf_op jit(solution)/shard_map/ppermute | solution.py:78
  145.2 7.3 %fusion.14 = f32[1024,512]{1,0:T(8,128)S(1)} fusion(f32[1024,512]{1,0:T(8,128)} %collective-permute-done.1, bf16[1024,512]{1,0:T(8,128)(2,1)} %copy-done.34, bf16[1024,512]{1,0:T(8,128)(2,1)} %copy-done.33, bf16[1024,1024]{1,0:T(8,128)(2,1)} %get-tuple-element.18, bf16[1024,1024]{1,0:T(8,128)(2,1)S(1)} %get-tuple-element.17), kind=kOutput, calls=%fused_computation.38 | convolution fusion | flops 3250061312 | bytes 10485760 | tf_op jit(solution)/shard_map/dot_general | solution.py:100
  153.7 6.4 collective-permute-start.2
  160.1 30.3 %collective-permute-done.5 = f32[1024,512]{1,0:T(8,128)} collective-permute-done((f32[1024,512]{1,0:T(8,128)}, f32[1024,512]{1,0:T(8,128)}, u32[]{:S(2)}, u32[]{:S(2)}) %collective-permute-start.5) | collective-permute-done | bytes 2097184 | tf_op jit(solution)/shard_map/ppermute | solution.py:78
  190.4 5.6 fusion.15
  196.2 5.3 collective-permute-start.6
  205.1 25.3 %collective-permute-done.6 = f32[2,256,512]{2,1,0:T(8,128)} collective-permute-done((f32[2,256,512]{2,1,0:T(8,128)S(1)}, f32[2,256,512]{2,1,0:T(8,128)}, u32[]{:S(2)}, u32[]{:S(2)}) %collective-permute-start.6) | collective-permute-done | bytes 1048608 | tf_op jit(solution)/shard_map/ppermute | solution.py:78
  232.1 4.3 collective-permute-done.3
  241.3 22.1 %collective-permute-done.7 = f32[1,256,512]{2,1,0:T(8,128)S(1)} collective-permute-done((f32[1,256,512]{2,1,0:T(8,128)S(1)}, f32[1,256,512]{2,1,0:T(8,128)S(1)}, u32[]{:S(2)}, u32[]{:S(2)}) %collective-permute-start.7) | collective-permute-done | bytes 524320 | tf_op jit(solution)/shard_map/ppermute | solution.py:78
  265.4 2.5 pad_maximum_fusion.2
  268.0 2.1 reduce-precision_convert_fusion.3
  270.9 4.7 fusion.8
  275.6 22.2 %collective-permute-start.9 = (f32[1024,512]{1,0:T(8,128)}, f32[1024,512]{1,0:T(8,128)}, u32[]{:S(2)}, u32[]{:S(2)}) collective-permute-start(f32[1024,512]{1,0:T(8,128)} %fusion.8), channel_id=1, source_target_pairs={{0,1},{1,0},{2,3},{3,2},{4,5},{5,4},{6,7},{7,6},{8,9},{9,8},{10,11... | collective-permute-start | bytes 6291464 | tf_op jit(solution)/shard_map/ppermute | solution.py:78
  299.4 55.2 %collective-permute-done.9 = f32[1024,512]{1,0:T(8,128)} collective-permute-done((f32[1024,512]{1,0:T(8,128)}, f32[1024,512]{1,0:T(8,128)}, u32[]{:S(2)}, u32[]{:S(2)}) %collective-permute-start.9) | collective-permute-done | bytes 2097184 | tf_op jit(solution)/shard_map/ppermute | solution.py:78
  354.5 7.8 %fusion.16 = f32[1024,512]{1,0:T(8,128)S(1)} fusion(f32[1024,512]{1,0:T(8,128)} %collective-permute-done.9, bf16[1024,512]{1,0:T(8,128)(2,1)} %copy-done.40, bf16[1024,512]{1,0:T(8,128)(2,1)} %copy-done.39, bf16[1024,1024]{1,0:T(8,128)(2,1)} %get-tuple-element.18, bf16[1024,1024]{1,0:T(8,128)(2,1)} %copy-done.24), kind=kOutput, calls=%fused_computation.40 | convolution fusion | flops 3250061312 | bytes 10485760 | tf_op jit(solution)/shard_map/dot_general | solution.py:100
  364.8 2.1 copy.35
  366.9 8.4 %all-gather.13.cloned.1.call-done = f32[1024,512]{1,0:T(8,128)} async-done(((f32[256,512]{1,0:T(8,128)}), f32[1024,512]{1,0:T(8,128)}) %all-gather.13.cloned.1.call-update) | async-done | bytes 2097168 | tf_op jit(solution)/shard_map/all_gather | solution.py:65
  375.3 3.4 reduce-precision_convert_fusion.2
  378.7 22.0 %collective-permute-done.10 = f32[2,256,512]{2,1,0:T(8,128)} collective-permute-done((f32[2,256,512]{2,1,0:T(8,128)}, f32[2,256,512]{2,1,0:T(8,128)}, u32[]{:S(2)}, u32[]{:S(2)}) %collective-permute-start.10) | collective-permute-done | bytes 1048608 | tf_op jit(solution)/shard_map/ppermute | solution.py:78
  404.0 69.5 %all-reduce.2.cloned.1.call-done = f32[4,128,512]{2,1,0:T(8,128)} async-done(((f32[4,128,512]{2,1,0:T(8,128)}), f32[4,128,512]{2,1,0:T(8,128)}) %all-reduce.2.cloned.1.call-update) | async-done | bytes 1048592 | tf_op jit(solution)/shard_map/psum | solution.py:114
  473.7 8.5 %fusion.6 = f32[1024,512]{1,0:T(8,128)} fusion(bf16[1024,512]{1,0:T(8,128)(2,1)} %get-tuple-element.30, bf16[1024,512]{1,0:T(8,128)(2,1)} %get-tuple-element.29, bf16[1024,1024]{1,0:T(8,128)(2,1)} %get-tuple-element.20, bf16[1024,1024]{1,0:T(8,128)(2,1)} %copy-done.28), kind=kOutput, calls=%fused_computation.30 | convolution fusion | flops 3249537024 | bytes 8388608 | tf_op jit(solution)/shard_map/dot_general | solution.py:97
  483.5 2.5 fusion.57
  494.0 3.0 collective-permute-done.16
  500.4 28.8 %collective-permute-done.13 = f32[1024,512]{1,0:T(8,128)} collective-permute-done((f32[1024,512]{1,0:T(8,128)}, f32[1024,512]{1,0:T(8,128)}, u32[]{:S(2)}, u32[]{:S(2)}) %collective-permute-start.13) | collective-permute-done | bytes 2097184 | tf_op jit(solution)/shard_map/ppermute | solution.py:78
  529.2 6.0 fusion.17
  538.0 9.8 %collective-permute-done.18 = f32[2,128,512]{2,1,0:T(8,128)S(1)} collective-permute-done((f32[2,128,512]{2,1,0:T(8,128)S(1)}, f32[2,128,512]{2,1,0:T(8,128)S(1)}, u32[]{:S(2)}, u32[]{:S(2)}) %collective-permute-start.18) | collective-permute-done | bytes 524320 | tf_op jit(solution)/shard_map/ppermute | solution.py:78
  548.2 23.6 %collective-permute-done.19 = f32[2,128,512]{2,1,0:T(8,128)S(1)} collective-permute-done((f32[2,128,512]{2,1,0:T(8,128)S(1)}, f32[2,128,512]{2,1,0:T(8,128)S(1)}, u32[]{:S(2)}, u32[]{:S(2)}) %collective-permute-start.19) | collective-permute-done | bytes 524320 | tf_op jit(solution)/shard_map/ppermute | solution.py:78
  571.9 2.7 collective-permute-start.20
  576.9 30.0 %collective-permute-done.20 = f32[2,128,512]{2,1,0:T(8,128)S(1)} collective-permute-done((f32[2,128,512]{2,1,0:T(8,128)S(1)}, f32[2,128,512]{2,1,0:T(8,128)S(1)}, u32[]{:S(2)}, u32[]{:S(2)}) %collective-permute-start.20) | collective-permute-done | bytes 524320 | tf_op jit(solution)/shard_map/ppermute | solution.py:78
  609.8 7.7 %collective-permute-done.15 = f32[1,256,512]{2,1,0:T(8,128)} collective-permute-done((f32[1,256,512]{2,1,0:T(8,128)}, f32[1,256,512]{2,1,0:T(8,128)}, u32[]{:S(2)}, u32[]{:S(2)}) %collective-permute-start.15) | collective-permute-done | bytes 524320 | tf_op jit(solution)/shard_map/ppermute | solution.py:78
  624.6 9.5 %collective-permute-done.22 = f32[1,1,128,512]{3,2,1,0:T(8,128)S(1)} collective-permute-done((f32[1,1,128,512]{3,2,1,0:T(8,128)S(1)}, f32[1,1,128,512]{3,2,1,0:T(8,128)S(1)}, u32[]{:S(2)}, u32[]{:S(2)}) %collective-permute-start.22) | collective-permute-done | bytes 262176 | tf_op jit(solution)/shard_map/ppermute | solution.py:78
  635.7 2.3 slice.85
  638.0 4.4 collective-permute-done.23
  648.2 2.4 collective-permute-done.24
  651.3 2.4 collective-permute-start.25
  653.8 4.6 constant_dynamic-update-slice_fusion.1
  658.4 3.1 constant_dynamic-update-slice_fusion
  661.5 3.9 fusion.94
  (200 shorter events, 79.7 us)
Async XLA Ops:
  7.2 73.0 %all-gather.7.cloned.1.call-start = ((), (), s32[]{:S(2)}) async-start(), calls=%async_computation.1 | async-start | bytes 2621440 | tf_op jit(solution)/shard_map/all_gather | solution.py:65
  10.5 108.3 %copy-start.7 = (f32[256,512]{1,0:T(8,128)}, f32[256,512]{1,0:T(8,128)S(1)}, u32[]{:S(2)}) copy-start(f32[256,512]{1,0:T(8,128)S(1)} %get-tuple-element.9) | copy-start | bytes 1572868
  10.5 0.7 collective-permute-start
  12.0 98.3 %all-gather.9.cloned.1.call-start = ((), (), s32[]{:S(2)}) async-start(), calls=%async_computation.2 | async-start | bytes 2621440 | tf_op jit(solution)/shard_map/all_gather | solution.py:65
  12.1 0.7 collective-permute-start.4
  13.6 254.4 %all-gather.11.cloned.1.call-start = ((), (), s32[]{:S(2)}) async-start(), calls=%async_computation.3 | async-start | bytes 2621440 | tf_op jit(solution)/shard_map/all_gather | solution.py:65
  22.7 89.7 %copy-start.28 = (bf16[1024,1024]{1,0:T(8,128)(2,1)}, bf16[1024,1024]{1,0:T(8,128)(2,1)S(1)}, u32[]{:S(2)}) copy-start(bf16[1024,1024]{1,0:T(8,128)(2,1)S(1)} %get-tuple-element.19) | copy-start | bytes 6291460
  87.2 58.1 %collective-permute-start.1 = (f32[1024,512]{1,0:T(8,128)}, f32[1024,512]{1,0:T(8,128)}, u32[]{:S(2)}, u32[]{:S(2)}) collective-permute-start(f32[1024,512]{1,0:T(8,128)} %fusion.12), channel_id=1, source_target_pairs={{0,1},{1,0},{2,3},{3,2},{4,5},{5,4},{6,7},{7,6},{8,9},{9,8},{10,11... | collective-permute-start | bytes 6291464 | tf_op jit(solution)/shard_map/ppermute | solution.py:78
  117.3 73.1 %collective-permute-start.5 = (f32[1024,512]{1,0:T(8,128)}, f32[1024,512]{1,0:T(8,128)}, u32[]{:S(2)}, u32[]{:S(2)}) collective-permute-start(f32[1024,512]{1,0:T(8,128)} %fusion.10), channel_id=1, source_target_pairs={{0,1},{1,0},{2,3},{3,2},{4,5},{5,4},{6,7},{7,6},{8,9},{9,8},{10,11... | collective-permute-start | bytes 6291464 | tf_op jit(solution)/shard_map/ppermute | solution.py:78
  118.8 5.1 collective-permute-start.8
  124.0 28.6 %copy-start.24 = (bf16[1024,1024]{1,0:T(8,128)(2,1)}, bf16[1024,1024]{1,0:T(8,128)(2,1)S(1)}, u32[]{:S(2)}) copy-start(bf16[1024,1024]{1,0:T(8,128)(2,1)S(1)} %get-tuple-element.17) | copy-start | bytes 6291460
  124.8 240.0 %reduce-scatter.2.cloned.1.call-start = ((), (), s32[]{:S(2)}) async-start(), calls=%async_computation.5 | async-start | bytes 5242880 | tf_op jit(solution)/shard_map/reduce_scatter | solution.py:113
  145.2 45.2 %copy-start.26 = (bf16[1024,1024]{1,0:T(8,128)(2,1)S(1)}, bf16[1024,1024]{1,0:T(8,128)(2,1)}, u32[]{:S(2)}) copy-start(bf16[1024,1024]{1,0:T(8,128)(2,1)} %get-tuple-element.18) | copy-start | bytes 6291460
  145.2 45.2 %copy-start.36 = (bf16[1024,512]{1,0:T(8,128)(2,1)S(1)}, bf16[1024,512]{1,0:T(8,128)(2,1)}, u32[]{:S(2)}) copy-start(bf16[1024,512]{1,0:T(8,128)(2,1)} %copy-done.35) | copy-start | bytes 3145732
  145.2 45.2 %copy-start.38 = (bf16[1024,512]{1,0:T(8,128)(2,1)S(1)}, bf16[1024,512]{1,0:T(8,128)(2,1)}, u32[]{:S(2)}) copy-start(bf16[1024,512]{1,0:T(8,128)(2,1)} %copy-done.37) | copy-start | bytes 3145732
  152.6 43.5 %copy-start.20 = (f32[1024,512]{1,0:T(8,128)}, f32[1024,512]{1,0:T(8,128)S(1)}, u32[]{:S(2)}) copy-start(f32[1024,512]{1,0:T(8,128)S(1)} %fusion.14) | copy-start | bytes 6291460
  153.7 47.8 %collective-permute-start.2 = (f32[2,256,512]{2,1,0:T(8,128)}, f32[2,256,512]{2,1,0:T(8,128)}, u32[]{:S(2)}, u32[]{:S(2)}) collective-permute-start(f32[2,256,512]{2,1,0:T(8,128)} %dynamic-slice_bitcast_fusion.3), channel_id=1, source_target_pairs={{0,2},{1,3},{2,0},{3,1},{4,6},{5,7},{6,4},{7,5},{8,10},{9,11},{10,... | collective-permute-start | bytes 3145736 | tf_op jit(solution)/shard_map/ppermute | solution.py:78
  196.2 34.3 %collective-permute-start.6 = (f32[2,256,512]{2,1,0:T(8,128)S(1)}, f32[2,256,512]{2,1,0:T(8,128)}, u32[]{:S(2)}, u32[]{:S(2)}) collective-permute-start(f32[2,256,512]{2,1,0:T(8,128)S(1)} %dynamic-slice_bitcast_fusion.2), channel_id=1, source_target_pairs={{0,2},{1,3},{2,0},{3,1},{4,6},{5,7},{6,4},{7,5},{8,10},{9,11},{10,... | collective-permute-start | bytes 3145736 | tf_op jit(solution)/shard_map/ppermute | solution.py:78
  205.1 31.2 %collective-permute-start.3 = (f32[1,256,512]{2,1,0:T(8,128)}, f32[1,256,512]{2,1,0:T(8,128)}, u32[]{:S(2)}, u32[]{:S(2)}) collective-permute-start(f32[1,256,512]{2,1,0:T(8,128)} %constant_dynamic-slice_fusion.4), channel_id=1, source_target_pairs={{0,4},{1,5},{2,6},{3,7},{4,0},{5,1},{6,2},{7,3},{8,12},{9,13},{10,... | collective-permute-start | bytes 1572872 | tf_op jit(solution)/shard_map/ppermute | solution.py:78
  205.1 31.2 %copy-start.16 = (f32[2,256,512]{2,1,0:T(8,128)S(1)}, f32[2,256,512]{2,1,0:T(8,128)}, u32[]{:S(2)}) copy-start(f32[2,256,512]{2,1,0:T(8,128)} %copy-done.15) | copy-start | bytes 3145732
  232.0 31.4 %copy-start = (f32[3,512,512]{2,1,0:T(8,128)S(1)}, f32[3,512,512]{2,1,0:T(8,128)}, u32[]{:S(2)}) copy-start(f32[3,512,512]{2,1,0:T(8,128)} %param.7) | copy-start | bytes 9437188
  232.0 31.4 %collective-permute-start.7 = (f32[1,256,512]{2,1,0:T(8,128)S(1)}, f32[1,256,512]{2,1,0:T(8,128)S(1)}, u32[]{:S(2)}, u32[]{:S(2)}) collective-permute-start(f32[1,256,512]{2,1,0:T(8,128)S(1)} %constant_dynamic-slice_fusion.3), channel_id=1, source_target_pairs={{0,4},{1,5},{2,6},{3,7},{4,0},{5,1},{6,2},{7,3},{8,12},{9,13},{10,... | collective-permute-start | bytes 1572872 | tf_op jit(solution)/shard_map/ppermute | solution.py:78
  237.5 26.5 %copy-start.1 = (f32[1,256,512]{2,1,0:T(8,128)}, f32[1,256,512]{2,1,0:T(8,128)S(1)}, u32[]{:S(2)}) copy-start(f32[1,256,512]{2,1,0:T(8,128)S(1)} %add_multiply_fusion) | copy-start | bytes 1572868
  267.9 107.3 %all-gather.13.cloned.1.call-start = ((), (), s32[]{:S(2)}) async-start(), calls=%async_computation.4 | async-start | bytes 2621440 | tf_op jit(solution)/shard_map/all_gather | solution.py:65
  270.9 27.0 %copy-start.17 = (f32[256,512]{1,0:T(8,128)S(1)}, f32[256,512]{1,0:T(8,128)}, u32[]{:S(2)}) copy-start(f32[256,512]{1,0:T(8,128)} %get-tuple-element.11) | copy-start | bytes 1572868
  275.6 78.9 %collective-permute-start.9 = (f32[1024,512]{1,0:T(8,128)}, f32[1024,512]{1,0:T(8,128)}, u32[]{:S(2)}, u32[]{:S(2)}) collective-permute-start(f32[1024,512]{1,0:T(8,128)} %fusion.8), channel_id=1, source_target_pairs={{0,1},{1,0},{2,3},{3,2},{4,5},{5,4},{6,7},{7,6},{8,9},{9,8},{10,11... | collective-permute-start | bytes 6291464 | tf_op jit(solution)/shard_map/ppermute | solution.py:78
  297.8 1.5 collective-permute-start.12
  299.3 174.2 %all-reduce.2.cloned.1.call-start = ((), (), s32[]{:S(2)}) async-start(), calls=%async_computation.6 | async-start | bytes 2097152 | tf_op jit(solution)/shard_map/psum | solution.py:114
  364.7 36.0 %collective-permute-start.10 = (f32[2,256,512]{2,1,0:T(8,128)}, f32[2,256,512]{2,1,0:T(8,128)}, u32[]{:S(2)}, u32[]{:S(2)}) collective-permute-start(f32[2,256,512]{2,1,0:T(8,128)} %dynamic-slice_bitcast_fusion.1), channel_id=1, source_target_pairs={{0,2},{1,3},{2,0},{3,1},{4,6},{5,7},{6,4},{7,5},{8,10},{9,11},{10,... | collective-permute-start | bytes 3145736 | tf_op jit(solution)/shard_map/ppermute | solution.py:78
  364.8 289.0 %all-gather.15.cloned.1.call-start = ((), (), s32[]{:S(2)}) async-start(), calls=%async_computation.7 | async-start | bytes 5242880 | tf_op jit(solution)/shard_map/all_gather | solution.py:114
  375.3 25.5 %copy-start.19 = (f32[1024,512]{1,0:T(8,128)S(1)}, f32[1024,512]{1,0:T(8,128)}, u32[]{:S(2)}) copy-start(f32[1024,512]{1,0:T(8,128)} %copy-done.18) | copy-start | bytes 6291460
  404.0 79.5 %collective-permute-start.11 = (f32[1,256,512]{2,1,0:T(8,128)}, f32[1,256,512]{2,1,0:T(8,128)}, u32[]{:S(2)}, u32[]{:S(2)}) collective-permute-start(f32[1,256,512]{2,1,0:T(8,128)} %constant_dynamic-slice_fusion.2), channel_id=1, source_target_pairs={{0,4},{1,5},{2,6},{3,7},{4,0},{5,1},{6,2},{7,3},{8,12},{9,13},{10,... | collective-permute-start | bytes 1572872 | tf_op jit(solution)/shard_map/ppermute | solution.py:78
  473.5 184.9 %all-gather.17.cloned.1.call-start = ((), (), s32[]{:S(2)}) async-start(), calls=%async_computation.8 | async-start | bytes 2621440 | tf_op jit(solution)/shard_map/all_gather | solution.py:120
  482.2 47.0 %collective-permute-start.13 = (f32[1024,512]{1,0:T(8,128)}, f32[1024,512]{1,0:T(8,128)}, u32[]{:S(2)}, u32[]{:S(2)}) collective-permute-start(f32[1024,512]{1,0:T(8,128)} %fusion.6), channel_id=1, source_target_pairs={{0,1},{1,0},{2,3},{3,2},{4,5},{5,4},{6,7},{7,6},{8,9},{9,8},{10,11... | collective-permute-start | bytes 6291464 | tf_op jit(solution)/shard_map/ppermute | solution.py:78
  494.0 3.0 collective-permute-start.16
  494.0 35.3 %copy-start.25 = (bf16[1024,1024]{1,0:T(8,128)(2,1)S(1)}, bf16[1024,1024]{1,0:T(8,128)(2,1)}, u32[]{:S(2)}) copy-start(bf16[1024,1024]{1,0:T(8,128)(2,1)} %copy-done.24) | copy-start | bytes 6291460
  494.0 35.3 %copy-start.27 = (bf16[1024,1024]{1,0:T(8,128)(2,1)S(1)}, bf16[1024,1024]{1,0:T(8,128)(2,1)}, u32[]{:S(2)}) copy-start(bf16[1024,1024]{1,0:T(8,128)(2,1)} %get-tuple-element.18) | copy-start | bytes 6291460
  498.8 36.4 %collective-permute-start.17 = (f32[2,1,128,512]{3,2,0,1:T(8,128)S(1)}, f32[2,1,128,512]{3,2,0,1:T(8,128)S(1)}, u32[]{:S(2)}, u32[]{:S(2)}) collective-permute-start(f32[2,1,128,512]{3,2,0,1:T(8,128)S(1)} %constant_dynamic-slice_fusion), channel_id=1, source_target_pairs={{0,16},{8,24},{16,0},{24,8},{1,17},{9,25},{17,1},{25,9},{2,18},{10... | collective-permute-start | bytes 1572872 | tf_op jit(solution)/shard_map/ppermute | solution.py:78
  535.3 12.4 %collective-permute-start.18 = (f32[2,128,512]{2,1,0:T(8,128)S(1)}, f32[2,128,512]{2,1,0:T(8,128)S(1)}, u32[]{:S(2)}, u32[]{:S(2)}) collective-permute-start(f32[2,128,512]{2,1,0:T(8,128)S(1)} %add_bitcast_fusion), channel_id=1, source_target_pairs={{0,1},{1,0},{2,3},{3,2},{4,5},{5,4},{6,7},{7,6},{8,9},{9,8},{10,11... | collective-permute-start | bytes 1572872 | tf_op jit(solution)/shard_map/ppermute | solution.py:78
  537.1 37.5 %collective-permute-start.14 = (f32[2,256,512]{2,1,0:T(8,128)S(1)}, f32[2,256,512]{2,1,0:T(8,128)S(1)}, u32[]{:S(2)}, u32[]{:S(2)}) collective-permute-start(f32[2,256,512]{2,1,0:T(8,128)S(1)} %dynamic-slice_bitcast_fusion), channel_id=1, source_target_pairs={{0,2},{1,3},{2,0},{3,1},{4,6},{5,7},{6,4},{7,5},{8,10},{9,11},{10,... | collective-permute-start | bytes 3145736 | tf_op jit(solution)/shard_map/ppermute | solution.py:78
  547.8 24.0 %collective-permute-start.19 = (f32[2,128,512]{2,1,0:T(8,128)S(1)}, f32[2,128,512]{2,1,0:T(8,128)S(1)}, u32[]{:S(2)}, u32[]{:S(2)}) collective-permute-start(f32[2,128,512]{2,1,0:T(8,128)S(1)} %add.233), channel_id=1, source_target_pairs={{0,2},{1,3},{2,0},{3,1},{4,6},{5,7},{6,4},{7,5},{8,10},{9,11},{10,... | collective-permute-start | bytes 1572872 | tf_op jit(solution)/shard_map/ppermute | solution.py:78
  571.9 35.0 %collective-permute-start.20 = (f32[2,128,512]{2,1,0:T(8,128)S(1)}, f32[2,128,512]{2,1,0:T(8,128)S(1)}, u32[]{:S(2)}, u32[]{:S(2)}) collective-permute-start(f32[2,128,512]{2,1,0:T(8,128)S(1)} %add.234), channel_id=1, source_target_pairs={{0,4},{1,5},{2,6},{3,7},{4,0},{5,1},{6,2},{7,3},{8,12},{9,13},{10,... | collective-permute-start | bytes 1572872 | tf_op jit(solution)/shard_map/ppermute | solution.py:78
  576.6 40.9 %collective-permute-start.15 = (f32[1,256,512]{2,1,0:T(8,128)}, f32[1,256,512]{2,1,0:T(8,128)}, u32[]{:S(2)}, u32[]{:S(2)}) collective-permute-start(f32[1,256,512]{2,1,0:T(8,128)} %constant_dynamic-slice_fusion.1), channel_id=1, source_target_pairs={{0,4},{1,5},{2,6},{3,7},{4,0},{5,1},{6,2},{7,3},{8,12},{9,13},{10,... | collective-permute-start | bytes 1572872 | tf_op jit(solution)/shard_map/ppermute | solution.py:78
  621.0 2.0 collective-permute-start.21
  623.1 11.0 %collective-permute-start.22 = (f32[1,1,128,512]{3,2,1,0:T(8,128)S(1)}, f32[1,1,128,512]{3,2,1,0:T(8,128)S(1)}, u32[]{:S(2)}, u32[]{:S(2)}) collective-permute-start(f32[1,1,128,512]{3,2,1,0:T(8,128)S(1)} %constant_dynamic-slice_fusion.7), channel_id=1, source_target_pairs={{0,16},{8,24},{16,0},{24,8},{1,17},{9,25},{17,1},{25,9},{2,18},{10... | collective-permute-start | bytes 786440 | tf_op jit(solution)/shard_map/ppermute | solution.py:78
  634.1 8.2 %collective-permute-start.23 = (f32[1,128,512]{2,1,0:T(8,128)S(1)}, f32[1,128,512]{2,1,0:T(8,128)}, u32[]{:S(2)}, u32[]{:S(2)}) collective-permute-start(f32[1,128,512]{2,1,0:T(8,128)S(1)} %add_bitcast_fusion.1), channel_id=1, source_target_pairs={{0,1},{1,0},{2,3},{3,2},{4,5},{5,4},{6,7},{7,6},{8,9},{9,8},{10,11... | collective-permute-start | bytes 786440 | tf_op jit(solution)/shard_map/ppermute | solution.py:78
  643.4 7.2 %collective-permute-start.24 = (f32[1,128,512]{2,1,0:T(8,128)S(1)}, f32[1,128,512]{2,1,0:T(8,128)S(1)}, u32[]{:S(2)}, u32[]{:S(2)}) collective-permute-start(f32[1,128,512]{2,1,0:T(8,128)S(1)} %add.242), channel_id=1, source_target_pairs={{0,2},{1,3},{2,0},{3,1},{4,6},{5,7},{6,4},{7,5},{8,10},{9,11},{10,... | collective-permute-start | bytes 786440 | tf_op jit(solution)/shard_map/ppermute | solution.py:78
  651.3 24.7 %collective-permute-start.25 = (f32[1,128,512]{2,1,0:T(8,128)}, f32[1,128,512]{2,1,0:T(8,128)}, u32[]{:S(2)}, u32[]{:S(2)}) collective-permute-start(f32[1,128,512]{2,1,0:T(8,128)} %add.243), channel_id=1, source_target_pairs={{0,4},{1,5},{2,6},{3,7},{4,0},{5,1},{6,2},{7,3},{8,12},{9,13},{10,... | collective-permute-start | bytes 786440 | tf_op jit(solution)/shard_map/ppermute | solution.py:78
  (31 other events, 177.0 us)
Sparse Core Ops, SparseCore 0:
  12.2 67.9 all-gather.6
  82.3 27.9 all-gather.8
  124.9 94.4 all-gather.10
  268.1 67.5 reduce-scatter.1
  337.1 38.1 all-gather.12
  379.0 94.3 all-reduce.1
  475.0 39.9 all-gather.14
  607.9 24.6 all-gather.16

commit v5 on v4

--- a/solution.py
+++ b/solution.py
@@ -90,34 +90,31 @@
         return parts
 
     columns = []
-    nearer = []
+    def first_exchange(k, earlier):
+        gone = jnp.dot(left[0], right[k], preferred_element_type=jnp.float32)
+        return exchange(after(gone, earlier), "col", 0)
+
     parts = []
-    early = STEPS - 3
+    arrived = [first_exchange(0, None), first_exchange(1, None)]
     for k in range(STEPS):
-        gone = jnp.dot(left[0], right[k], preferred_element_type=jnp.float32)
-        gone = exchange(after(gone, nearer[k - 2] if k > 1 else None), "col", 0)
-        nearer.append(gone)
-        total = jnp.dot(left[1], right[k], preferred_element_type=jnp.float32) + gone
+        total = jnp.dot(left[1], right[k], preferred_element_type=jnp.float32) + arrived[k]
         for stage in range(1, col_count.bit_length() - 1):
             bit = (col_index >> stage) % 2
             pieces = total.reshape(total.shape[0] // (2 * share), 2, share, width)
             gone = exchange(pick(pieces, 1 - bit), "col", stage)
             total = (pick(pieces, bit) + gone).reshape(-1, width)
+            if stage == 1 and k + 2 < STEPS:
+                arrived.append(first_exchange(k + 2, gone))
         if k > 0:
             total = total + dot(columns[-1], parent_panel[k - 1])
         columns.append(-own_masks[k] * total)
         parts.append(dot_t(masked[k], columns[k]))
         if k + 1 < STEPS:
             parts.append(dot_t(columns[k], masked[k + 1]))
-        if k == early:
-            sums = lax.psum_scatter(jnp.stack(parts), "row", scatter_dimension=1, tiled=True)
-            sums = lax.all_gather(lax.psum(sums, "col"), "row", axis=1, tiled=True)
+        if k == STEPS - 2:
+            sums = lax.psum(after(jnp.stack(parts), arrived[-1]), ("row", "col"))
             parts = []
-        elif k > early:
-            slab = reduce_slab(jnp.stack(parts))
-            parts = []
-            if k + 1 < STEPS:
-                sums = jnp.concatenate([sums, lax.all_gather(slab, "row", axis=1, tiled=True)])
+    slab = reduce_slab(jnp.stack(parts))
     diag_sums = sums[0::2]
     cross_sums = sums[1::2]
 
@@ -127,16 +124,19 @@
     def own_columns(value):
         return lax.dynamic_slice_in_dim(value, row_index * out_rows, out_rows, 1)
 
+    offsets = [lax.optimization_barrier(dot_t(value, value)) for value in diag_inverse[:-1]]
     links = []
     diagonals = []
     for k in range(STEPS - 1):
-        diagonal = dot_t(diag_inverse[k], diag_inverse[k]) - diag_sums[k]
+        diagonal = offsets[k] - diag_sums[k]
         if k > 0:
             diagonal = diagonal - dot_t(parent_panel[k - 1], links[-1])
         diagonals.append(diagonal)
         links.append(-(cross_sums[k] + dot(diagonal, parent_panel[k])))
-    last = dot_t(own_columns(diag_inverse[-1]), diag_inverse[-1])
-    last = last - dot_t(own_columns(parent_panel[-1]), links[-1]) - slab[0]
+    last = lax.optimization_barrier(
+        dot_t(own_columns(diag_inverse[-1]), diag_inverse[-1]) - slab[0]
+    )
+    last = last - dot_t(own_columns(parent_panel[-1]), links[-1])
     return (
         jnp.stack(columns),
         jnp.stack([own_slab(value) for value in links]),

time: 693 us -> 578 us (0.83)
  waiting for transfers between devices: 457 us -> 288 us
  starting transfers between devices: 57.4 us -> 154 us
  local copies, waits for them, and re-layouts: 42.2 us -> 21.6 us
  other arithmetic: 38.6 us -> 24.3 us
    ppermute x22 -> x17, waiting for transfers between devices: 300 us -> 114 us  [exchange(): lax.ppermute(value, axis, [(i, i ^ 1 << stage) for i in range(count)])]
    ppermute x22 -> x17, starting transfers between devices: 52.9 us -> 151 us  [exchange(): lax.ppermute(value, axis, [(i, i ^ 1 << stage) for i in range(count)])]
    psum x1, waiting for transfers between devices: 69.5 us -> 86.4 us  [shards(): sums = lax.psum(after(jnp.stack(parts), arrived[-1]), ('row', 'col'))]
    dot_general x8, matrix products: 49.5 us -> 40.3 us  [the longest x4 21.4 us: shards(): jnp.dot(left[1], right[k], preferred_element_type=jnp.float32) + arrived[k]]
  transfers between devices with their start and end apart: 34 -> 26, of which waited for: 21 -> 13; matrix products, arithmetic and copies ran while one was open for 21% -> 16% of each run, Pallas kernels for 0% -> 0%
where the time goes in v5:
time: 578 us; the launch traced here: 572 us
  waiting for transfers between devices  288 us (50%)
  starting transfers between devices  154 us (27%)
  matrix products  68.7 us (12%)
  other arithmetic  24.3 us (4%)
  local copies, waits for them, and re-layouts  21.6 us (4%)
  between operations  14.7 us (3%)
    ppermute x17, starting transfers between devices, exchange(): lax.ppermute(value, axis, [(i, i ^ 1 << stage) for i in range(count)])  151 us
    ppermute x17, waiting for transfers between devices, exchange(): lax.ppermute(value, axis, [(i, i ^ 1 << stage) for i in range(count)])  114 us
    all_gather x4, waiting for transfers between devices, shards(): whole = lax.all_gather(part, 'row', axis=0, tiled=True)  87.7 us
    psum x1, waiting for transfers between devices, shards(): sums = lax.psum(after(jnp.stack(parts), arrived[-1]), ('row', 'col'))  86.4 us
    dot_general x14, matrix products, dot_t(): lax.dot_general(a, b, (((0,), (0,)), ((), ())), precision=HIGH, preferred...  21.9 us
    dot_general x4, matrix products, shards(): jnp.dot(left[1], right[k], preferred_element_type=jnp.float32) + arrived[k]  21.4 us
    dot_general x4, matrix products, first_exchange(): gone = jnp.dot(left[0], right[k], preferred_element_type=jnp.float32)  18.9 us
    convert_element_type x6, other arithmetic, split(): return (upper.astype(jnp.bfloat16), (value - upper).astype(jnp.bfloat16))  15.7 us
  transfers between devices with their start and end apart: 26, of which 13 were waited for; matrix products, arithmetic and copies ran while one was open for 16% of the time, Pallas kernels for 0%

profile of v5, /device:TPU:0, one launch (start us, length us, event | category | flops | bytes accessed | tf_op | source)
XLA Modules:
  0.0 571.8 jit_solution(11771942118300128065)
XLA Ops:
  8.0 1.7 bitcast_multiply_fusion.3
  14.6 6.8 %constant_dynamic-slice_fusion.6 = (f32[4,1,256,1024]{3,2,1,0:T(8,128)}, f32[4,1,256,1024]{3,2,1,0:T(8,128)S(1)}) fusion(f32[4,2,256,1024]{3,2,1,0:T(8,128)} %bitcast.224, s32[]{:T(128)S(6)} %select_n.145, s32[]{:T(128)S(6)} %select_n.146), kind=kLoop, calls=%fused_computation.155 | loop fusion | bytes 16777224 | tf_op jit(solution)/shard_map/jit(dynamic_index_in_dim)/dynamic_slice | solution.py:40
  22.0 2.2 fusion.1
  25.3 5.1 fusion
  31.4 53.4 %all-gather.5.cloned.1.call-done = f32[1024,512]{1,0:T(8,128)} async-done(((f32[256,512]{1,0:T(8,128)}), f32[1024,512]{1,0:T(8,128)}) %all-gather.5.cloned.1.call-update) | async-done | bytes 2097168 | tf_op jit(solution)/shard_map/all_gather | solution.py:65
  84.8 2.1 reduce-precision_convert_fusion.5
  87.0 4.8 fusion.12
  91.8 34.2 %collective-permute-start.1 = (f32[1024,512]{1,0:T(8,128)}, f32[1024,512]{1,0:T(8,128)}, u32[]{:S(2)}, u32[]{:S(2)}) collective-permute-start(f32[1024,512]{1,0:T(8,128)} %fusion.12), channel_id=1, source_target_pairs={{0,1},{1,0},{2,3},{3,2},{4,5},{5,4},{6,7},{7,6},{8,9},{9,8},{10,11... | collective-permute-start | bytes 6291464 | tf_op jit(solution)/shard_map/ppermute | solution.py:78
  126.0 2.1 reduce-precision_convert_fusion.4
  128.4 4.7 fusion.10
  133.1 11.1 %all-gather.9.cloned.1.call-done = f32[1024,512]{1,0:T(8,128)} async-done(((f32[256,512]{1,0:T(8,128)}), f32[1024,512]{1,0:T(8,128)}) %all-gather.9.cloned.1.call-update) | async-done | bytes 2097168 | tf_op jit(solution)/shard_map/all_gather | solution.py:65
  144.2 2.1 reduce-precision_convert_fusion.3
  147.6 4.7 fusion.8
  152.3 23.2 %all-gather.11.cloned.1.call-done = f32[1024,512]{1,0:T(8,128)} async-done(((f32[256,512]{1,0:T(8,128)}), f32[1024,512]{1,0:T(8,128)}) %all-gather.11.cloned.1.call-update) | async-done | bytes 2097168 | tf_op jit(solution)/shard_map/all_gather | solution.py:65
  175.5 2.1 reduce-precision_convert_fusion.2
  178.4 6.1 %fusion.14 = f32[1024,512]{1,0:T(8,128)S(1)} fusion(f32[1024,512]{1,0:T(8,128)} %collective-permute-done.1, bf16[1024,512]{1,0:T(8,128)(2,1)} %copy-done.34, bf16[1024,512]{1,0:T(8,128)(2,1)} %copy-done.33, bf16[1024,1024]{1,0:T(8,128)(2,1)S(1)} %copy-done.28, bf16[1024,1024]{1,0:T(8,128)(2,1)S(1)} %copy-done.27), kind=kOutput, calls=%fused_computation.33 | convolution fusion | flops 3250061312 | bytes 10485760 | tf_op jit(solution)/shard_map/dot_general | solution.py:100
  186.2 29.3 %collective-permute-done.5 = f32[1024,512]{1,0:T(8,128)} collective-permute-done((f32[1024,512]{1,0:T(8,128)}, f32[1024,512]{1,0:T(8,128)}, u32[]{:S(2)}, u32[]{:S(2)}) %collective-permute-start.5) | collective-permute-done | bytes 2097184 | tf_op jit(solution)/shard_map/ppermute | solution.py:78
  215.5 5.2 fusion.15
  220.8 3.2 collective-permute-start.6
  224.0 2.5 collective-permute-start.9
  226.8 19.1 %collective-permute-start.3 = (f32[1,256,512]{2,1,0:T(8,128)S(1)}, f32[1,256,512]{2,1,0:T(8,128)S(1)}, u32[]{:S(2)}, u32[]{:S(2)}) collective-permute-start(f32[1,256,512]{2,1,0:T(8,128)S(1)} %constant_dynamic-slice_fusion.4), channel_id=1, source_target_pairs={{0,4},{1,5},{2,6},{3,7},{4,0},{5,1},{6,2},{7,3},{8,12},{9,13},{10,... | collective-permute-start | bytes 1572872 | tf_op jit(solution)/shard_map/ppermute | solution.py:78
  245.9 4.7 fusion.6
  250.6 7.1 %collective-permute-start.13 = (f32[1024,512]{1,0:T(8,128)}, f32[1024,512]{1,0:T(8,128)}, u32[]{:S(2)}, u32[]{:S(2)}) collective-permute-start(f32[1024,512]{1,0:T(8,128)} %fusion.6), channel_id=1, source_target_pairs={{0,1},{1,0},{2,3},{3,2},{4,5},{5,4},{6,7},{7,6},{8,9},{9,8},{10,11... | collective-permute-start | bytes 6291464 | tf_op jit(solution)/shard_map/ppermute | solution.py:78
  258.0 19.2 %collective-permute-start.7 = (f32[1,256,512]{2,1,0:T(8,128)S(1)}, f32[1,256,512]{2,1,0:T(8,128)S(1)}, u32[]{:S(2)}, u32[]{:S(2)}) collective-permute-start(f32[1,256,512]{2,1,0:T(8,128)S(1)} %constant_dynamic-slice_fusion.3), channel_id=1, source_target_pairs={{0,4},{1,5},{2,6},{3,7},{4,0},{5,1},{6,2},{7,3},{8,12},{9,13},{10,... | collective-permute-start | bytes 1572872 | tf_op jit(solution)/shard_map/ppermute | solution.py:78
  277.3 1.8 fusion.28
  279.1 1.8 fusion.27
  280.9 5.0 fusion.16
  286.0 2.6 collective-permute-start.10
  288.6 25.7 %collective-permute-done.13 = f32[1024,512]{1,0:T(8,128)} collective-permute-done((f32[1024,512]{1,0:T(8,128)}, f32[1024,512]{1,0:T(8,128)}, u32[]{:S(2)}, u32[]{:S(2)}) %collective-permute-start.13) | collective-permute-done | bytes 2097184 | tf_op jit(solution)/shard_map/ppermute | solution.py:78
  314.3 5.0 fusion.17
  320.4 2.0 fusion.26
  322.7 20.9 %collective-permute-start.11 = (f32[1,256,512]{2,1,0:T(8,128)S(1)}, f32[1,256,512]{2,1,0:T(8,128)S(1)}, u32[]{:S(2)}, u32[]{:S(2)}) collective-permute-start(f32[1,256,512]{2,1,0:T(8,128)S(1)} %constant_dynamic-slice_fusion.2), channel_id=1, source_target_pairs={{0,4},{1,5},{2,6},{3,7},{4,0},{5,1},{6,2},{7,3},{8,12},{9,13},{10,... | collective-permute-start | bytes 1572872 | tf_op jit(solution)/shard_map/ppermute | solution.py:78
  345.2 8.8 %collective-permute-done.14 = f32[2,256,512]{2,1,0:T(8,128)S(1)} collective-permute-done((f32[2,256,512]{2,1,0:T(8,128)S(1)}, f32[2,256,512]{2,1,0:T(8,128)S(1)}, u32[]{:S(2)}, u32[]{:S(2)}) %collective-permute-start.14) | collective-permute-done | bytes 1048608 | tf_op jit(solution)/shard_map/ppermute | solution.py:78
  355.0 17.8 %collective-permute-start.15 = (f32[1,256,512]{2,1,0:T(8,128)}, f32[1,256,512]{2,1,0:T(8,128)}, u32[]{:S(2)}, u32[]{:S(2)}) collective-permute-start(f32[1,256,512]{2,1,0:T(8,128)} %constant_dynamic-slice_fusion.1), channel_id=1, source_target_pairs={{0,4},{1,5},{2,6},{3,7},{4,0},{5,1},{6,2},{7,3},{8,12},{9,13},{10,... | collective-permute-start | bytes 1572872 | tf_op jit(solution)/shard_map/ppermute | solution.py:78
  376.8 20.9 %collective-permute-done.15 = f32[1,256,512]{2,1,0:T(8,128)} collective-permute-done((f32[1,256,512]{2,1,0:T(8,128)}, f32[1,256,512]{2,1,0:T(8,128)}, u32[]{:S(2)}, u32[]{:S(2)}) %collective-permute-start.15) | collective-permute-done | bytes 524320 | tf_op jit(solution)/shard_map/ppermute | solution.py:78
  397.8 2.0 fusion.64
  403.0 2.2 collective-permute-done.16
  406.6 18.6 %collective-permute-start.17 = (f32[1,1,128,512]{3,2,1,0:T(8,128)S(1)}, f32[1,1,128,512]{3,2,1,0:T(8,128)S(1)}, u32[]{:S(2)}, u32[]{:S(2)}) collective-permute-start(f32[1,1,128,512]{3,2,1,0:T(8,128)S(1)} %constant_dynamic-slice_fusion), channel_id=1, source_target_pairs={{0,16},{8,24},{16,0},{24,8},{1,17},{9,25},{17,1},{25,9},{2,18},{10... | collective-permute-start | bytes 786440 | tf_op jit(solution)/shard_map/ppermute | solution.py:78
  425.1 3.6 fusion.38
  428.7 3.0 collective-permute-done.17
  433.3 2.1 fusion.36
  435.3 4.3 collective-permute-done.18
  440.1 2.1 fusion.34
  442.2 9.3 %collective-permute-done.19 = f32[1,128,512]{2,1,0:T(8,128)S(1)} collective-permute-done((f32[1,128,512]{2,1,0:T(8,128)S(1)}, f32[1,128,512]{2,1,0:T(8,128)S(1)}, u32[]{:S(2)}, u32[]{:S(2)}) %collective-permute-start.19) | collective-permute-done | bytes 262176 | tf_op jit(solution)/shard_map/ppermute | solution.py:78
  451.5 2.6 collective-permute-start.20
  456.2 10.2 %collective-permute-done.20 = f32[1,128,512]{2,1,0:T(8,128)S(1)} collective-permute-done((f32[1,128,512]{2,1,0:T(8,128)S(1)}, f32[1,128,512]{2,1,0:T(8,128)S(1)}, u32[]{:S(2)}, u32[]{:S(2)}) %collective-permute-start.20) | collective-permute-done | bytes 262176 | tf_op jit(solution)/shard_map/ppermute | solution.py:78
  466.4 86.4 %all-reduce.2.cloned.1.call-done = f32[6,512,512]{2,1,0:T(8,128)} async-done(((f32[6,512,512]{2,1,0:T(8,128)}), f32[6,512,512]{2,1,0:T(8,128)}) %all-reduce.2.cloned.1.call-update) | async-done | bytes 6291472 | tf_op jit(solution)/shard_map/psum | solution.py:115
  552.8 3.6 fusion.99
  (171 shorter events, 38.0 us)
Async XLA Ops:
  7.2 77.6 %all-gather.5.cloned.1.call-start = ((), (), s32[]{:S(2)}) async-start(), calls=%async_computation | async-start | bytes 2621440 | tf_op jit(solution)/shard_map/all_gather | solution.py:65
  9.7 11.6 %copy-start.10 = (f32[256,512]{1,0:T(8,128)}, f32[256,512]{1,0:T(8,128)S(1)}, u32[]{:S(2)}) copy-start(f32[256,512]{1,0:T(8,128)S(1)} %get-tuple-element.10) | copy-start | bytes 1572868
  9.7 14.5 %copy-start.8 = (f32[256,512]{1,0:T(8,128)}, f32[256,512]{1,0:T(8,128)S(1)}, u32[]{:S(2)}) copy-start(f32[256,512]{1,0:T(8,128)S(1)} %get-tuple-element.12) | copy-start | bytes 1572868
  9.8 0.7 collective-permute-start
  11.3 114.7 %all-gather.7.cloned.1.call-start = ((), (), s32[]{:S(2)}) async-start(), calls=%async_computation.1 | async-start | bytes 2621440 | tf_op jit(solution)/shard_map/all_gather | solution.py:65
  11.4 0.7 collective-permute-start.4
  12.9 131.3 %all-gather.9.cloned.1.call-start = ((), (), s32[]{:S(2)}) async-start(), calls=%async_computation.2 | async-start | bytes 2621440 | tf_op jit(solution)/shard_map/all_gather | solution.py:65
  13.0 0.7 collective-permute-start.8
  14.5 161.0 %all-gather.11.cloned.1.call-start = ((), (), s32[]{:S(2)}) async-start(), calls=%async_computation.3 | async-start | bytes 2621440 | tf_op jit(solution)/shard_map/all_gather | solution.py:65
  21.3 9.0 %collective-permute-start.12 = (f32[256,512]{1,0:T(8,128)S(1)}, f32[256,512]{1,0:T(8,128)S(1)}, u32[]{:S(2)}, u32[]{:S(2)}) collective-permute-start(f32[256,512]{1,0:T(8,128)S(1)} %get-tuple-element.12), channel_id=1, source_target_pairs={{0,0},{1,8},{2,16},{3,24},{4,1},{5,9},{6,17},{7,25},{8,2},{9,10},{... | collective-permute-start | bytes 1572872 | tf_op jit(solution)/shard_map/ppermute | solution.py:64
  31.2 521.6 %all-reduce.2.cloned.1.call-start = ((), (), s32[]{:S(2)}) async-start(), calls=%async_computation.4 | async-start | bytes 12582912 | tf_op jit(solution)/shard_map/psum | solution.py:115
  91.8 85.9 %collective-permute-start.1 = (f32[1024,512]{1,0:T(8,128)}, f32[1024,512]{1,0:T(8,128)}, u32[]{:S(2)}, u32[]{:S(2)}) collective-permute-start(f32[1024,512]{1,0:T(8,128)} %fusion.12), channel_id=1, source_target_pairs={{0,1},{1,0},{2,3},{3,2},{4,5},{5,4},{6,7},{7,6},{8,9},{9,8},{10,11... | collective-permute-start | bytes 6291464 | tf_op jit(solution)/shard_map/ppermute | solution.py:78
  133.1 82.3 %collective-permute-start.5 = (f32[1024,512]{1,0:T(8,128)}, f32[1024,512]{1,0:T(8,128)}, u32[]{:S(2)}, u32[]{:S(2)}) collective-permute-start(f32[1024,512]{1,0:T(8,128)} %fusion.10), channel_id=1, source_target_pairs={{0,1},{1,0},{2,3},{3,2},{4,5},{5,4},{6,7},{7,6},{8,9},{9,8},{10,11... | collective-permute-start | bytes 6291464 | tf_op jit(solution)/shard_map/ppermute | solution.py:78
  178.4 37.1 %copy-start.36 = (bf16[1024,512]{1,0:T(8,128)(2,1)S(1)}, bf16[1024,512]{1,0:T(8,128)(2,1)}, u32[]{:S(2)}) copy-start(bf16[1024,512]{1,0:T(8,128)(2,1)} %copy-done.35) | copy-start | bytes 3145732
  178.4 37.1 %copy-start.38 = (bf16[1024,512]{1,0:T(8,128)(2,1)S(1)}, bf16[1024,512]{1,0:T(8,128)(2,1)}, u32[]{:S(2)}) copy-start(bf16[1024,512]{1,0:T(8,128)(2,1)} %copy-done.37) | copy-start | bytes 3145732
  184.6 39.4 %copy-start.43 = (f32[1024,512]{1,0:T(8,128)S(1)}, f32[1024,512]{1,0:T(8,128)}, u32[]{:S(2)}) copy-start(f32[1024,512]{1,0:T(8,128)} %fusion.8) | copy-start | bytes 6291460
  184.6 39.4 %collective-permute-start.2 = (f32[2,256,512]{2,1,0:T(8,128)S(1)}, f32[2,256,512]{2,1,0:T(8,128)S(1)}, u32[]{:S(2)}, u32[]{:S(2)}) collective-permute-start(f32[2,256,512]{2,1,0:T(8,128)S(1)} %dynamic-slice_bitcast_fusion.3), channel_id=1, source_target_pairs={{0,2},{1,3},{2,0},{3,1},{4,6},{5,7},{6,4},{7,5},{8,10},{9,11},{10,... | collective-permute-start | bytes 3145736 | tf_op jit(solution)/shard_map/ppermute | solution.py:78
  220.7 25.2 %copy-start.26 = (bf16[1024,1024]{1,0:T(8,128)(2,1)S(1)}, bf16[1024,1024]{1,0:T(8,128)(2,1)}, u32[]{:S(2)}) copy-start(bf16[1024,1024]{1,0:T(8,128)(2,1)} %get-tuple-element.22) | copy-start | bytes 6291460
  220.8 29.8 %collective-permute-start.6 = (f32[2,256,512]{2,1,0:T(8,128)S(1)}, f32[2,256,512]{2,1,0:T(8,128)S(1)}, u32[]{:S(2)}, u32[]{:S(2)}) collective-permute-start(f32[2,256,512]{2,1,0:T(8,128)S(1)} %dynamic-slice_bitcast_fusion.2), channel_id=1, source_target_pairs={{0,2},{1,3},{2,0},{3,1},{4,6},{5,7},{6,4},{7,5},{8,10},{9,11},{10,... | collective-permute-start | bytes 3145736 | tf_op jit(solution)/shard_map/ppermute | solution.py:78
  224.0 56.9 %collective-permute-start.9 = (f32[1024,512]{1,0:T(8,128)S(1)}, f32[1024,512]{1,0:T(8,128)}, u32[]{:S(2)}, u32[]{:S(2)}) collective-permute-start(f32[1024,512]{1,0:T(8,128)S(1)} %copy-done.43), channel_id=1, source_target_pairs={{0,1},{1,0},{2,3},{3,2},{4,5},{5,4},{6,7},{7,6},{8,9},{9,8},{10,11... | collective-permute-start | bytes 6291464 | tf_op jit(solution)/shard_map/ppermute | solution.py:78
  226.8 50.5 %collective-permute-start.3 = (f32[1,256,512]{2,1,0:T(8,128)S(1)}, f32[1,256,512]{2,1,0:T(8,128)S(1)}, u32[]{:S(2)}, u32[]{:S(2)}) collective-permute-start(f32[1,256,512]{2,1,0:T(8,128)S(1)} %constant_dynamic-slice_fusion.4), channel_id=1, source_target_pairs={{0,4},{1,5},{2,6},{3,7},{4,0},{5,1},{6,2},{7,3},{8,12},{9,13},{10,... | collective-permute-start | bytes 1572872 | tf_op jit(solution)/shard_map/ppermute | solution.py:78
  250.6 26.7 %copy-start.7 = (f32[4,256,512]{2,1,0:T(8,128)S(1)}, f32[4,256,512]{2,1,0:T(8,128)}, u32[]{:S(2)}) copy-start(f32[4,256,512]{2,1,0:T(8,128)} %param.6) | copy-start | bytes 6291460
  250.6 63.7 %collective-permute-start.13 = (f32[1024,512]{1,0:T(8,128)}, f32[1024,512]{1,0:T(8,128)}, u32[]{:S(2)}, u32[]{:S(2)}) collective-permute-start(f32[1024,512]{1,0:T(8,128)} %fusion.6), channel_id=1, source_target_pairs={{0,1},{1,0},{2,3},{3,2},{4,5},{5,4},{6,7},{7,6},{8,9},{9,8},{10,11... | collective-permute-start | bytes 6291464 | tf_op jit(solution)/shard_map/ppermute | solution.py:78
  258.0 22.9 %copy-start.30 = (bf16[1024,512]{1,0:T(8,128)(2,1)S(1)}, bf16[1024,512]{1,0:T(8,128)(2,1)}, u32[]{:S(2)}) copy-start(bf16[1024,512]{1,0:T(8,128)(2,1)} %copy-done.29) | copy-start | bytes 3145732
  258.0 22.9 %copy-start.32 = (bf16[1024,512]{1,0:T(8,128)(2,1)S(1)}, bf16[1024,512]{1,0:T(8,128)(2,1)}, u32[]{:S(2)}) copy-start(bf16[1024,512]{1,0:T(8,128)(2,1)} %copy-done.31) | copy-start | bytes 3145732
  258.0 61.5 %collective-permute-start.7 = (f32[1,256,512]{2,1,0:T(8,128)S(1)}, f32[1,256,512]{2,1,0:T(8,128)S(1)}, u32[]{:S(2)}, u32[]{:S(2)}) collective-permute-start(f32[1,256,512]{2,1,0:T(8,128)S(1)} %constant_dynamic-slice_fusion.3), channel_id=1, source_target_pairs={{0,4},{1,5},{2,6},{3,7},{4,0},{5,1},{6,2},{7,3},{8,12},{9,13},{10,... | collective-permute-start | bytes 1572872 | tf_op jit(solution)/shard_map/ppermute | solution.py:78
  277.3 42.2 %copy-start.1 = (f32[1,256,512]{2,1,0:T(8,128)}, f32[1,256,512]{2,1,0:T(8,128)S(1)}, u32[]{:S(2)}) copy-start(f32[1,256,512]{2,1,0:T(8,128)S(1)} %add_multiply_fusion) | copy-start | bytes 1572868
  286.0 33.5 %copy-start = (f32[3,512,512]{2,1,0:T(8,128)S(1)}, f32[3,512,512]{2,1,0:T(8,128)}, u32[]{:S(2)}) copy-start(f32[3,512,512]{2,1,0:T(8,128)} %param.7) | copy-start | bytes 9437188
  286.0 36.4 %collective-permute-start.10 = (f32[2,256,512]{2,1,0:T(8,128)S(1)}, f32[2,256,512]{2,1,0:T(8,128)S(1)}, u32[]{:S(2)}, u32[]{:S(2)}) collective-permute-start(f32[2,256,512]{2,1,0:T(8,128)S(1)} %dynamic-slice_bitcast_fusion.1), channel_id=1, source_target_pairs={{0,2},{1,3},{2,0},{3,1},{4,6},{5,7},{6,4},{7,5},{8,10},{9,11},{10,... | collective-permute-start | bytes 3145736 | tf_op jit(solution)/shard_map/ppermute | solution.py:78
  319.4 34.5 %collective-permute-start.14 = (f32[2,256,512]{2,1,0:T(8,128)S(1)}, f32[2,256,512]{2,1,0:T(8,128)S(1)}, u32[]{:S(2)}, u32[]{:S(2)}) collective-permute-start(f32[2,256,512]{2,1,0:T(8,128)S(1)} %dynamic-slice_bitcast_fusion), channel_id=1, source_target_pairs={{0,2},{1,3},{2,0},{3,1},{4,6},{5,7},{6,4},{7,5},{8,10},{9,11},{10,... | collective-permute-start | bytes 3145736 | tf_op jit(solution)/shard_map/ppermute | solution.py:78
  320.4 52.5 %copy-start.3 = (f32[256,512]{1,0:T(8,128)}, f32[256,512]{1,0:T(8,128)S(1)}, u32[]{:S(2)}) copy-start(f32[256,512]{1,0:T(8,128)S(1)} %fusion.69) | copy-start | bytes 1572868
  320.4 23.2 %copy-start.11 = (f32[256,512]{1,0:T(8,128)S(1)}, f32[256,512]{1,0:T(8,128)}, u32[]{:S(2)}) copy-start(f32[256,512]{1,0:T(8,128)} %copy-done.10) | copy-start | bytes 1572868
  322.7 50.2 %collective-permute-start.11 = (f32[1,256,512]{2,1,0:T(8,128)S(1)}, f32[1,256,512]{2,1,0:T(8,128)S(1)}, u32[]{:S(2)}, u32[]{:S(2)}) collective-permute-start(f32[1,256,512]{2,1,0:T(8,128)S(1)} %constant_dynamic-slice_fusion.2), channel_id=1, source_target_pairs={{0,4},{1,5},{2,6},{3,7},{4,0},{5,1},{6,2},{7,3},{8,12},{9,13},{10,... | collective-permute-start | bytes 1572872 | tf_op jit(solution)/shard_map/ppermute | solution.py:78
  354.2 21.0 %copy-start.19 = (f32[2,256,512]{2,1,0:T(8,128)}, f32[2,256,512]{2,1,0:T(8,128)S(1)}, u32[]{:S(2)}) copy-start(f32[2,256,512]{2,1,0:T(8,128)S(1)} %bitcast_add_fusion) | copy-start | bytes 3145732
  354.2 21.0 %copy-start.9 = (f32[256,512]{1,0:T(8,128)S(1)}, f32[256,512]{1,0:T(8,128)}, u32[]{:S(2)}) copy-start(f32[256,512]{1,0:T(8,128)} %copy-done.8) | copy-start | bytes 1572868
  355.0 42.7 %collective-permute-start.15 = (f32[1,256,512]{2,1,0:T(8,128)}, f32[1,256,512]{2,1,0:T(8,128)}, u32[]{:S(2)}, u32[]{:S(2)}) collective-permute-start(f32[1,256,512]{2,1,0:T(8,128)} %constant_dynamic-slice_fusion.1), channel_id=1, source_target_pairs={{0,4},{1,5},{2,6},{3,7},{4,0},{5,1},{6,2},{7,3},{8,12},{9,13},{10,... | collective-permute-start | bytes 1572872 | tf_op jit(solution)/shard_map/ppermute | solution.py:78
  376.8 23.7 %copy-start.22 = (f32[512,256]{1,0:T(8,128)S(1)}, f32[512,256]{1,0:T(8,128)}, u32[]{:S(2)}) copy-start(f32[512,256]{1,0:T(8,128)} %copy.25) | copy-start | bytes 1572868
  403.0 2.3 collective-permute-start.16
  403.0 30.3 %copy-start.17 = (f32[4,512,512]{2,1,0:T(8,128)S(1)}, f32[4,512,512]{2,1,0:T(8,128)}, u32[]{:S(2)}) copy-start(f32[4,512,512]{2,1,0:T(8,128)} %param.8) | copy-start | bytes 12582916
  406.6 25.2 %collective-permute-start.17 = (f32[1,1,128,512]{3,2,1,0:T(8,128)S(1)}, f32[1,1,128,512]{3,2,1,0:T(8,128)S(1)}, u32[]{:S(2)}, u32[]{:S(2)}) collective-permute-start(f32[1,1,128,512]{3,2,1,0:T(8,128)S(1)} %constant_dynamic-slice_fusion), channel_id=1, source_target_pairs={{0,16},{8,24},{16,0},{24,8},{1,17},{9,25},{17,1},{25,9},{2,18},{10... | collective-permute-start | bytes 786440 | tf_op jit(solution)/shard_map/ppermute | solution.py:78
  428.7 25.4 %slice-start.1 = ((f32[4,512,512]{2,1,0:T(8,128)}), f32[1,512,512]{2,1,0:T(8,128)S(1)}, s32[]{:S(2)}) async-start(f32[4,512,512]{2,1,0:T(8,128)} %param.8), calls=%async_computation.6 | async-start | bytes 2097152 | tf_op jit(solution)/shard_map/slice | solution.py:137
  431.8 7.9 %collective-permute-start.18 = (f32[1,128,512]{2,1,0:T(8,128)S(1)}, f32[1,128,512]{2,1,0:T(8,128)S(1)}, u32[]{:S(2)}, u32[]{:S(2)}) collective-permute-start(f32[1,128,512]{2,1,0:T(8,128)S(1)} %add_bitcast_fusion), channel_id=1, source_target_pairs={{0,1},{1,0},{2,3},{3,2},{4,5},{5,4},{6,7},{7,6},{8,9},{9,8},{10,11... | collective-permute-start | bytes 786440 | tf_op jit(solution)/shard_map/ppermute | solution.py:78
  439.7 14.9 %copy-start.2 = (f32[1,256,512]{2,1,0:T(8,128)S(1)}, f32[1,256,512]{2,1,0:T(8,128)}, u32[]{:S(2)}) copy-start(f32[1,256,512]{2,1,0:T(8,128)} %copy-done.1) | copy-start | bytes 1572868
  439.7 14.9 %copy-start.4 = (f32[256,512]{1,0:T(8,128)S(1)}, f32[256,512]{1,0:T(8,128)}, u32[]{:S(2)}) copy-start(f32[256,512]{1,0:T(8,128)} %copy-done.3) | copy-start | bytes 1572868
  439.7 14.9 %copy-start.6 = (f32[256,512]{1,0:T(8,128)S(1)}, f32[256,512]{1,0:T(8,128)}, u32[]{:S(2)}) copy-start(f32[256,512]{1,0:T(8,128)} %copy-done.5) | copy-start | bytes 1572868
  439.7 14.9 %copy-start.13 = (f32[256,512]{1,0:T(8,128)S(1)}, f32[256,512]{1,0:T(8,128)}, u32[]{:S(2)}) copy-start(f32[256,512]{1,0:T(8,128)} %copy-done.12) | copy-start | bytes 1572868
  439.8 11.7 %collective-permute-start.19 = (f32[1,128,512]{2,1,0:T(8,128)S(1)}, f32[1,128,512]{2,1,0:T(8,128)S(1)}, u32[]{:S(2)}, u32[]{:S(2)}) collective-permute-start(f32[1,128,512]{2,1,0:T(8,128)S(1)} %add.212), channel_id=1, source_target_pairs={{0,2},{1,3},{2,0},{3,1},{4,6},{5,7},{6,4},{7,5},{8,10},{9,11},{10,... | collective-permute-start | bytes 786440 | tf_op jit(solution)/shard_map/ppermute | solution.py:78
  451.5 14.8 %collective-permute-start.20 = (f32[1,128,512]{2,1,0:T(8,128)S(1)}, f32[1,128,512]{2,1,0:T(8,128)S(1)}, u32[]{:S(2)}, u32[]{:S(2)}) collective-permute-start(f32[1,128,512]{2,1,0:T(8,128)S(1)} %add.213), channel_id=1, source_target_pairs={{0,4},{1,5},{2,6},{3,7},{4,0},{5,1},{6,2},{7,3},{8,12},{9,13},{10,... | collective-permute-start | bytes 786440 | tf_op jit(solution)/shard_map/ppermute | solution.py:78
  (24 other events, 61.8 us)
Sparse Core Ops, SparseCore 0:
  11.4 73.3 all-gather.4
  86.3 29.4 all-gather.6
  117.9 26.2 all-gather.8
  146.2 29.2 all-gather.10
  376.9 175.8 all-reduce.1
